TPU v7x, 32 devices: a whole 2x2x4 slice. The times are simulated.
32 devices in a mesh: groups: 2 (over x), dp: 16 (over z, y, core).
Axes of the slice: x: 2, y: 2, z: 4, core: 2. Of those that a mesh axis runs over, the one named last changes fastest.
Arguments:
- tokens: bfloat16 [8192, 7168], P(('groups', 'dp')), parts along dimension 0, may hold values from -6 to 6
- lengths: int32 [32], P('groups'), parts along dimension 0, may hold values from 0 to 256, as said below
- latent_weight: bfloat16 [7168, 576], P('dp'), may hold values from -0.0625 to 0.0625
- latent_gain: float32 [512], replicated, may hold values from 0.25 to 1.75
- expert_ids: int32 [8192, 1], P(('groups', 'dp')), parts along dimension 0, may hold values from 0 to 1; in each aligned block of 256 rows (0 to 255, 256 to 511, ...) at most 130 rows name the same one
- gate_weights: float32 [8192, 1], P(('groups', 'dp')), parts along dimension 0, may hold values from 0.5 to 1.5
- gate_up: bfloat16 [14336, 2048], P('dp'), may hold values from -0.0625 to 0.0625
- down_weight: bfloat16 [16384, 896], P('dp'), may hold values from -0.1875 to 0.1875
Outputs:
- latent_cache: bfloat16 [8192, 576], P(('groups', 'dp')), parts along dimension 0
- moe_out: bfloat16 [8192, 7168], P(('groups', 'dp')), parts along dimension 0
There are 2 independent parts, one for each index of `groups`. A program takes and returns all parts, laid end to end along the dimension named above; an argument that names none is the same for every part. Nothing has to cross between parts.
Inputs may be any that keep to these rules, and one draw needn't show every extreme that they name: Only the first lengths[r] of rank r's 256 rows are prompt tokens. `expert_ids`: of the 256 rows of one rank, at most 130 name one expert.
All inputs are finite; a program needn't handle non-finite values.
Results may differ from a plain program's by a relative error of at most 0.019.
Values may be sent and summed in bfloat16 or wider, within the bound.
No kernel may reach another device: no remote copies, remote signals or barrier semaphores. Data moves between devices by JAX's collectives and lax.ppermute only.
A program may use at most 128 MiB of HBM per device.

v0:
```python
import jax
import jax.numpy as jnp
from jax import lax
from jax.sharding import PartitionSpec as P

GROUP = 8
BLOCK = 128


rope_base = 10000.0
norm_eps = 1e-06


def swapped(block, axis, bit):
    count = lax.axis_size(axis)
    route = []
    for low in range(count):
        high = low | 1 << bit
        if high != low and high < count:
            route += [(low, high), (high, low)]
    return lax.ppermute(block, axis, route)


def latent_rows(token_rows, weight, gain, first_pos, length):
    projected = jnp.dot(token_rows, weight, preferred_element_type=jnp.float32)
    lat_width = gain.shape[0]
    compressed = projected[:, :lat_width]
    rotary = projected[:, lat_width:]
    inverse_rms = lax.rsqrt(jnp.mean(compressed * compressed, axis=1, keepdims=True) + norm_eps)
    normed = compressed * inverse_rms * gain[None, :]
    half_cols = rotary.shape[1] // 2
    positions = first_pos + jnp.arange(token_rows.shape[0], dtype=jnp.int32)
    frequency = rope_base ** (-jnp.arange(half_cols, dtype=jnp.float32) / half_cols)
    angles = positions.astype(jnp.float32)[:, None] * frequency[None, :]
    cosine = jnp.cos(angles)
    sine_part = jnp.sin(angles)
    left_half = rotary[:, :half_cols]
    right_half = rotary[:, half_cols:]
    turned = jnp.concatenate(
        [left_half * cosine - right_half * sine_part, left_half * sine_part + right_half * cosine],
        axis=1,
    )
    result = jnp.concatenate([normed, turned], axis=1)
    alive_rows = positions < length
    return jnp.where(alive_rows[:, None], result, 0.0).astype(jnp.bfloat16)


def encode_blocks(latent_store, source, block_count, weight, gain, length, first_block, block_rows):

    def encode_one(block_index, buffer):
        token_rows = lax.dynamic_slice_in_dim(source, block_index * block_rows, block_rows, 0)
        made = latent_rows(
            token_rows, weight, gain, (first_block + block_index) * block_rows, length
        )
        return lax.dynamic_update_slice_in_dim(buffer, made, block_index * block_rows, 0)

    return lax.fori_loop(0, block_count, encode_one, latent_store)


def shards(
    tokens, lengths, latent_weight, latent_gain, expert_ids, gate_weights, gate_up, down_weight
):
    block_rows = BLOCK
    slot_count = tokens.shape[0]
    block_total = slot_count // block_rows
    rank_count = lax.axis_size("dp")
    my_rank = lax.axis_index("dp")
    weight = lax.all_gather(latent_weight, "dp", axis=0, tiled=True)
    out_width = weight.shape[1]
    length = lengths[my_rank]
    own_blocks = (length + block_rows - 1) // block_rows
    spare_rows = block_total // 2 * block_rows
    latent_store = jnp.zeros((slot_count + spare_rows, out_width), jnp.bfloat16)
    latent_store = encode_blocks(
        latent_store, tokens, own_blocks, weight, latent_gain, length, 0, block_rows
    )
    latent_cache = latent_store[:slot_count]
    experts = rank_count // GROUP
    top_count = expert_ids.shape[1]
    capacity = slot_count * top_count // experts + 2
    part_width = tokens.shape[1] // GROUP
    pair_count = slot_count * top_count
    levels = GROUP.bit_length() - 1
    alive_rows = jnp.arange(slot_count, dtype=jnp.int32) < length
    pair_live = jnp.repeat(alive_rows, top_count)
    pair_expert = expert_ids.reshape(pair_count)
    expert_hits = (
        (pair_expert[:, None] == jnp.arange(experts, dtype=jnp.int32)[None, :]) & pair_live[:, None]
    ).astype(jnp.int32)
    slot_place = jnp.sum((jnp.cumsum(expert_hits, axis=0) - expert_hits) * expert_hits, axis=1)
    target = jnp.where(pair_live, pair_expert, experts)
    pieces = jnp.repeat(tokens, top_count, axis=0).reshape(pair_count, GROUP, part_width)
    outbox = (
        jnp.zeros((experts, GROUP, capacity, part_width), jnp.bfloat16)
        .at[target, :, slot_place]
        .set(pieces, mode="drop")
    )
    outbox = outbox.reshape(rank_count, capacity, part_width)
    arrived = lax.all_to_all(outbox, "dp", split_axis=0, concat_axis=0, tiled=True)
    source_count, item_count, slice_width = arrived.shape
    flat_rows = arrived.reshape(source_count * item_count, slice_width)
    partial_value = jnp.dot(flat_rows, gate_up, preferred_element_type=jnp.float32).astype(
        jnp.bfloat16
    )
    hidden_units = gate_up.shape[1] // 2
    current = partial_value
    for level in range(levels - 1, -1, -1):
        half_rows = current.shape[0] // 2
        upper = my_rank >> level & 1 == 1
        lower_half = current[:half_rows]
        upper_half = current[half_rows:]
        kept_half = jnp.where(upper, upper_half, lower_half)
        outgoing_half = jnp.where(upper, lower_half, upper_half).astype(jnp.bfloat16)
        received = swapped(outgoing_half, "dp", level)
        current = kept_half.astype(jnp.float32) + received.astype(jnp.float32)
    hidden = (jax.nn.silu(current[:, :hidden_units]) * current[:, hidden_units:]).astype(
        jnp.bfloat16
    )
    for level in range(levels):
        partner_rows = swapped(hidden, "dp", level)
        upper = my_rank >> level & 1 == 1
        hidden = jnp.where(
            upper,
            jnp.concatenate([partner_rows, hidden], axis=0),
            jnp.concatenate([hidden, partner_rows], axis=0),
        )
    produced = jnp.dot(hidden, down_weight, preferred_element_type=jnp.float32).astype(jnp.bfloat16)
    processed = produced.reshape(source_count, item_count, produced.shape[1])
    returned_rows = lax.all_to_all(processed, "dp", split_axis=0, concat_axis=0, tiled=True)
    returned_rows = returned_rows.reshape(experts, GROUP, capacity, part_width)
    picked = returned_rows[jnp.minimum(target, experts - 1), :, slot_place]
    pair_weight = jnp.where(pair_live, gate_weights.reshape(pair_count), 0.0)
    blended = (
        picked.astype(jnp.float32).reshape(pair_count, GROUP * part_width) * pair_weight[:, None]
    )
    moe_out = (
        blended.reshape(slot_count, top_count, GROUP * part_width).sum(axis=1).astype(jnp.bfloat16)
    )
    return (latent_cache, moe_out)


def solution(mesh):
    placed = (
        P(("groups", "dp"), None),
        P("groups"),
        P("dp", None),
        P(),
        P(("groups", "dp"), None),
        P(("groups", "dp"), None),
        P("dp", None),
        P("dp", None),
    )
    return jax.shard_map(
        shards,
        mesh=mesh,
        in_specs=placed,
        out_specs=(P(("groups", "dp"), None), P(("groups", "dp"), None)),
        check_vma=False,
    )
```

profile of v0, /device:TPU:8, one launch (start us, length us, event | category | flops | bytes accessed | tf_op | source)
XLA Modules:
  0.0 596.2 jit_solution(6212875703847898004)
XLA Ops:
  13.9 4.6 copy.23
  20.6 35.3 %scatter_fusion = bf16[2,8,130,896]{3,1,2,0:T(8,128)(2,1)} fusion(bf16[2,8,130,896]{3,1,2,0:T(8,128)(2,1)} %broadcast_in_dim.30, s32[256]{0:T(256)S(1)} %bitcast.44, bf16[256,8,896]{2,1,0:T(8,128)(2,1)} %bitcast.47), kind=kCustom, calls=%fused_computation.1 | custom fusion | bytes 11012096 | tf_op jit(solution)/shard_map/scatter | solution.py:96
  60.9 4.5 all-to-all-start
  65.5 84.5 %all-to-all-done = bf16[16,130,896]{2,1,0:T(8,128)(2,1)} async-done(((bf16[16,130,896]{2,1,0:T(8,128)(2,1)}), bf16[16,130,896]{2,1,0:T(8,128)(2,1)}, u32[]{:S(2)}, u32[]{:S(2)}) %all-to-all-start) | async-done | bytes 3727392 | tf_op jit(solution)/shard_map/all_to_all | solution.py:99
  149.9 4.9 reshape.103
  154.8 11.8 %convolution_convert_fusion = bf16[2080,2048]{1,0:T(8,128)(2,1)S(1)} fusion(bf16[2080,896]{1,0:T(8,128)(2,1)} %reshape.103, bf16[896,2048]{1,0:T(8,128)(2,1)} %param.16), kind=kOutput, calls=%fused_computation.23 | convolution fusion | flops 7637893120 | bytes 15917056 | tf_op jit(solution)/shard_map/dot_general | solution.py:102
  171.2 149.1 %collective-permute-done = bf16[1040,2048]{1,0:T(8,128)(2,1)} collective-permute-done((bf16[1040,2048]{1,0:T(8,128)(2,1)}, bf16[1040,2048]{1,0:T(8,128)(2,1)}, u32[]{:S(2)}, u32[]{:S(2)}) %collective-permute-start) | collective-permute-done | bytes 4259872 | tf_op jit(solution)/shard_map/ppermute | solution.py:21
  320.4 6.1 %convert_add_fusion = f32[1040,2048]{1,0:T(8,128)S(1)} fusion(bf16[1040,2048]{1,0:T(8,128)(2,1)} %collective-permute-done, pred[]{:T(512)S(6)} %eq.37, bf16[2080,2048]{1,0:T(8,128)(2,1)} %copy-done.3), kind=kLoop, calls=%fused_computation.24 | loop fusion | flops 8519680 | bytes 21299200 | tf_op jit(solution)/shard_map/add | solution.py:115
  326.5 3.3 copy-done.2
  331.5 3.6 collective-permute-start.1
  335.1 46.3 %collective-permute-done.1 = bf16[520,2048]{1,0:T(8,128)(2,1)} collective-permute-done((bf16[520,2048]{1,0:T(8,128)(2,1)}, bf16[520,2048]{1,0:T(8,128)(2,1)}, u32[]{:S(2)}, u32[]{:S(2)}) %collective-permute-start.1) | collective-permute-done | bytes 2129952 | tf_op jit(solution)/shard_map/ppermute | solution.py:21
  381.4 5.7 convert_add_fusion.1
  395.3 23.8 %collective-permute-done.4 = bf16[520,1024]{1,0:T(8,128)(2,1)S(1)} collective-permute-done((bf16[520,1024]{1,0:T(8,128)(2,1)S(1)}, bf16[520,1024]{1,0:T(8,128)(2,1)S(1)}, u32[]{:S(2)}, u32[]{:S(2)}) %collective-permute-start.4) | collective-permute-done | bytes 1064992 | tf_op jit(solution)/shard_map/ppermute | solution.py:21
  423.6 45.8 %collective-permute-done.5 = bf16[1040,1024]{1,0:T(8,128)(2,1)} collective-permute-done((bf16[1040,1024]{1,0:T(8,128)(2,1)}, bf16[1040,1024]{1,0:T(8,128)(2,1)}, u32[]{:S(2)}, u32[]{:S(2)}) %collective-permute-start.5) | collective-permute-done | bytes 2129952 | tf_op jit(solution)/shard_map/ppermute | solution.py:21
  469.4 9.9 %convolution_convert_fusion.1 = bf16[2080,896]{1,0:T(8,128)(2,1)} fusion(bf16[1024,896]{1,0:T(8,128)(2,1)S(1)} %copy-done, bf16[1040,1024]{1,0:T(8,128)(2,1)} %maximum_select_fusion.3, bf16[1040,1024]{1,0:T(8,128)(2,1)} %collective-permute-done.5, pred[]{:T(512)S(6)} %eq.37), kind=kOutput, calls=%fused_computation.26 | convolution fusion | flops 3837849600 | bytes 9822209 | tf_op jit(solution)/shard_map/dot_general | solution.py:127
  479.3 4.9 reshape.104
  484.2 5.5 all-to-all-start.1
  489.8 18.1 %while.10 = (s32[]{:T(128)}, bf16[384,576]{0,1:T(8,128)(2,1)S(1)}, s32[]{:T(128)}, s32[]{:T(128)}, bf16[256,7168]{1,0:T(8,128)(2,1)}, /*index=5*/bf16[7168,576]{...) while((s32[]{:T(128)}, bf16[384,576]{0,1:T(8,128)(2,1)S(1)}, ...), condition=%wide.region_2.3_spmd, body=%wide.region_0.2_spmd.sunk | while | flops 1057845952 | bytes 12310608 | solution.py:57
  489.8 7.7 %fusion.41 = f32[128,576]{0,1:T(8,128)S(1)} fusion(bf16[7168,576]{1,0:T(8,128)(2,1)} %get-tuple-element.136, bf16[256,7168]{1,0:T(8,128)(2,1)} %get-tuple-element.135, s32[]{:T(128)S(6)} %select_n.183), kind=kOutput, calls=%fused_computation.2.clone.1 | convolution fusion | flops 1056964608 | bytes 11304964 | tf_op jit(solution)/shard_map/while/body/dot_general | solution.py:25
  498.7 7.7 %fusion.41 = f32[128,576]{0,1:T(8,128)S(1)} fusion(bf16[7168,576]{1,0:T(8,128)(2,1)} %get-tuple-element.136, bf16[256,7168]{1,0:T(8,128)(2,1)} %get-tuple-element.135, s32[]{:T(128)S(6)} %select_n.183), kind=kOutput, calls=%fused_computation.2.clone.1 | convolution fusion | flops 1056964608 | bytes 11304964 | tf_op jit(solution)/shard_map/while/body/dot_general | solution.py:25
  508.6 65.6 %all-to-all-done.1 = bf16[16,130,896]{2,1,0:T(8,128)(2,1)} async-done(((bf16[16,130,896]{2,1,0:T(8,128)(2,1)}), bf16[16,130,896]{2,1,0:T(8,128)(2,1)}, u32[]{:S(2)}, u32[]{:S(2)}) %all-to-all-start.1) | async-done | bytes 3727392 | tf_op jit(solution)/shard_map/all_to_all | solution.py:129
  574.2 4.4 copy.19
  578.6 5.2 gather_fusion
  583.7 3.0 copy.24
  (61 shorter events, 37.7 us)
Async XLA Ops:
  7.2 462.2 %copy-start = (bf16[1024,896]{1,0:T(8,128)(2,1)S(1)}, bf16[1024,896]{1,0:T(8,128)(2,1)}, u32[]{:S(2)}) copy-start(bf16[1024,896]{1,0:T(8,128)(2,1)} %param.17) | copy-start | bytes 5505028
  60.9 89.0 %all-to-all-start = ((bf16[16,130,896]{2,1,0:T(8,128)(2,1)}), bf16[16,130,896]{2,1,0:T(8,128)(2,1)}, u32[]{:S(2)}, u32[]{:S(2)}) async-start(bf16[16,130,896]{2,1,0:T(8,128)(2,1)} %copy.17), calls=%async_computation | async-start | bytes 7798784 | tf_op jit(solution)/shard_map/all_to_all | solution.py:99
  65.4 424.3 %all-gather.2.cloned.1.call-start = ((), (), s32[]{:S(2)}) async-start(), calls=%async_computation.2 | async-start | bytes 9748480 | tf_op jit(solution)/shard_map/all_gather | solution.py:68
  166.6 4.6 copy-start.3
  171.2 149.1 %collective-permute-start = (bf16[1040,2048]{1,0:T(8,128)(2,1)}, bf16[1040,2048]{1,0:T(8,128)(2,1)}, u32[]{:S(2)}, u32[]{:S(2)}) collective-permute-start(bf16[1040,2048]{1,0:T(8,128)(2,1)} %broadcast_select_fusion), channel_id=1, source_target_pairs={{0,4},{4,0},{1,5},{5,1},{2,6},{6,2},{3,7},{7,3},{8,12},{12,8},{9,1... | collective-permute-start | bytes 12779528 | tf_op jit(solution)/shard_map/ppermute | solution.py:21
  326.5 3.3 copy-start.2
  331.5 49.9 %collective-permute-start.1 = (bf16[520,2048]{1,0:T(8,128)(2,1)}, bf16[520,2048]{1,0:T(8,128)(2,1)}, u32[]{:S(2)}, u32[]{:S(2)}) collective-permute-start(bf16[520,2048]{1,0:T(8,128)(2,1)} %select_convert_fusion), channel_id=1, source_target_pairs={{0,2},{2,0},{1,3},{3,1},{4,6},{6,4},{5,7},{7,5},{8,10},{10,8},{9,1... | collective-permute-start | bytes 6389768 | tf_op jit(solution)/shard_map/ppermute | solution.py:21
  387.4 2.8 collective-permute-start.2
  391.1 31.8 %copy-start.5 = (f32[256,1]{0,1:T(1,128)S(1)}, f32[256,1]{0,1:T(1,128)}, u32[]{:S(2)}) copy-start(f32[256,1]{0,1:T(1,128)} %param.15) | copy-start | bytes 3076
  391.1 2.0 collective-permute-start.3
  393.5 25.6 %collective-permute-start.4 = (bf16[520,1024]{1,0:T(8,128)(2,1)S(1)}, bf16[520,1024]{1,0:T(8,128)(2,1)S(1)}, u32[]{:S(2)}, u32[]{:S(2)}) collective-permute-start(bf16[520,1024]{1,0:T(8,128)(2,1)S(1)} %maximum_select_fusion.4), channel_id=1, source_target_pairs={{0,2},{2,0},{1,3},{3,1},{4,6},{6,4},{5,7},{7,5},{8,10},{10,8},{9,1... | collective-permute-start | bytes 3194888 | tf_op jit(solution)/shard_map/ppermute | solution.py:21
  421.5 47.9 %collective-permute-start.5 = (bf16[1040,1024]{1,0:T(8,128)(2,1)}, bf16[1040,1024]{1,0:T(8,128)(2,1)}, u32[]{:S(2)}, u32[]{:S(2)}) collective-permute-start(bf16[1040,1024]{1,0:T(8,128)(2,1)} %maximum_select_fusion.3), channel_id=1, source_target_pairs={{0,4},{4,0},{1,5},{5,1},{2,6},{6,2},{3,7},{7,3},{8,12},{12,8},{9,1... | collective-permute-start | bytes 6389768 | tf_op jit(solution)/shard_map/ppermute | solution.py:21
  484.2 5.5 copy-start.4
  484.2 90.0 %all-to-all-start.1 = ((bf16[16,130,896]{2,1,0:T(8,128)(2,1)}), bf16[16,130,896]{2,1,0:T(8,128)(2,1)}, u32[]{:S(2)}, u32[]{:S(2)}) async-start(bf16[16,130,896]{2,1,0:T(8,128)(2,1)} %reshape.104), calls=%async_computation.1 | async-start | bytes 7798784 | tf_op jit(solution)/shard_map/all_to_all | solution.py:129
  586.7 2.6 copy-start.1
Sparse Core Ops, SparseCore 0:
  171.4 133.8 all-gather.1
where the time goes:
time: 601 us; the launch traced here: 596 us
  waiting for transfers between devices  420 us (70%)
  local copies, waits for them, and re-layouts  76.9 us (13%)
  matrix products  37.1 us (6%)
  other arithmetic  30.9 us (5%)
  starting transfers between devices  16.3 us (3%)
  between operations  15 us (2%)
    ppermute x6, waiting for transfers between devices, swapped(): return lax.ppermute(block, axis, route)  270 us
    all_to_all x1, waiting for transfers between devices, shards(): lax.all_to_all(outbox, 'dp', split_axis=0, concat_axis=0, tiled=True)  84.5 us
    all_to_all x1, waiting for transfers between devices, shards(): lax.all_to_all(processed, 'dp', split_axis=0, concat_axis=0, tiled=True)  65.6 us
    scatter x2, local copies, waits for them, and re-layouts, shards(): outbox = jnp.zeros((experts, GROUP, capacity, part_width), jnp.bfloat16)....  37.6 us
    dot_general x2, matrix products, latent_rows(): projected = jnp.dot(token_rows, weight, preferred_element_type=jnp.float32)  15.4 us
    unnamed x14, local copies, waits for them, and re-layouts  12.8 us
    add x3, other arithmetic, shards(): current = kept_half.astype(jnp.float32) + received.astype(jnp.float32)  12.4 us
  transfers between devices with their start and end apart: 9, of which 8 were waited for; matrix products, arithmetic and copies ran while one was open for 9% of the time, Pallas kernels for 0%

commit v1 on v0

v1 whole, which is shorter than its diff:
```python
import functools

import jax
import jax.numpy as jnp
from jax import lax
from jax.experimental import pallas as pl
from jax.experimental.pallas import tpu as pltpu
from jax.sharding import PartitionSpec as P

GROUP = 8
QUAD = 4

rope_base = 10000.0
norm_eps = 1e-06


def swapped(block, bits):
    count = lax.axis_size("dp")
    return lax.ppermute(block, "dp", [(low, low ^ bits) for low in range(count)])


def chosen_slots(meta_ref, column_ids, row_ids):
    rows = column_ids.shape[0]
    length = meta_ref[1]
    own = lax.broadcasted_iota(jnp.int32, (rows, rows), 0)
    other = lax.broadcasted_iota(jnp.int32, (rows, rows), 1)
    earlier = (column_ids == row_ids) & (other < own) & (other < length)
    place = jnp.sum(earlier.astype(jnp.float32), axis=1, keepdims=True).astype(jnp.int32)
    live = lax.broadcasted_iota(jnp.int32, (rows, 1), 0) < length
    return jnp.where(live, column_ids, -1), place


def selector(expert_column, place_column, expert, start, size):
    rows = expert_column.shape[0]
    slot = lax.broadcasted_iota(jnp.int32, (rows, size), 1) + start
    hit = (place_column == slot) & (expert_column == expert)
    return hit.astype(jnp.float32).astype(jnp.bfloat16)


def pack_body(chunks, pieces, meta_ref, column_ref, row_ref, same_ref, other_ref, *outs):
    expert_column, place_column = chosen_slots(meta_ref, column_ref[...], row_ref[...])
    my_expert = meta_ref[0] // GROUP
    same = same_ref[...]
    other = other_ref[...]
    for number, (start, size) in enumerate(chunks):
        for far in range(pieces // 2):
            picks = selector(expert_column, place_column, my_expert ^ far, start, size)
            for side, source in enumerate((same, other)):
                outs[number * pieces + 2 * far + side][...] = lax.dot_general(
                    picks,
                    source,
                    (((0,), (0,)), ((), ())),
                    preferred_element_type=jnp.float32,
                ).astype(jnp.bfloat16)


def pack(meta, ids, tokens, chunks, pieces):
    rows, width = tokens.shape
    part = width // GROUP

    def column_of(side):
        def index(k, meta_ref):
            quarter = meta_ref[0] % QUAD
            high = (meta_ref[0] // QUAD) % 2
            return (0, (high ^ side) * QUAD + (quarter ^ k))

        return index

    whole = lambda k, meta_ref: (0, 0)
    sizes = [size for _, size in chunks for _ in range(pieces)]
    return pl.pallas_call(
        functools.partial(pack_body, chunks, pieces),
        grid_spec=pltpu.PrefetchScalarGridSpec(
            num_scalar_prefetch=1,
            grid=(QUAD,),
            in_specs=[
                pl.BlockSpec((rows, 1), whole),
                pl.BlockSpec((1, rows), whole),
                pl.BlockSpec((rows, part), column_of(0)),
                pl.BlockSpec((rows, part), column_of(1)),
            ],
            out_specs=[pl.BlockSpec((size, part), lambda k, meta_ref: (0, k)) for size in sizes],
        ),
        out_shape=[jax.ShapeDtypeStruct((size, QUAD * part), jnp.bfloat16) for size in sizes],
        compiler_params=pltpu.CompilerParams(vmem_limit_bytes=48 << 20),
        cost_estimate=pl.CostEstimate(
            flops=2 * rows * width * sum(sizes), bytes_accessed=8 * rows * width, transcendentals=0
        ),
        name="pack_rows",
    )(meta, ids, ids.reshape(1, rows), tokens, tokens)


def unpack_body(chunks, pieces, meta_ref, column_ref, row_ref, gate_ref, *refs):
    parts, out_ref = refs[:-1], refs[-1]
    expert_column, place_column = chosen_slots(meta_ref, column_ref[...], row_ref[...])
    my_expert = meta_ref[0] // GROUP
    gate = gate_ref[...]

    def blend(side):
        total = jnp.zeros(out_ref.shape, jnp.float32)
        for number, (start, size) in enumerate(chunks):
            for far in range(pieces // 2):
                picks = selector(expert_column, place_column, my_expert ^ far, start, size)
                part = parts[number * pieces + 2 * far + side]
                total = total + jnp.dot(picks, part[...], preferred_element_type=jnp.float32)
        out_ref[...] = (total * gate).astype(jnp.bfloat16)

    for side in range(2):
        pl.when(pl.program_id(0) == side)(functools.partial(blend, side))


def unpack(meta, ids, gates, returned, chunks, pieces, width):
    rows = ids.shape[0]
    part = width // GROUP

    def out_index(side, k, meta_ref):
        quarter = meta_ref[0] % QUAD
        high = (meta_ref[0] // QUAD) % 2
        return (0, (high ^ side) * QUAD + (quarter ^ k))

    near = lambda side, k, meta_ref: (0, jnp.where(side == 0, k, QUAD - 1))
    far = lambda side, k, meta_ref: (0, jnp.where(side == 1, k, 0))
    whole = lambda side, k, meta_ref: (0, 0)
    specs = []
    for _, size in chunks:
        for piece in range(pieces):
            specs.append(pl.BlockSpec((size, part), far if piece % 2 else near))
    return pl.pallas_call(
        functools.partial(unpack_body, chunks, pieces),
        grid_spec=pltpu.PrefetchScalarGridSpec(
            num_scalar_prefetch=1,
            grid=(2, QUAD),
            in_specs=[
                pl.BlockSpec((rows, 1), whole),
                pl.BlockSpec((1, rows), whole),
                pl.BlockSpec((rows, 1), whole),
            ]
            + specs,
            out_specs=pl.BlockSpec((rows, part), out_index),
        ),
        out_shape=jax.ShapeDtypeStruct((rows, width), jnp.bfloat16),
        compiler_params=pltpu.CompilerParams(vmem_limit_bytes=48 << 20),
        cost_estimate=pl.CostEstimate(
            flops=4 * rows * rows * width, bytes_accessed=4 * rows * width, transcendentals=0
        ),
        name="unpack_rows",
    )(meta, ids, ids.reshape(1, rows), gates, *returned)


def latent_rows(token_rows, weight, gain, length):
    projected = jnp.dot(token_rows, weight, preferred_element_type=jnp.float32)
    lat_width = gain.shape[0]
    compressed = projected[:, :lat_width]
    rotary = projected[:, lat_width:]
    inverse_rms = lax.rsqrt(jnp.mean(compressed * compressed, axis=1, keepdims=True) + norm_eps)
    normed = compressed * inverse_rms * gain[None, :]
    half_cols = rotary.shape[1] // 2
    positions = jnp.arange(token_rows.shape[0], dtype=jnp.int32)
    frequency = rope_base ** (-jnp.arange(half_cols, dtype=jnp.float32) / half_cols)
    angles = positions.astype(jnp.float32)[:, None] * frequency[None, :]
    cosine = jnp.cos(angles)
    sine_part = jnp.sin(angles)
    left_half = rotary[:, :half_cols]
    right_half = rotary[:, half_cols:]
    turned = jnp.concatenate(
        [left_half * cosine - right_half * sine_part, left_half * sine_part + right_half * cosine],
        axis=1,
    )
    result = jnp.concatenate([normed, turned], axis=1)
    return jnp.where((positions < length)[:, None], result, 0.0).astype(jnp.bfloat16)


def gathered_latent(latent_weight, rank, rank_count):
    held = latent_weight
    levels = rank_count.bit_length() - 1
    for step, level in enumerate(range(levels - 1, -1, -1)):
        came = swapped(held, 1 << level)
        upper = (rank >> level) & 1 == 1
        held = jnp.where(
            upper, jnp.stack([came, held], axis=step), jnp.stack([held, came], axis=step)
        )
    return held.reshape(rank_count * latent_weight.shape[0], latent_weight.shape[1])


def four_shards(own):
    next_core = swapped(own, 1)
    across = swapped(own, 2)
    return [own, next_core, across, swapped(across, 1)]


def shards(
    tokens, lengths, latent_weight, latent_gain, expert_ids, gate_weights, gate_up, down_weight
):
    rows, width = tokens.shape
    rank_count = lax.axis_size("dp")
    rank = lax.axis_index("dp")
    experts = rank_count // GROUP
    pieces = rank_count // QUAD
    hidden_units = gate_up.shape[1] // 2
    length = lengths[rank]
    meta = jnp.stack([rank.astype(jnp.int32), length])
    capacity = rows // experts + 2
    chunks = [(0, -(-capacity // 8) * 8)]
    evens, odds = range(0, pieces, 2), range(1, pieces, 2)

    packed = pack(meta, expert_ids, tokens, chunks, pieces)
    weight_in = jnp.concatenate(four_shards(gate_up), axis=0)
    weight_out = jnp.concatenate(four_shards(down_weight), axis=1)

    returned = []
    for number, (_, size) in enumerate(chunks):
        sent = packed[number * pieces : (number + 1) * pieces]
        arrived = [sent[0]] + [swapped(sent[t], QUAD * t) for t in range(1, pieces)]
        theirs = jnp.dot(
            jnp.concatenate([arrived[t] for t in odds], axis=0),
            weight_in,
            preferred_element_type=jnp.float32,
        ).astype(jnp.bfloat16)
        ours = jnp.dot(
            jnp.concatenate([arrived[t] for t in evens], axis=0),
            weight_in,
            preferred_element_type=jnp.float32,
        )
        summed = ours + swapped(theirs, QUAD).astype(jnp.float32)
        hidden = (
            jax.nn.silu(summed[:, :hidden_units]) * summed[:, hidden_units:]
        ).astype(jnp.bfloat16)
        partner = swapped(hidden, QUAD)
        made = [
            jnp.dot(block, weight_out, preferred_element_type=jnp.float32).astype(jnp.bfloat16)
            for block in (hidden, partner)
        ]
        back = []
        for t in range(pieces):
            piece = made[t % 2][t // 2 * size : (t // 2 + 1) * size]
            back.append(swapped(piece, QUAD * t) if t else piece)
        returned += back
    moe_out = unpack(meta, expert_ids, gate_weights, returned, chunks, pieces, width)

    weight = gathered_latent(latent_weight, rank, rank_count)
    latent_cache = latent_rows(tokens, weight, latent_gain, length)
    return (latent_cache, moe_out)


def solution(mesh):
    placed = (
        P(("groups", "dp"), None),
        P("groups"),
        P("dp", None),
        P(),
        P(("groups", "dp"), None),
        P(("groups", "dp"), None),
        P("dp", None),
        P("dp", None),
    )
    return jax.shard_map(
        shards,
        mesh=mesh,
        in_specs=placed,
        out_specs=(P(("groups", "dp"), None), P(("groups", "dp"), None)),
        check_vma=False,
    )
```

time: 601 us -> 395 us (0.66)
  waiting for transfers between devices: 420 us -> 272 us
  local copies, waits for them, and re-layouts: 76.9 us -> 31.7 us
  between operations: 15 us -> 0.91 us
  Pallas kernels: 0 us -> 13.1 us
  matrix products: 37.1 us -> 28.3 us
    all_to_all x2 -> x0, waiting for transfers between devices: 150 us -> none  [the longest x1 84.5 us: shards(): lax.all_to_all(outbox, 'dp', split_axis=0, concat_axis=0, tiled=True)]
    scatter x2 -> x0, local copies, waits for them, and re-layouts: 37.6 us -> none  [shards(): outbox = jnp.zeros((experts, GROUP, capacity, part_width), jnp.bfloat16)....]
    select_n x4 -> x7, other arithmetic: 6.3 us -> 25.1 us  [gathered_latent(): jnp.where(upper, jnp.stack([came, held], axis=step), jnp.stack([held, cam...]
    reshape x4 -> x0, local copies, waits for them, and re-layouts: 16.8 us -> none  [the longest x1 4.89 us: shards(): processed = produced.reshape(source_count, item_count, produced.shape[1])]
    ppermute x6 -> x18, starting transfers between devices: 6.3 us -> 20.8 us  [swapped(): lax.ppermute(block, 'dp', [(low, low ^ bits) for low in range(count)])]
    pallas_call x0 -> x2, Pallas kernels: none -> 13.1 us  [the longest x1 7.69 us: unpack(): pl.pallas_call(functools.partial(unpack_body, chunks, pieces), grid_spec=...]
    add x3 -> x0, other arithmetic: 12.4 us -> none  [shards(): current = kept_half.astype(jnp.float32) + received.astype(jnp.float32)]
    all_to_all x2 -> x0, starting transfers between devices: 9.99 us -> none  [the longest x1 5.46 us: shards(): lax.all_to_all(processed, 'dp', split_axis=0, concat_axis=0, tiled=True)]
  transfers between devices with their start and end apart: 9 -> 18, of which waited for: 8 -> 12; matrix products, arithmetic and copies ran while one was open for 9% -> 20% of each run, Pallas kernels for 0% -> 1%
where the time goes in v1:
time: 395 us
  waiting for transfers between devices  272 us (69%)
  local copies, waits for them, and re-layouts  31.7 us (8%)
  matrix products  28.3 us (7%)
  other arithmetic  27.8 us (7%)
  starting transfers between devices  20.8 us (5%)
  Pallas kernels  13.1 us (3%)
    ppermute x18, waiting for transfers between devices, swapped(): lax.ppermute(block, 'dp', [(low, low ^ bits) for low in range(count)])  272 us
    select_n x7, other arithmetic, gathered_latent(): jnp.where(upper, jnp.stack([came, held], axis=step), jnp.stack([held, cam...  25.1 us
    ppermute x18, starting transfers between devices, swapped(): lax.ppermute(block, 'dp', [(low, low ^ bits) for low in range(count)])  20.8 us
    unnamed x30, local copies, waits for them, and re-layouts  17.5 us
    dot_general x1, matrix products, shards(): jnp.dot(jnp.concatenate([arrived[t] for t in odds], axis=0), weight_in, p...  8.74 us
    select_n x1, local copies, waits for them, and re-layouts, gathered_latent(): jnp.where(upper, jnp.stack([came, held], axis=step), jnp.stack([held, cam...  7.95 us
  transfers between devices with their start and end apart: 18, of which 12 were waited for; matrix products, arithmetic and copies ran while one was open for 20% of the time, Pallas kernels for 1%

profile of v1, /device:TPU:8, one launch (start us, length us, event | category | flops | bytes accessed | tf_op | source)
XLA Modules:
  0.0 394.8 jit_solution(242233547430285307)
XLA Ops:
  4.8 24.4 %collective-permute-done = bf16[448,576]{1,0:T(8,128)(2,1)S(1)} collective-permute-done((bf16[448,576]{1,0:T(8,128)(2,1)}, bf16[448,576]{1,0:T(8,128)(2,1)S(1)}, u32[]{:S(2)}, u32[]{:S(2)}) %collective-permute-start) | collective-permute-done | bytes 516128 | tf_op jit(solution)/shard_map/ppermute | solution.py:19
  34.9 23.2 %collective-permute-done.1 = bf16[2,448,576]{2,1,0:T(8,128)(2,1)S(1)} collective-permute-done((bf16[2,448,576]{2,1,0:T(8,128)(2,1)S(1)}, bf16[2,448,576]{2,1,0:T(8,128)(2,1)S(1)}, u32[]{:S(2)}, u32[]{:S(2)}) %collective-permute-start.1) | collective-permute-done | bytes 1032224 | tf_op jit(solution)/shard_map/ppermute | solution.py:19
  63.3 19.9 %collective-permute-done.6 = bf16[896,2048]{1,0:T(8,128)(2,1)} collective-permute-done((bf16[896,2048]{1,0:T(8,128)(2,1)}, bf16[896,2048]{1,0:T(8,128)(2,1)}, u32[]{:S(2)}, u32[]{:S(2)}) %collective-permute-start.6) | collective-permute-done | bytes 3670048 | tf_op jit(solution)/shard_map/ppermute | solution.py:19
  83.7 4.0 %fusion.9 = (bf16[2,2,1,448,576]{4,3,0,1,2:T(8,128)(2,1)S(1)}, bf16[2,2,1,1,448,576]{5,4,0,1,3,2:T(8,128)(2,1)}) fusion(bf16[2,1,1,448,576]{4,3,0,2,1:T(8,128)(2,1)} %bitcast.39, bf16[2,1,1,448,576]{4,3,0,2,1:T(8,128)(2,1)} %get-tuple-element.17, pred[]{:T(512)S(6)} %eq.14), kind=kLoop, calls=%fused_computation.25 | loop fusion | flops 3096576 | bytes 6193153 | tf_op jit(solution)/shard_map/jit(_where)/select_n | solution.py:179
  87.7 82.8 %collective-permute-done.12 = bf16[1024,896]{1,0:T(8,128)(2,1)} collective-permute-done((bf16[1024,896]{1,0:T(8,128)(2,1)}, bf16[1024,896]{1,0:T(8,128)(2,1)}, u32[]{:S(2)}, u32[]{:S(2)}) %collective-permute-start.12) | collective-permute-done | bytes 1835040 | tf_op jit(solution)/shard_map/ppermute | solution.py:19
  170.6 2.9 maximum_select_fusion.1
  176.1 2.9 constant_dynamic-update-slice_fusion.7
  179.1 5.4 %pack_rows.1 = (bf16[136,3584]{1,0:T(8,128)(2,1)S(1)}, bf16[136,3584]{1,0:T(8,128)(2,1)S(1)}, bf16[136,3584]{1,0:T(8,128)(2,1)S(1)}, bf16[136,3584]{1,0:T(8,128)(2,1)S(1)}) custom-call(s32[2]{0:T(128)S(1)} %pad_add_fusion.meta_ref, s32[256,1]{1,0:T(8,128)S(1)} %copy.23.column_ref, s32[1,256]{1,0:T(1,128)S(1)} %bitcast.33, bf16[256,7168]{1,0:T(8,128)(2,1)} %other_ref.1, ...), custom_call_target="tpu_custom_call" | custom-call | flops 1996488704 | bytes 14680064 | tf_op jit(solution)/shard_map/pack_rows/pallas_call | solution.py:71
  188.6 2.9 constant_dynamic-update-slice_fusion.6
  191.5 2.9 constant_dynamic-update-slice_fusion.5
  198.2 2.9 constant_dynamic-update-slice_fusion.4
  208.6 24.4 %collective-permute-done.9 = bf16[136,3584]{1,0:T(8,128)(2,1)S(1)} collective-permute-done((bf16[136,3584]{1,0:T(8,128)(2,1)S(1)}, bf16[136,3584]{1,0:T(8,128)(2,1)S(1)}, u32[]{:S(2)}, u32[]{:S(2)}) %collective-permute-start.9) | collective-permute-done | bytes 974880 | tf_op jit(solution)/shard_map/ppermute | solution.py:19
  234.5 8.7 %convolution_convert_fusion.2 = bf16[272,2048]{1,0:T(8,128)(2,1)} fusion(bf16[3584,2048]{1,0:T(8,128)(2,1)} %copy-done.5, bf16[136,3584]{1,0:T(8,128)(2,1)S(1)} %collective-permute-done.9, bf16[136,3584]{1,0:T(8,128)(2,1)S(1)} %collective-permute-done.8), kind=kOutput, calls=%fused_computation.6 | convolution fusion | flops 3997433856 | bytes 17743872 | tf_op jit(solution)/shard_map/dot_general | solution.py:214
  243.6 10.5 %maximum_select_fusion = bf16[2,2,2,2,448,576]{5,4,0,1,3,2:T(8,128)(2,1)} fusion(bf16[2,2,2,1,448,576]{5,4,0,1,3,2:T(8,128)(2,1)S(1)} %maximum_select_fusion.2, bf16[2,2,2,1,448,576]{5,4,0,1,3,2:T(8,128)(2,1)} %bitcast.13, pred[]{:T(512)S(6)} %eq.12), kind=kLoop, calls=%fused_computation | loop fusion | flops 12386304 | bytes 16515073 | tf_op jit(solution)/shard_map/jit(_where)/select_n | solution.py:179
  254.1 8.0 %copy.21 = bf16[2,2,2,2,448,576]{5,4,3,2,1,0:T(8,128)(2,1)} copy(bf16[2,2,2,2,448,576]{5,4,0,1,3,2:T(8,128)(2,1)} %maximum_select_fusion) | data formatting | bytes 16515072 | tf_op jit(solution)/shard_map/jit(_where)/select_n | solution.py:179
  262.1 7.4 %convolution_bitcast_fusion = f32[256,576]{0,1:T(8,128)S(1)} fusion(bf16[7168,576]{1,0:T(8,128)(2,1)} %bitcast.37, bf16[256,7168]{1,0:T(8,128)(2,1)} %other_ref.1), kind=kOutput, calls=%fused_computation.15 | convolution fusion | flops 2113929216 | bytes 12517376 | tf_op jit(solution)/shard_map/dot_general | solution.py:151
  269.4 2.9 collective-permute-done.4
  272.3 15.6 %collective-permute-done.10 = bf16[272,2048]{1,0:T(8,128)(2,1)S(1)} collective-permute-done((bf16[272,2048]{1,0:T(8,128)(2,1)}, bf16[272,2048]{1,0:T(8,128)(2,1)S(1)}, u32[]{:S(2)}, u32[]{:S(2)}) %collective-permute-start.10) | collective-permute-done | bytes 1114144 | tf_op jit(solution)/shard_map/ppermute | solution.py:19
  287.9 7.9 %convolution_add_fusion = f32[272,2048]{1,0:T(8,128)S(1)} fusion(bf16[3584,2048]{1,0:T(8,128)(2,1)} %copy-done.5, bf16[272,2048]{1,0:T(8,128)(2,1)S(1)} %collective-permute-done.10, bf16[136,3584]{1,0:T(8,128)(2,1)} %collective-permute-done.4, bf16[136,3584]{1,0:T(8,128)(2,1)S(1)} %get-tuple-element.6), kind=kOutput, calls=%fused_computation.5 | convolution fusion | flops 3997990912 | bytes 19972096 | tf_op jit(solution)/shard_map/dot_general | solution.py:219
  303.1 16.1 %collective-permute-done.14 = bf16[272,1024]{1,0:T(8,128)(2,1)S(1)} collective-permute-done((bf16[272,1024]{1,0:T(8,128)(2,1)S(1)}, bf16[272,1024]{1,0:T(8,128)(2,1)S(1)}, u32[]{:S(2)}, u32[]{:S(2)}) %collective-permute-start.14) | collective-permute-done | bytes 557088 | tf_op jit(solution)/shard_map/ppermute | solution.py:19
  325.8 20.2 %collective-permute-done.16.refs_2_ = bf16[136,3584]{1,0:T(8,128)(2,1)S(1)} collective-permute-done((bf16[136,3584]{1,0:T(8,128)(2,1)S(1)}, bf16[136,3584]{1,0:T(8,128)(2,1)S(1)}, u32[]{:S(2)}, u32[]{:S(2)}) %collective-permute-start.16) | collective-permute-done | bytes 974880 | tf_op jit(solution)/shard_map/ppermute | solution.py:19
  346.0 29.9 %collective-permute-done.15.refs_1_ = bf16[136,3584]{1,0:T(8,128)(2,1)S(1)} collective-permute-done((bf16[136,3584]{1,0:T(8,128)(2,1)S(1)}, bf16[136,3584]{1,0:T(8,128)(2,1)S(1)}, u32[]{:S(2)}, u32[]{:S(2)}) %collective-permute-start.15) | collective-permute-done | bytes 974880 | tf_op jit(solution)/shard_map/ppermute | solution.py:19
  375.9 11.2 %collective-permute-done.17.refs_3_ = bf16[136,3584]{1,0:T(8,128)(2,1)S(1)} collective-permute-done((bf16[136,3584]{1,0:T(8,128)(2,1)S(1)}, bf16[136,3584]{1,0:T(8,128)(2,1)S(1)}, u32[]{:S(2)}, u32[]{:S(2)}) %collective-permute-start.17) | collective-permute-done | bytes 974880 | tf_op jit(solution)/shard_map/ppermute | solution.py:19
  387.1 7.7 %unpack_rows.1 = bf16[256,7168]{1,0:T(8,128)(2,1)} custom-call(s32[2]{0:T(128)S(1)} %pad_add_fusion.meta_ref, s32[256,1]{1,0:T(8,128)S(1)} %copy.23.column_ref, s32[1,256]{1,0:T(1,128)S(1)} %bitcast.34, f32[256,1]{1,0:T(8,128)S(1)} %copy.24.gate_ref, bf16[136,3584]{1,0:T(8,128)(2,1)S(1)} %get-tuple-element.15.refs_0_, ...), custom_call_target="tpu_custom_call" | custom-call | flops 1879048192 | bytes 7340032 | tf_op jit(solution)/shard_map/unpack_rows/pallas_call | solution.py:128
  (73 shorter events, 49.2 us)
Async XLA Ops:
  0.6 82.6 %collective-permute-start.6 = (bf16[896,2048]{1,0:T(8,128)(2,1)}, bf16[896,2048]{1,0:T(8,128)(2,1)}, u32[]{:S(2)}, u32[]{:S(2)}) collective-permute-start(bf16[896,2048]{1,0:T(8,128)(2,1)} %param.14), channel_id=1, source_target_pairs={{0,2},{1,3},{2,0},{3,1},{4,6},{5,7},{6,4},{7,5},{8,10},{9,11},{10,... | collective-permute-start | bytes 11010056 | tf_op jit(solution)/shard_map/ppermute | solution.py:19
  2.2 27.0 %collective-permute-start = (bf16[448,576]{1,0:T(8,128)(2,1)}, bf16[448,576]{1,0:T(8,128)(2,1)S(1)}, u32[]{:S(2)}, u32[]{:S(2)}) collective-permute-start(bf16[448,576]{1,0:T(8,128)(2,1)} %param.10), channel_id=1, source_target_pairs={{0,8},{1,9},{2,10},{3,11},{4,12},{5,13},{6,14},{7,15},{8,0},{9,1},... | collective-permute-start | bytes 1548296 | tf_op jit(solution)/shard_map/ppermute | solution.py:19
  30.9 27.3 %collective-permute-start.1 = (bf16[2,448,576]{2,1,0:T(8,128)(2,1)S(1)}, bf16[2,448,576]{2,1,0:T(8,128)(2,1)S(1)}, u32[]{:S(2)}, u32[]{:S(2)}) collective-permute-start(bf16[2,448,576]{2,1,0:T(8,128)(2,1)S(1)} %maximum_select_fusion.5), channel_id=1, source_target_pairs={{0,4},{1,5},{2,6},{3,7},{4,0},{5,1},{6,2},{7,3},{8,12},{9,13},{10,... | collective-permute-start | bytes 3096584 | tf_op jit(solution)/shard_map/ppermute | solution.py:19
  61.3 109.3 %collective-permute-start.2 = (bf16[2,2,448,576]{3,2,0,1:T(8,128)(2,1)}, bf16[2,2,448,576]{3,2,0,1:T(8,128)(2,1)S(1)}, u32[]{:S(2)}, u32[]{:S(2)}) collective-permute-start(bf16[2,2,448,576]{3,2,0,1:T(8,128)(2,1)} %maximum_select_fusion.3), channel_id=1, source_target_pairs={{0,2},{1,3},{2,0},{3,1},{4,6},{5,7},{6,4},{7,5},{8,10},{9,11},{10,... | collective-permute-start | bytes 6193160 | tf_op jit(solution)/shard_map/ppermute | solution.py:19
  61.8 108.8 %collective-permute-start.12 = (bf16[1024,896]{1,0:T(8,128)(2,1)}, bf16[1024,896]{1,0:T(8,128)(2,1)}, u32[]{:S(2)}, u32[]{:S(2)}) collective-permute-start(bf16[1024,896]{1,0:T(8,128)(2,1)} %param.15), channel_id=1, source_target_pairs={{0,2},{1,3},{2,0},{3,1},{4,6},{5,7},{6,4},{7,5},{8,10},{9,11},{10,... | collective-permute-start | bytes 5505032 | tf_op jit(solution)/shard_map/ppermute | solution.py:19
  63.3 137.8 %collective-permute-start.5 = (bf16[896,2048]{1,0:T(8,128)(2,1)}, bf16[896,2048]{1,0:T(8,128)(2,1)}, u32[]{:S(2)}, u32[]{:S(2)}) collective-permute-start(bf16[896,2048]{1,0:T(8,128)(2,1)} %param.14), channel_id=1, source_target_pairs={{0,1},{1,0},{2,3},{3,2},{4,5},{5,4},{6,7},{7,6},{8,9},{9,8},{10,11... | collective-permute-start | bytes 11010056 | tf_op jit(solution)/shard_map/ppermute | solution.py:19
  83.2 122.9 %collective-permute-start.7 = (bf16[896,2048]{1,0:T(8,128)(2,1)}, bf16[896,2048]{1,0:T(8,128)(2,1)}, u32[]{:S(2)}, u32[]{:S(2)}) collective-permute-start(bf16[896,2048]{1,0:T(8,128)(2,1)} %collective-permute-done.6), channel_id=1, source_target_pairs={{0,1},{1,0},{2,3},{3,2},{4,5},{5,4},{6,7},{7,6},{8,9},{9,8},{10,11... | collective-permute-start | bytes 11010056 | tf_op jit(solution)/shard_map/ppermute | solution.py:19
  83.2 103.7 %collective-permute-start.11 = (bf16[1024,896]{1,0:T(8,128)(2,1)}, bf16[1024,896]{1,0:T(8,128)(2,1)}, u32[]{:S(2)}, u32[]{:S(2)}) collective-permute-start(bf16[1024,896]{1,0:T(8,128)(2,1)} %param.15), channel_id=1, source_target_pairs={{0,1},{1,0},{2,3},{3,2},{4,5},{5,4},{6,7},{7,6},{8,9},{9,8},{10,11... | collective-permute-start | bytes 5505032 | tf_op jit(solution)/shard_map/ppermute | solution.py:19
  170.6 25.1 %collective-permute-start.13 = (bf16[1024,896]{1,0:T(8,128)(2,1)}, bf16[1024,896]{1,0:T(8,128)(2,1)}, u32[]{:S(2)}, u32[]{:S(2)}) collective-permute-start(bf16[1024,896]{1,0:T(8,128)(2,1)} %collective-permute-done.12), channel_id=1, source_target_pairs={{0,1},{1,0},{2,3},{3,2},{4,5},{5,4},{6,7},{7,6},{8,9},{9,8},{10,11... | collective-permute-start | bytes 5505032 | tf_op jit(solution)/shard_map/ppermute | solution.py:19
  170.6 3.7 copy-start.8
  173.5 70.1 %collective-permute-start.3 = (bf16[2,2,2,448,576]{4,3,0,1,2:T(8,128)(2,1)}, bf16[2,2,2,448,576]{4,3,0,1,2:T(8,128)(2,1)}, u32[]{:S(2)}, u32[]{:S(2)}) collective-permute-start(bf16[2,2,2,448,576]{4,3,0,1,2:T(8,128)(2,1)} %maximum_select_fusion.1), channel_id=1, source_target_pairs={{0,1},{1,0},{2,3},{3,2},{4,5},{5,4},{6,7},{7,6},{8,9},{9,8},{10,11... | collective-permute-start | bytes 12386312 | tf_op jit(solution)/shard_map/ppermute | solution.py:19
  186.9 7.5 %copy-start.2 = (bf16[2,2,448,576]{3,2,0,1:T(8,128)(2,1)S(1)}, bf16[2,2,448,576]{3,2,0,1:T(8,128)(2,1)}, u32[]{:S(2)}) copy-start(bf16[2,2,448,576]{3,2,0,1:T(8,128)(2,1)} %copy-done.1) | copy-start | bytes 6193156
  187.0 7.5 %copy-start.3 = (bf16[2,2,1,1,448,576]{5,4,0,1,3,2:T(8,128)(2,1)S(1)}, bf16[2,2,1,1,448,576]{5,4,0,1,3,2:T(8,128)(2,1)}, u32[]{:S(2)}) copy-start(bf16[2,2,1,1,448,576]{5,4,0,1,3,2:T(8,128)(2,1)} %get-tuple-element.11) | copy-start | bytes 6193156
  187.0 46.0 %collective-permute-start.9 = (bf16[136,3584]{1,0:T(8,128)(2,1)S(1)}, bf16[136,3584]{1,0:T(8,128)(2,1)S(1)}, u32[]{:S(2)}, u32[]{:S(2)}) collective-permute-start(bf16[136,3584]{1,0:T(8,128)(2,1)S(1)} %get-tuple-element.9), channel_id=1, source_target_pairs={{0,12},{1,13},{2,14},{3,15},{4,8},{5,9},{6,10},{7,11},{8,4},{9,5},... | collective-permute-start | bytes 2924552 | tf_op jit(solution)/shard_map/ppermute | solution.py:19
  195.7 38.8 %collective-permute-start.8 = (bf16[136,3584]{1,0:T(8,128)(2,1)S(1)}, bf16[136,3584]{1,0:T(8,128)(2,1)S(1)}, u32[]{:S(2)}, u32[]{:S(2)}) collective-permute-start(bf16[136,3584]{1,0:T(8,128)(2,1)S(1)} %get-tuple-element.8), channel_id=1, source_target_pairs={{0,4},{1,5},{2,6},{3,7},{4,0},{5,1},{6,2},{7,3},{8,12},{9,13},{10,... | collective-permute-start | bytes 2924552 | tf_op jit(solution)/shard_map/ppermute | solution.py:19
  201.1 71.2 %collective-permute-start.4 = (bf16[136,3584]{1,0:T(8,128)(2,1)S(1)}, bf16[136,3584]{1,0:T(8,128)(2,1)}, u32[]{:S(2)}, u32[]{:S(2)}) collective-permute-start(bf16[136,3584]{1,0:T(8,128)(2,1)S(1)} %get-tuple-element.7), channel_id=1, source_target_pairs={{0,8},{1,9},{2,10},{3,11},{4,12},{5,13},{6,14},{7,15},{8,0},{9,1},... | collective-permute-start | bytes 2924552 | tf_op jit(solution)/shard_map/ppermute | solution.py:19
  208.6 24.4 %copy-start.5 = (bf16[3584,2048]{1,0:T(8,128)(2,1)}, bf16[3584,2048]{1,0:T(8,128)(2,1)S(1)}, u32[]{:S(2)}) copy-start(bf16[3584,2048]{1,0:T(8,128)(2,1)S(1)} %constant_dynamic-update-slice_fusion) | copy-start | bytes 44040196
  243.2 44.7 %collective-permute-start.10 = (bf16[272,2048]{1,0:T(8,128)(2,1)}, bf16[272,2048]{1,0:T(8,128)(2,1)S(1)}, u32[]{:S(2)}, u32[]{:S(2)}) collective-permute-start(bf16[272,2048]{1,0:T(8,128)(2,1)} %convolution_convert_fusion.2), channel_id=1, source_target_pairs={{0,4},{1,5},{2,6},{3,7},{4,0},{5,1},{6,2},{7,3},{8,12},{9,13},{10,... | collective-permute-start | bytes 3342344 | tf_op jit(solution)/shard_map/ppermute | solution.py:19
  262.1 36.5 %slice-start = ((s8[7340032]{0:T(1024)(128)(4,1)}), s8[4194304]{0:T(1024)(128)(4,1)S(1)}, s32[]{:S(2)}) async-start(s8[7340032]{0:T(1024)(128)(4,1)} %bitcast.44), calls=%async_computation | async-start | bytes 8388608
  287.9 10.7 %slice-start.1 = ((s8[7340032]{0:T(1024)(128)(4,1)}), s8[3145728]{0:T(1024)(128)(4,1)S(1)}, s32[]{:S(2)}) async-start(s8[7340032]{0:T(1024)(128)(4,1)} %bitcast.44), calls=%async_computation.1 | async-start | bytes 6291456
  296.1 23.1 %collective-permute-start.14 = (bf16[272,1024]{1,0:T(8,128)(2,1)S(1)}, bf16[272,1024]{1,0:T(8,128)(2,1)S(1)}, u32[]{:S(2)}, u32[]{:S(2)}) collective-permute-start(bf16[272,1024]{1,0:T(8,128)(2,1)S(1)} %fusion.6), channel_id=1, source_target_pairs={{0,4},{1,5},{2,6},{3,7},{4,0},{5,1},{6,2},{7,3},{8,12},{9,13},{10,... | collective-permute-start | bytes 1671176 | tf_op jit(solution)/shard_map/ppermute | solution.py:19
  300.9 45.2 %collective-permute-start.16 = (bf16[136,3584]{1,0:T(8,128)(2,1)S(1)}, bf16[136,3584]{1,0:T(8,128)(2,1)S(1)}, u32[]{:S(2)}, u32[]{:S(2)}) collective-permute-start(bf16[136,3584]{1,0:T(8,128)(2,1)S(1)} %get-tuple-element.14), channel_id=1, source_target_pairs={{0,8},{1,9},{2,10},{3,11},{4,12},{5,13},{6,14},{7,15},{8,0},{9,1},... | collective-permute-start | bytes 2924552 | tf_op jit(solution)/shard_map/ppermute | solution.py:19
  321.5 54.4 %collective-permute-start.15 = (bf16[136,3584]{1,0:T(8,128)(2,1)S(1)}, bf16[136,3584]{1,0:T(8,128)(2,1)S(1)}, u32[]{:S(2)}, u32[]{:S(2)}) collective-permute-start(bf16[136,3584]{1,0:T(8,128)(2,1)S(1)} %get-tuple-element.13), channel_id=1, source_target_pairs={{0,4},{1,5},{2,6},{3,7},{4,0},{5,1},{6,2},{7,3},{8,12},{9,13},{10,... | collective-permute-start | bytes 2924552 | tf_op jit(solution)/shard_map/ppermute | solution.py:19
  324.1 63.0 %collective-permute-start.17 = (bf16[136,3584]{1,0:T(8,128)(2,1)S(1)}, bf16[136,3584]{1,0:T(8,128)(2,1)S(1)}, u32[]{:S(2)}, u32[]{:S(2)}) collective-permute-start(bf16[136,3584]{1,0:T(8,128)(2,1)S(1)} %get-tuple-element.12), channel_id=1, source_target_pairs={{0,12},{1,13},{2,14},{3,15},{4,8},{5,9},{6,10},{7,11},{8,4},{9,5},... | collective-permute-start | bytes 2924552 | tf_op jit(solution)/shard_map/ppermute | solution.py:19
  (5 other events, 14.5 us)

commit v2 on v1

--- a/solution.py
+++ b/solution.py
@@ -37,16 +37,14 @@
     return hit.astype(jnp.float32).astype(jnp.bfloat16)
 
 
-def pack_body(chunks, pieces, meta_ref, column_ref, row_ref, same_ref, other_ref, *outs):
+def pack_body(chunks, meta_ref, column_ref, row_ref, low_ref, high_ref, *outs):
     expert_column, place_column = chosen_slots(meta_ref, column_ref[...], row_ref[...])
-    my_expert = meta_ref[0] // GROUP
-    same = same_ref[...]
-    other = other_ref[...]
-    for number, (start, size) in enumerate(chunks):
-        for far in range(pieces // 2):
-            picks = selector(expert_column, place_column, my_expert ^ far, start, size)
-            for side, source in enumerate((same, other)):
-                outs[number * pieces + 2 * far + side][...] = lax.dot_general(
+    sources = (low_ref[...], high_ref[...])
+    for (start, size), out_ref in zip(chunks, outs):
+        for expert in range(out_ref.shape[0] // 2):
+            picks = selector(expert_column, place_column, expert, start, size)
+            for side, source in enumerate(sources):
+                out_ref[2 * expert + side] = lax.dot_general(
                     picks,
                     source,
                     (((0,), (0,)), ((), ())),
@@ -59,17 +57,11 @@
     part = width // GROUP
 
     def column_of(side):
-        def index(k, meta_ref):
-            quarter = meta_ref[0] % QUAD
-            high = (meta_ref[0] // QUAD) % 2
-            return (0, (high ^ side) * QUAD + (quarter ^ k))
-
-        return index
+        return lambda k, meta_ref: (0, side * QUAD + ((meta_ref[0] % QUAD) ^ k))
 
     whole = lambda k, meta_ref: (0, 0)
-    sizes = [size for _, size in chunks for _ in range(pieces)]
-    return pl.pallas_call(
-        functools.partial(pack_body, chunks, pieces),
+    return pl.pallas_call(
+        functools.partial(pack_body, chunks),
         grid_spec=pltpu.PrefetchScalarGridSpec(
             num_scalar_prefetch=1,
             grid=(QUAD,),
@@ -79,12 +71,17 @@
                 pl.BlockSpec((rows, part), column_of(0)),
                 pl.BlockSpec((rows, part), column_of(1)),
             ],
-            out_specs=[pl.BlockSpec((size, part), lambda k, meta_ref: (0, k)) for size in sizes],
-        ),
-        out_shape=[jax.ShapeDtypeStruct((size, QUAD * part), jnp.bfloat16) for size in sizes],
-        compiler_params=pltpu.CompilerParams(vmem_limit_bytes=48 << 20),
+            out_specs=[
+                pl.BlockSpec((pieces, size, part), lambda k, meta_ref: (0, 0, k))
+                for _, size in chunks
+            ],
+        ),
+        out_shape=[
+            jax.ShapeDtypeStruct((pieces, size, QUAD * part), jnp.bfloat16) for _, size in chunks
+        ],
+        compiler_params=pltpu.CompilerParams(vmem_limit_bytes=58 << 20),
         cost_estimate=pl.CostEstimate(
-            flops=2 * rows * width * sum(sizes), bytes_accessed=8 * rows * width, transcendentals=0
+            flops=4 * rows * rows * width, bytes_accessed=4 * rows * width, transcendentals=0
         ),
         name="pack_rows",
     )(meta, ids, ids.reshape(1, rows), tokens, tokens)
@@ -139,7 +136,7 @@
             out_specs=pl.BlockSpec((rows, part), out_index),
         ),
         out_shape=jax.ShapeDtypeStruct((rows, width), jnp.bfloat16),
-        compiler_params=pltpu.CompilerParams(vmem_limit_bytes=48 << 20),
+        compiler_params=pltpu.CompilerParams(vmem_limit_bytes=58 << 20),
         cost_estimate=pl.CostEstimate(
             flops=4 * rows * rows * width, bytes_accessed=4 * rows * width, transcendentals=0
         ),
@@ -147,15 +144,138 @@
     )(meta, ids, ids.reshape(1, rows), gates, *returned)
 
 
-def latent_rows(token_rows, weight, gain, length):
-    projected = jnp.dot(token_rows, weight, preferred_element_type=jnp.float32)
+def idle_body(*refs):
+    del refs
+
+
+def after(value, *events):
+    anywhere = pl.BlockSpec(memory_space=pl.ANY)
+    return pl.pallas_call(
+        idle_body,
+        in_specs=[anywhere] * (1 + len(events)),
+        out_specs=anywhere,
+        out_shape=jax.ShapeDtypeStruct(value.shape, value.dtype),
+        input_output_aliases={0: 0},
+        name="after",
+    )(value, *events)
+
+
+def together(*values):
+    anywhere = pl.BlockSpec(memory_space=pl.ANY)
+    return pl.pallas_call(
+        idle_body,
+        in_specs=[anywhere] * len(values),
+        out_specs=[anywhere] * len(values),
+        out_shape=[jax.ShapeDtypeStruct(value.shape, value.dtype) for value in values],
+        input_output_aliases={number: number for number in range(len(values))},
+        name="together",
+    )(*values)
+
+
+def gate_up_body(count, first, meta_ref, *refs):
+    del meta_ref
+    parts, rest, out_ref, joined = refs[:count], refs[count:-2], refs[-2], refs[-1]
+    size = parts[0].shape[1]
+
+    @pl.when(pl.program_id(0) == 0)
+    def _():
+        for number, part in enumerate(parts):
+            joined[pl.ds(number * size, size), :] = part[0]
+
+    shares, start = rest, first
+    total = jnp.zeros(out_ref.shape, jnp.float32)
+    if first:
+        shares, total = rest[1:], rest[0][...]
+    for share in shares:
+        depth = share.shape[0]
+        total += jnp.dot(
+            joined[:, start : start + depth], share[...], preferred_element_type=jnp.float32
+        )
+        start += depth
+    out_ref[...] = total.astype(out_ref.dtype)
+
+
+def gate_up_product(meta, arrived, shares, side, dtype, first=0, base=()):
+    pieces, size, width = arrived.shape
+    count = pieces // 2
+    rows = size * count
+    columns = shares[0].shape[1]
+    tile = columns // 4
+
+    def source(number):
+        def index(n, meta_ref):
+            rank = meta_ref[0]
+            return (2 * ((rank // GROUP) ^ number) + (((rank // QUAD) % 2) ^ side), 0, 0)
+
+        return index
+
+    across = lambda n, meta_ref: (0, n)
+    return pl.pallas_call(
+        functools.partial(gate_up_body, count, first),
+        grid_spec=pltpu.PrefetchScalarGridSpec(
+            num_scalar_prefetch=1,
+            grid=(columns // tile,),
+            in_specs=[pl.BlockSpec((1, size, width), source(number)) for number in range(count)]
+            + [pl.BlockSpec((rows, tile), across) for _ in base]
+            + [pl.BlockSpec((share.shape[0], tile), across) for share in shares],
+            out_specs=pl.BlockSpec((rows, tile), across),
+            scratch_shapes=[pltpu.VMEM((rows, width), jnp.bfloat16)],
+        ),
+        out_shape=jax.ShapeDtypeStruct((rows, columns), dtype),
+        compiler_params=pltpu.CompilerParams(vmem_limit_bytes=32 << 20),
+        cost_estimate=pl.CostEstimate(
+            flops=2 * rows * width * columns,
+            bytes_accessed=2 * width * (rows + columns),
+            transcendentals=0,
+        ),
+        name="gate_up_product",
+    )(meta, *[arrived] * count, *base, *shares)
+
+
+def down_body(hidden_ref, *refs):
+    k = pl.program_id(0)
+    shares, outs = refs[:QUAD], refs[QUAD:]
+    size = outs[0].shape[0]
+    for turn in range(QUAD):
+
+        @pl.when(k == turn)
+        def _(turn=turn):
+            made = jnp.dot(
+                hidden_ref[...], shares[turn][...], preferred_element_type=jnp.float32
+            )
+            for number, out_ref in enumerate(outs):
+                out_ref[...] = made[number * size : (number + 1) * size].astype(jnp.bfloat16)
+
+
+def down_product(hidden, shares, count):
+    rows, depth = hidden.shape
+    part = shares[0].shape[1]
+    size = rows // count
+    return pl.pallas_call(
+        down_body,
+        grid=(QUAD,),
+        in_specs=[pl.BlockSpec((rows, depth), lambda k: (0, 0))]
+        + [pl.BlockSpec((depth, part), lambda k: (0, 0)) for _ in shares],
+        out_specs=[pl.BlockSpec((size, part), lambda k: (0, k)) for _ in range(count)],
+        out_shape=[jax.ShapeDtypeStruct((size, QUAD * part), jnp.bfloat16) for _ in range(count)],
+        compiler_params=pltpu.CompilerParams(vmem_limit_bytes=58 << 20),
+        cost_estimate=pl.CostEstimate(
+            flops=2 * rows * depth * QUAD * part,
+            bytes_accessed=2 * (rows * depth + QUAD * part * (rows + depth)),
+            transcendentals=0,
+        ),
+        name="down_product",
+    )(hidden, *shares)
+
+
+def latent_finish(projected, gain, length):
     lat_width = gain.shape[0]
     compressed = projected[:, :lat_width]
     rotary = projected[:, lat_width:]
     inverse_rms = lax.rsqrt(jnp.mean(compressed * compressed, axis=1, keepdims=True) + norm_eps)
     normed = compressed * inverse_rms * gain[None, :]
     half_cols = rotary.shape[1] // 2
-    positions = jnp.arange(token_rows.shape[0], dtype=jnp.int32)
+    positions = jnp.arange(projected.shape[0], dtype=jnp.int32)
     frequency = rope_base ** (-jnp.arange(half_cols, dtype=jnp.float32) / half_cols)
     angles = positions.astype(jnp.float32)[:, None] * frequency[None, :]
     cosine = jnp.cos(angles)
@@ -170,22 +290,69 @@
     return jnp.where((positions < length)[:, None], result, 0.0).astype(jnp.bfloat16)
 
 
-def gathered_latent(latent_weight, rank, rank_count):
-    held = latent_weight
-    levels = rank_count.bit_length() - 1
-    for step, level in enumerate(range(levels - 1, -1, -1)):
-        came = swapped(held, 1 << level)
-        upper = (rank >> level) & 1 == 1
-        held = jnp.where(
-            upper, jnp.stack([came, held], axis=step), jnp.stack([held, came], axis=step)
-        )
-    return held.reshape(rank_count * latent_weight.shape[0], latent_weight.shape[1])
-
-
-def four_shards(own):
-    next_core = swapped(own, 1)
-    across = swapped(own, 2)
-    return [own, next_core, across, swapped(across, 1)]
+def latent_body(codes, meta_ref, mine_ref, other_ref, *refs):
+    parts, sums, weight, done = refs[: len(codes)], refs[len(codes) : -2], refs[-2], refs[-1]
+    size = parts[0].shape[1]
+    moves = []
+    for part, group in zip(parts, codes):
+        for number, code in enumerate(group):
+            row = pl.multiple_of(((meta_ref[0] ^ code) // 2) * size, 16)
+            move = pltpu.make_async_copy(
+                part.at[number], weight.at[pl.ds(row, size), :], done.at[len(moves)]
+            )
+            move.start()
+            moves.append(move)
+    for move in moves:
+        move.wait()
+    for tokens_ref, sum_ref in zip((other_ref, mine_ref), sums):
+        product = jnp.dot(tokens_ref[...], weight[...], preferred_element_type=jnp.float32)
+        sum_ref[...] = product.astype(sum_ref.dtype)
+
+
+def latent_product(meta, mine, other, parts, codes):
+    rows, width = mine.shape
+    columns = parts[0].shape[2]
+    total = sum(len(group) for group in codes)
+    inside = pl.BlockSpec(memory_space=pltpu.VMEM)
+    return pl.pallas_call(
+        functools.partial(latent_body, codes),
+        in_specs=[pl.BlockSpec(memory_space=pltpu.SMEM), inside, inside]
+        + [pl.BlockSpec(memory_space=pl.ANY)] * len(parts),
+        out_specs=[inside, inside],
+        out_shape=[
+            jax.ShapeDtypeStruct((rows, columns), jnp.bfloat16),
+            jax.ShapeDtypeStruct((rows, columns), jnp.float32),
+        ],
+        scratch_shapes=[
+            pltpu.VMEM((width, columns), jnp.bfloat16),
+            pltpu.SemaphoreType.DMA((total,)),
+        ],
+        compiler_params=pltpu.CompilerParams(vmem_limit_bytes=32 << 20),
+        cost_estimate=pl.CostEstimate(
+            flops=4 * rows * width * columns,
+            bytes_accessed=2 * width * (2 * rows + columns),
+            transcendentals=0,
+        ),
+        name="latent_product",
+    )(meta, mine, other, *parts)
+
+
+def latent_sums(meta, mine, other, parts, codes):
+    if parts[0].shape[1] % 16 == 0:
+        return latent_product(meta, mine, other, parts, codes)
+    joined = jnp.concatenate(parts, axis=0)
+    flat = jnp.array([code for group in codes for code in group], jnp.int32)
+    order = jnp.argsort((flat ^ meta[0]) // 2)
+    weight = joined[order].reshape(mine.shape[1], joined.shape[2])
+    theirs = jnp.dot(other, weight, preferred_element_type=jnp.float32)
+    return theirs.astype(jnp.bfloat16), jnp.dot(mine, weight, preferred_element_type=jnp.float32)
+
+
+def core_columns(tokens, size, core):
+    rows, width = tokens.shape
+    both = tokens.reshape(rows, width // size // 2, 2, size)
+    picked = lax.dynamic_index_in_dim(both, core, axis=2, keepdims=False)
+    return picked.reshape(rows, width // 2)
 
 
 def shards(
@@ -201,44 +368,66 @@
     meta = jnp.stack([rank.astype(jnp.int32), length])
     capacity = rows // experts + 2
     chunks = [(0, -(-capacity // 8) * 8)]
-    evens, odds = range(0, pieces, 2), range(1, pieces, 2)
-
-    packed = pack(meta, expert_ids, tokens, chunks, pieces)
-    weight_in = jnp.concatenate(four_shards(gate_up), axis=0)
-    weight_out = jnp.concatenate(four_shards(down_weight), axis=1)
-
-    returned = []
-    for number, (_, size) in enumerate(chunks):
-        sent = packed[number * pieces : (number + 1) * pieces]
-        arrived = [sent[0]] + [swapped(sent[t], QUAD * t) for t in range(1, pieces)]
-        theirs = jnp.dot(
-            jnp.concatenate([arrived[t] for t in odds], axis=0),
-            weight_in,
-            preferred_element_type=jnp.float32,
-        ).astype(jnp.bfloat16)
-        ours = jnp.dot(
-            jnp.concatenate([arrived[t] for t in evens], axis=0),
-            weight_in,
-            preferred_element_type=jnp.float32,
+
+    (packed,) = pack(meta, expert_ids, tokens, chunks, pieces)
+    columns = [[QUAD * s + low for s in range(pieces)] for low in range(QUAD)]
+
+    core = rank % 2
+    size = latent_weight.shape[0]
+    arrived, gate_1, gate_2, down_1, latent_1, mine, other = together(
+        lax.all_to_all(packed, "dp", 0, 0, axis_index_groups=columns, tiled=True),
+        swapped(gate_up, 1),
+        swapped(gate_up, 2),
+        swapped(down_weight, 1),
+        swapped(latent_weight[None], QUAD),
+        core_columns(tokens, size, core),
+        swapped(core_columns(tokens, size, 1 - core), 1),
+    )
+    gate_3 = swapped(gate_2, 1)
+    down_3 = swapped(down_1, 2)
+    held, codes = jnp.concatenate([latent_weight[None], latent_1], axis=0), [0, QUAD]
+    for level in range(3, rank_count.bit_length() - 2):
+        held = jnp.concatenate([held, swapped(held, 1 << level)], axis=0)
+        codes = codes + [code ^ (1 << level) for code in codes]
+    bit = rank_count // 2
+    half = held.shape[1] // 2
+    halved = lax.axis_size("groups") == 2 and half % 16 == 0
+    group = lax.axis_index("groups")
+    sent = lax.dynamic_slice_in_dim(held, group * half, half, 1) if halved else held
+    cut = swapped(sent, bit)
+
+    begun = gate_up_product(meta, arrived, [gate_up, gate_1, gate_2], 1, jnp.float32)
+    theirs = gate_up_product(
+        meta, arrived, [gate_3], 1, jnp.bfloat16, 3 * gate_up.shape[0], [begun]
+    )
+    ours = gate_up_product(meta, arrived, [gate_up, gate_1, gate_2, gate_3], 0, jnp.float32)
+    came, ours, down_3, cut = together(swapped(theirs, QUAD), ours, down_3, cut)
+    summed = ours + came.astype(jnp.float32)
+    hidden = (jax.nn.silu(summed[:, :hidden_units]) * summed[:, hidden_units:]).astype(jnp.bfloat16)
+
+    partner, down_2, other_half = together(
+        swapped(hidden, QUAD),
+        swapped(down_3, 1),
+        lax.ppermute(cut, "groups", [(0, 1), (1, 0)]) if halved else cut,
+    )
+    weight_out = [down_weight, down_1, down_2, down_3]
+    made = [down_product(block, weight_out, pieces // 2) for block in (hidden, partner)]
+    if halved:
+        first = group == 0
+        cut = jnp.where(
+            first,
+            jnp.concatenate([cut, other_half], axis=1),
+            jnp.concatenate([other_half, cut], axis=1),
         )
-        summed = ours + swapped(theirs, QUAD).astype(jnp.float32)
-        hidden = (
-            jax.nn.silu(summed[:, :hidden_units]) * summed[:, hidden_units:]
-        ).astype(jnp.bfloat16)
-        partner = swapped(hidden, QUAD)
-        made = [
-            jnp.dot(block, weight_out, preferred_element_type=jnp.float32).astype(jnp.bfloat16)
-            for block in (hidden, partner)
-        ]
-        back = []
-        for t in range(pieces):
-            piece = made[t % 2][t // 2 * size : (t // 2 + 1) * size]
-            back.append(swapped(piece, QUAD * t) if t else piece)
-        returned += back
+    held = after(jnp.concatenate([held, cut], axis=0), made[1][0])
+    codes = codes + [code ^ bit for code in codes]
+    latent_parts, latent_codes = [held, swapped(held, 2)], [codes, [code ^ 2 for code in codes]]
+
+    returned = [made[0][0]] + [swapped(made[t % 2][t // 2], QUAD * t) for t in range(1, pieces)]
     moe_out = unpack(meta, expert_ids, gate_weights, returned, chunks, pieces, width)
-
-    weight = gathered_latent(latent_weight, rank, rank_count)
-    latent_cache = latent_rows(tokens, weight, latent_gain, length)
+    given, kept = latent_sums(meta, mine, other, latent_parts, latent_codes)
+    projected = kept + swapped(given, 1).astype(jnp.float32)
+    latent_cache = latent_finish(projected, latent_gain, length)
     return (latent_cache, moe_out)
 
 

time: 395 us -> 299 us (0.76)
  waiting for transfers between devices: 272 us -> 177 us
  Pallas kernels: 13.1 us -> 60.3 us
  matrix products: 28.3 us -> 0 us
  other arithmetic: 27.8 us -> 10.1 us
    ppermute x18 -> x16, waiting for transfers between devices: 272 us -> 162 us  [swapped(): lax.ppermute(block, 'dp', [(low, low ^ bits) for low in range(count)])]
    pallas_call x1 -> x11, Pallas kernels: 5.39 us -> 49.9 us  [the longest x3 21.8 us: gate_up_product(): pl.pallas_call(functools.partial(gate_up_body, count, first), grid_spec=p...]
    dot_general x5 -> x0, matrix products: 28.3 us -> none  [the longest x1 8.74 us: shards(): jnp.dot(jnp.concatenate([arrived[t] for t in odds], axis=0), weight_in, p...]
    select_n x7 -> x1, other arithmetic: 25.1 us -> 1.99 us  [shards(): jnp.where(first, jnp.concatenate([cut, other_half], axis=1), jnp.concaten...]
    ppermute x0 -> x1, waiting for transfers between devices: none -> 13.9 us  [shards(): lax.ppermute(cut, 'groups', [(0, 1), (1, 0)])]
    ppermute x18 -> x16, starting transfers between devices: 20.8 us -> 12.8 us  [swapped(): lax.ppermute(block, 'dp', [(low, low ^ bits) for low in range(count)])]
    select_n x1 -> x0, local copies, waits for them, and re-layouts: 7.95 us -> none  [gathered_latent(): jnp.where(upper, jnp.stack([came, held], axis=step), jnp.stack([held, cam...]
    reshape x0 -> x2, local copies, waits for them, and re-layouts: none -> 6.38 us  [core_columns(): return picked.reshape(rows, width // 2)]
  transfers between devices with their start and end apart: 18 -> 18, of which waited for: 12 -> 8; matrix products, arithmetic and copies ran while one was open for 20% -> 7% of each run, Pallas kernels for 1% -> 16%
where the time goes in v2:
time: 299 us; the launch traced here: 298 us
  waiting for transfers between devices  177 us (59%)
  Pallas kernels  60.3 us (20%)
  local copies, waits for them, and re-layouts  30.4 us (10%)
  starting transfers between devices  19.6 us (7%)
  other arithmetic  10.1 us (3%)
    ppermute x16, waiting for transfers between devices, swapped(): lax.ppermute(block, 'dp', [(low, low ^ bits) for low in range(count)])  162 us
    pallas_call x3, Pallas kernels, gate_up_product(): pl.pallas_call(functools.partial(gate_up_body, count, first), grid_spec=p...  21.8 us
    unnamed x40, local copies, waits for them, and re-layouts  19.1 us
    pallas_call x2, Pallas kernels, down_product(): pl.pallas_call(down_body, grid=(QUAD,), in_specs=[pl.BlockSpec((rows, dep...  15 us
    ppermute x1, waiting for transfers between devices, shards(): lax.ppermute(cut, 'groups', [(0, 1), (1, 0)])  13.9 us
    ppermute x16, starting transfers between devices, swapped(): lax.ppermute(block, 'dp', [(low, low ^ bits) for low in range(count)])  12.8 us
    pallas_call x1, Pallas kernels, unpack(): pl.pallas_call(functools.partial(unpack_body, chunks, pieces), grid_spec=...  10.4 us
    pallas_call x1, Pallas kernels, pack(): pl.pallas_call(functools.partial(pack_body, chunks), grid_spec=pltpu.Pref...  6.66 us
  transfers between devices with their start and end apart: 18, of which 8 were waited for; matrix products, arithmetic and copies ran while one was open for 7% of the time, Pallas kernels for 16%

profile of v2, /device:TPU:8, one launch (start us, length us, event | category | flops | bytes accessed | tf_op | source)
XLA Modules:
  0.0 298.3 jit_solution(1683455330565572839)
XLA Ops:
  4.7 6.7 %pack_rows.1 = bf16[4,136,3584]{2,1,0:T(8,128)(2,1)} custom-call(s32[2]{0:T(128)} %pad_add_fusion.meta_ref, s32[256,1]{1,0:T(8,128)} %copy.38.column_ref, s32[1,256]{1,0:T(1,128)} %bitcast.13, bf16[256,7168]{1,0:T(8,128)(2,1)} %high_ref.1, bf16[256,7168]{1,0:T(8,128)(2,1)} %high_ref.1), custom_call_target="tpu_custom_call" | custom-call | flops 1879048192 | bytes 7340032 | tf_op jit(solution)/shard_map/pack_rows/pallas_call | solution.py:63
  11.4 5.3 %all-to-all-start = ((bf16[4,136,3584]{2,1,0:T(8,128)(2,1)}), bf16[4,136,3584]{2,1,0:T(8,128)(2,1)}, u32[]{:S(2)}, u32[]{:S(2)}) async-start(bf16[4,136,3584]{2,1,0:T(8,128)(2,1)} %pack_rows.1), calls=%async_computation | async-start | bytes 7798784 | tf_op jit(solution)/shard_map/all_to_all | solution.py:378
  18.2 5.9 %copy.39 = bf16[256,7168]{0,1:T(8,128)(2,1)} copy(bf16[256,7168]{1,0:T(8,128)(2,1)} %high_ref.1) | data formatting | bytes 7340032 | tf_op args[0]
  24.1 3.6 %constant_dynamic-slice_fusion = (bf16[256,8,1,448]{0,3,2,1:T(8,128)(2,1)S(1)}, bf16[256,8,1,448]{0,3,2,1:T(8,128)(2,1)}) fusion(bf16[256,8,2,448]{0,3,2,1:T(8,128)(2,1)} %bitcast.7, s32[]{:T(128)S(6)} %select_n.35, s32[]{:T(128)S(6)} %select_n.34), kind=kLoop, calls=%fused_computation.23 | loop fusion | bytes 7340040 | tf_op jit(solution)/shard_map/jit(dynamic_index_in_dim)/dynamic_slice | solution.py:354
  27.7 2.5 copy.41
  30.8 3.8 %copy.40.refs_5_ = bf16[256,3584]{1,0:T(8,128)(2,1)} copy(bf16[256,3584]{0,1:T(8,128)(2,1)} %bitcast.8) | data formatting | bytes 3670016 | tf_op jit(solution)/shard_map/reshape | solution.py:355
  34.6 57.7 %collective-permute-done.3.refs_4_ = bf16[1,448,576]{2,1,0:T(8,128)(2,1)S(1)} collective-permute-done((bf16[1,448,576]{2,1,0:T(8,128)(2,1)}, bf16[1,448,576]{2,1,0:T(8,128)(2,1)S(1)}, u32[]{:S(2)}, u32[]{:S(2)}) %collective-permute-start.3) | collective-permute-done | bytes 516128 | tf_op jit(solution)/shard_map/ppermute | solution.py:19
  92.3 6.4 %collective-permute-done.1.refs_2_ = bf16[896,2048]{1,0:T(8,128)(2,1)} collective-permute-done((bf16[896,2048]{1,0:T(8,128)(2,1)}, bf16[896,2048]{1,0:T(8,128)(2,1)}, u32[]{:S(2)}, u32[]{:S(2)}) %collective-permute-start.1) | collective-permute-done | bytes 3670048 | tf_op jit(solution)/shard_map/ppermute | solution.py:19
  102.0 2.0 copy-done.5
  104.0 7.7 %gate_up_product.3.refs_2_ = f32[272,2048]{1,0:T(8,128)S(1)} custom-call(s32[2]{0:T(128)S(1)} %copy-done.11, bf16[4,136,3584]{2,1,0:T(8,128)(2,1)} %get-tuple-element.25.refs_0_.refs_1_, bf16[4,136,3584]{2,1,0:T(8,128)(2,1)} %get-tuple-element.25.refs_0_.refs_1_, bf16[896,2048]{1,0:T(8,128)(2,1)S(1)} %copy-done.5, ...), custom_call_target="tpu_custom_call" | custom-call | flops 3992977408 | bytes 16629760 | tf_op jit(solution)/shard_map/gate_up_product/pallas_call | solution.py:213
  111.8 5.4 %gate_up_product.4 = bf16[272,2048]{1,0:T(8,128)(2,1)S(1)} custom-call(s32[2]{0:T(128)S(1)} %copy-done.11, bf16[4,136,3584]{2,1,0:T(8,128)(2,1)} %get-tuple-element.25.refs_0_.refs_1_, bf16[4,136,3584]{2,1,0:T(8,128)(2,1)} %get-tuple-element.25.refs_0_.refs_1_, f32[272,2048]{1,0:T(8,128)S(1)} %gate_up_product.3.refs_2_, ...), custom_call_target="tpu_custom_call" | custom-call | flops 3992977408 | bytes 16629760 | tf_op jit(solution)/shard_map/gate_up_product/pallas_call | solution.py:213
  117.2 3.5 %collective-permute-start.6 = (bf16[272,2048]{1,0:T(8,128)(2,1)S(1)}, bf16[272,2048]{1,0:T(8,128)(2,1)}, u32[]{:S(2)}, u32[]{:S(2)}) collective-permute-start(bf16[272,2048]{1,0:T(8,128)(2,1)S(1)} %gate_up_product.4), channel_id=1, source_target_pairs={{0,4},{1,5},{2,6},{3,7},{4,0},{5,1},{6,2},{7,3},{8,12},{9,13},{10,... | collective-permute-start | bytes 3342344 | tf_op jit(solution)/shard_map/ppermute | solution.py:19
  120.8 2.0 copy-done.4
  124.9 8.7 %gate_up_product.5.refs_1_ = f32[272,2048]{1,0:T(8,128)S(1)} custom-call(s32[2]{0:T(128)S(1)} %copy-done.11, bf16[4,136,3584]{2,1,0:T(8,128)(2,1)} %get-tuple-element.25.refs_0_.refs_1_, bf16[4,136,3584]{2,1,0:T(8,128)(2,1)} %get-tuple-element.25.refs_0_.refs_1_, bf16[896,2048]{1,0:T(8,128)(2,1)S(1)} %copy-done.6, ...), custom_call_target="tpu_custom_call" | custom-call | flops 3992977408 | bytes 16629760 | tf_op jit(solution)/shard_map/gate_up_product/pallas_call | solution.py:213
  135.0 23.0 %collective-permute-done.8.refs_3_ = bf16[2,224,576]{2,1,0:T(8,128)(2,1)} collective-permute-done((bf16[2,224,576]{2,1,0:T(8,128)(2,1)S(1)}, bf16[2,224,576]{2,1,0:T(8,128)(2,1)}, u32[]{:S(2)}, u32[]{:S(2)}) %collective-permute-start.8) | collective-permute-done | bytes 516128 | tf_op jit(solution)/shard_map/ppermute | solution.py:19
  158.0 2.2 convert_add_fusion
  164.5 13.9 %collective-permute-done.11.refs_2_ = bf16[2,224,576]{2,1,0:T(8,128)(2,1)} collective-permute-done((bf16[2,224,576]{2,1,0:T(8,128)(2,1)}, bf16[2,224,576]{2,1,0:T(8,128)(2,1)}, u32[]{:S(2)}, u32[]{:S(2)}) %collective-permute-start.11) | collective-permute-done | bytes 516128 | tf_op jit(solution)/shard_map/ppermute | solution.py:411
  183.5 7.3 %down_product.2 = (bf16[136,3584]{1,0:T(8,128)(2,1)}, bf16[136,3584]{1,0:T(8,128)(2,1)}) custom-call(bf16[272,1024]{1,0:T(8,128)(2,1)} %get-tuple-element.34.hidden_ref, bf16[1024,896]{1,0:T(8,128)(2,1)} %refs_0_.3, bf16[1024,896]{1,0:T(8,128)(2,1)} %get-tuple-element.28.refs_1_, bf16[1024,896]{1,0:T(8,128)(2,1)} %get-tuple-element.35.refs_2_, ...), custom_call_target="tpu_custom_call" | custom-call | flops 1996488704 | bytes 9846784 | tf_op jit(solution)/shard_map/down_product/pallas_call | solution.py:254
  191.6 7.7 %down_product.3 = (bf16[136,3584]{1,0:T(8,128)(2,1)}, bf16[136,3584]{1,0:T(8,128)(2,1)}) custom-call(bf16[272,1024]{1,0:T(8,128)(2,1)} %fusion.hidden_ref, bf16[1024,896]{1,0:T(8,128)(2,1)} %refs_0_.3, bf16[1024,896]{1,0:T(8,128)(2,1)} %get-tuple-element.28.refs_1_, bf16[1024,896]{1,0:T(8,128)(2,1)} %get-tuple-element.35.refs_2_, ...), custom_call_target="tpu_custom_call" | custom-call | flops 1996488704 | bytes 9846784 | tf_op jit(solution)/shard_map/down_product/pallas_call | solution.py:254
  202.1 40.2 %collective-permute-done.12.refs_1_ = bf16[4,448,576]{2,1,0:T(8,128)(2,1)} collective-permute-done((bf16[4,448,576]{2,1,0:T(8,128)(2,1)}, bf16[4,448,576]{2,1,0:T(8,128)(2,1)}, u32[]{:S(2)}, u32[]{:S(2)}) %collective-permute-start.12) | collective-permute-done | bytes 2064416 | tf_op jit(solution)/shard_map/ppermute | solution.py:19
  242.3 6.5 %latent_product.1 = (bf16[256,576]{1,0:T(8,128)(2,1)}, f32[256,576]{1,0:T(8,128)S(1)}) custom-call(s32[2]{0:T(128)S(1)} %copy-done.11, bf16[256,3584]{1,0:T(8,128)(2,1)S(1)} %copy-done.2, bf16[256,3584]{1,0:T(8,128)(2,1)S(1)} %copy-done.8, bf16[4,448,576]{2,1,0:T(8,128)(2,1)S(1)} %copy-done, bf16[4,448,576]{2,1,0:T(8,128)(2,1)} %collective-permute-done.12.refs_1_), custom_call_target="tpu_custom_call" | custom-call | flops 2113929216 | bytes 7798784 | tf_op jit(solution)/shard_map/latent_product/pallas_call | solution.py:317
  251.1 14.1 %collective-permute-done.15.refs_2_ = bf16[136,3584]{1,0:T(8,128)(2,1)} collective-permute-done((bf16[136,3584]{1,0:T(8,128)(2,1)}, bf16[136,3584]{1,0:T(8,128)(2,1)}, u32[]{:S(2)}, u32[]{:S(2)}) %collective-permute-start.15) | collective-permute-done | bytes 974880 | tf_op jit(solution)/shard_map/ppermute | solution.py:19
  265.2 20.3 %collective-permute-done.16.refs_3_ = bf16[136,3584]{1,0:T(8,128)(2,1)} collective-permute-done((bf16[136,3584]{1,0:T(8,128)(2,1)}, bf16[136,3584]{1,0:T(8,128)(2,1)}, u32[]{:S(2)}, u32[]{:S(2)}) %collective-permute-start.16) | collective-permute-done | bytes 974880 | tf_op jit(solution)/shard_map/ppermute | solution.py:19
  285.5 10.4 %unpack_rows.1 = bf16[256,7168]{1,0:T(8,128)(2,1)} custom-call(s32[2]{0:T(128)} %pad_add_fusion.meta_ref, s32[256,1]{1,0:T(8,128)} %copy.38.column_ref, s32[1,256]{1,0:T(1,128)} %bitcast.14, f32[256,1]{1,0:T(8,128)} %copy.44.gate_ref, bf16[136,3584]{1,0:T(8,128)(2,1)} %get-tuple-element.39.refs_0_, bf16[136,3584]{1,0:T(8,128)(2,1)} %collective-permute-done.14.refs_1_, ...), custom_call_target="tpu_custom_call" | custom-call | flops 1879048192 | bytes 7340032 | tf_op jit(solution)/shard_map/unpack_rows/pallas_call | solution.py:125
  (83 shorter events, 30.7 us)
Async XLA Ops:
  11.4 88.9 %all-to-all-start = ((bf16[4,136,3584]{2,1,0:T(8,128)(2,1)}), bf16[4,136,3584]{2,1,0:T(8,128)(2,1)}, u32[]{:S(2)}, u32[]{:S(2)}) async-start(bf16[4,136,3584]{2,1,0:T(8,128)(2,1)} %pack_rows.1), calls=%async_computation | async-start | bytes 7798784 | tf_op jit(solution)/shard_map/all_to_all | solution.py:378
  16.7 75.6 %collective-permute-start = (bf16[896,2048]{1,0:T(8,128)(2,1)}, bf16[896,2048]{1,0:T(8,128)(2,1)}, u32[]{:S(2)}, u32[]{:S(2)}) collective-permute-start(bf16[896,2048]{1,0:T(8,128)(2,1)} %refs_2_.3), channel_id=1, source_target_pairs={{0,1},{1,0},{2,3},{3,2},{4,5},{5,4},{6,7},{7,6},{8,9},{9,8},{10,11... | collective-permute-start | bytes 11010056 | tf_op jit(solution)/shard_map/ppermute | solution.py:19
  16.7 82.1 %collective-permute-start.1 = (bf16[896,2048]{1,0:T(8,128)(2,1)}, bf16[896,2048]{1,0:T(8,128)(2,1)}, u32[]{:S(2)}, u32[]{:S(2)}) collective-permute-start(bf16[896,2048]{1,0:T(8,128)(2,1)} %refs_2_.3), channel_id=1, source_target_pairs={{0,2},{1,3},{2,0},{3,1},{4,6},{5,7},{6,4},{7,5},{8,10},{9,11},{10,... | collective-permute-start | bytes 11010056 | tf_op jit(solution)/shard_map/ppermute | solution.py:19
  30.2 62.1 %collective-permute-start.4 = (bf16[256,3584]{1,0:T(8,128)(2,1)}, bf16[256,3584]{1,0:T(8,128)(2,1)S(1)}, u32[]{:S(2)}, u32[]{:S(2)}) collective-permute-start(bf16[256,3584]{1,0:T(8,128)(2,1)} %copy.41), channel_id=1, source_target_pairs={{0,1},{1,0},{2,3},{3,2},{4,5},{5,4},{6,7},{7,6},{8,9},{9,8},{10,11... | collective-permute-start | bytes 5505032 | tf_op jit(solution)/shard_map/ppermute | solution.py:19
  30.4 61.9 %collective-permute-start.2 = (bf16[1024,896]{1,0:T(8,128)(2,1)}, bf16[1024,896]{1,0:T(8,128)(2,1)}, u32[]{:S(2)}, u32[]{:S(2)}) collective-permute-start(bf16[1024,896]{1,0:T(8,128)(2,1)} %refs_0_.3), channel_id=1, source_target_pairs={{0,1},{1,0},{2,3},{3,2},{4,5},{5,4},{6,7},{7,6},{8,9},{9,8},{10,11... | collective-permute-start | bytes 5505032 | tf_op jit(solution)/shard_map/ppermute | solution.py:19
  30.7 61.6 %collective-permute-start.3 = (bf16[1,448,576]{2,1,0:T(8,128)(2,1)}, bf16[1,448,576]{2,1,0:T(8,128)(2,1)S(1)}, u32[]{:S(2)}, u32[]{:S(2)}) collective-permute-start(bf16[1,448,576]{2,1,0:T(8,128)(2,1)} %bitcast.10), channel_id=1, source_target_pairs={{0,4},{1,5},{2,6},{3,7},{4,0},{5,1},{6,2},{7,3},{8,12},{9,13},{10,... | collective-permute-start | bytes 1548296 | tf_op jit(solution)/shard_map/ppermute | solution.py:19
  34.6 67.3 %copy-start.11 = (s32[2]{0:T(128)S(1)}, s32[2]{0:T(128)}, u32[]{:S(2)}) copy-start(s32[2]{0:T(128)} %pad_add_fusion.meta_ref) | copy-start | bytes 28
  100.2 11.6 %collective-permute-start.5 = (bf16[896,2048]{1,0:T(8,128)(2,1)}, bf16[896,2048]{1,0:T(8,128)(2,1)S(1)}, u32[]{:S(2)}, u32[]{:S(2)}) collective-permute-start(bf16[896,2048]{1,0:T(8,128)(2,1)} %get-tuple-element.27.refs_4_), channel_id=1, source_target_pairs={{0,1},{1,0},{2,3},{3,2},{4,5},{5,4},{6,7},{7,6},{8,9},{9,8},{10,11... | collective-permute-start | bytes 11010056 | tf_op jit(solution)/shard_map/ppermute | solution.py:19
  100.2 57.7 %collective-permute-start.7 = (bf16[1024,896]{1,0:T(8,128)(2,1)}, bf16[1024,896]{1,0:T(8,128)(2,1)}, u32[]{:S(2)}, u32[]{:S(2)}) collective-permute-start(bf16[1024,896]{1,0:T(8,128)(2,1)} %get-tuple-element.28.refs_1_), channel_id=1, source_target_pairs={{0,2},{1,3},{2,0},{3,1},{4,6},{5,7},{6,4},{7,5},{8,10},{9,11},{10,... | collective-permute-start | bytes 5505032 | tf_op jit(solution)/shard_map/ppermute | solution.py:19
  111.8 8.9 %copy-start.14 = (bf16[1,448,576]{2,1,0:T(8,128)(2,1)S(1)}, bf16[1,448,576]{2,1,0:T(8,128)(2,1)}, u32[]{:S(2)}) copy-start(bf16[1,448,576]{2,1,0:T(8,128)(2,1)} %get-tuple-element.24) | copy-start | bytes 1548292
  117.2 40.7 %collective-permute-start.6 = (bf16[272,2048]{1,0:T(8,128)(2,1)S(1)}, bf16[272,2048]{1,0:T(8,128)(2,1)}, u32[]{:S(2)}, u32[]{:S(2)}) collective-permute-start(bf16[272,2048]{1,0:T(8,128)(2,1)S(1)} %gate_up_product.4), channel_id=1, source_target_pairs={{0,4},{1,5},{2,6},{3,7},{4,0},{5,1},{6,2},{7,3},{8,12},{9,13},{10,... | collective-permute-start | bytes 3342344 | tf_op jit(solution)/shard_map/ppermute | solution.py:19
  120.7 37.2 %collective-permute-start.8 = (bf16[2,224,576]{2,1,0:T(8,128)(2,1)S(1)}, bf16[2,224,576]{2,1,0:T(8,128)(2,1)}, u32[]{:S(2)}, u32[]{:S(2)}) collective-permute-start(bf16[2,224,576]{2,1,0:T(8,128)(2,1)S(1)} %fusion.2), channel_id=1, source_target_pairs={{0,8},{1,9},{2,10},{3,11},{4,12},{5,13},{6,14},{7,15},{8,0},{9,1},... | collective-permute-start | bytes 1548296 | tf_op jit(solution)/shard_map/ppermute | solution.py:19
  158.0 20.5 %collective-permute-start.10 = (bf16[1024,896]{1,0:T(8,128)(2,1)}, bf16[1024,896]{1,0:T(8,128)(2,1)S(1)}, u32[]{:S(2)}, u32[]{:S(2)}) collective-permute-start(bf16[1024,896]{1,0:T(8,128)(2,1)} %get-tuple-element.32.refs_3_), channel_id=1, source_target_pairs={{0,1},{1,0},{2,3},{3,2},{4,5},{5,4},{6,7},{7,6},{8,9},{9,8},{10,11... | collective-permute-start | bytes 5505032 | tf_op jit(solution)/shard_map/ppermute | solution.py:19
  161.4 17.1 %collective-permute-start.9 = (bf16[272,1024]{1,0:T(8,128)(2,1)}, bf16[272,1024]{1,0:T(8,128)(2,1)}, u32[]{:S(2)}, u32[]{:S(2)}) collective-permute-start(bf16[272,1024]{1,0:T(8,128)(2,1)} %fusion.hidden_ref), channel_id=1, source_target_pairs={{0,4},{1,5},{2,6},{3,7},{4,0},{5,1},{6,2},{7,3},{8,12},{9,13},{10,... | collective-permute-start | bytes 1671176 | tf_op jit(solution)/shard_map/ppermute | solution.py:19
  163.0 15.4 %collective-permute-start.11 = (bf16[2,224,576]{2,1,0:T(8,128)(2,1)}, bf16[2,224,576]{2,1,0:T(8,128)(2,1)}, u32[]{:S(2)}, u32[]{:S(2)}) collective-permute-start(bf16[2,224,576]{2,1,0:T(8,128)(2,1)} %get-tuple-element.29), channel_id=1, source_target_pairs={{0,16},{16,0},{1,17},{17,1},{2,18},{18,2},{3,19},{19,3},{4,20},{20... | collective-permute-start | bytes 1548296 | tf_op jit(solution)/shard_map/ppermute | solution.py:411
  190.7 51.6 %copy-start = (bf16[4,448,576]{2,1,0:T(8,128)(2,1)S(1)}, bf16[4,448,576]{2,1,0:T(8,128)(2,1)}, u32[]{:S(2)}) copy-start(bf16[4,448,576]{2,1,0:T(8,128)(2,1)} %after.1.refs_0_) | copy-start | bytes 6193156
  190.7 51.6 %copy-start.2 = (bf16[256,3584]{1,0:T(8,128)(2,1)S(1)}, bf16[256,3584]{1,0:T(8,128)(2,1)}, u32[]{:S(2)}) copy-start(bf16[256,3584]{1,0:T(8,128)(2,1)} %get-tuple-element.22.mine_ref) | copy-start | bytes 5505028
  190.7 51.6 %copy-start.8 = (bf16[256,3584]{1,0:T(8,128)(2,1)S(1)}, bf16[256,3584]{1,0:T(8,128)(2,1)}, u32[]{:S(2)}) copy-start(bf16[256,3584]{1,0:T(8,128)(2,1)} %get-tuple-element.23.other_ref) | copy-start | bytes 5505028
  190.7 51.5 %collective-permute-start.12 = (bf16[4,448,576]{2,1,0:T(8,128)(2,1)}, bf16[4,448,576]{2,1,0:T(8,128)(2,1)}, u32[]{:S(2)}, u32[]{:S(2)}) collective-permute-start(bf16[4,448,576]{2,1,0:T(8,128)(2,1)} %after.1.refs_0_), channel_id=1, source_target_pairs={{0,2},{1,3},{2,0},{3,1},{4,6},{5,7},{6,4},{7,5},{8,10},{9,11},{10,... | collective-permute-start | bytes 6193160 | tf_op jit(solution)/shard_map/ppermute | solution.py:19
  191.3 73.9 %collective-permute-start.14 = (bf16[136,3584]{1,0:T(8,128)(2,1)}, bf16[136,3584]{1,0:T(8,128)(2,1)}, u32[]{:S(2)}, u32[]{:S(2)}) collective-permute-start(bf16[136,3584]{1,0:T(8,128)(2,1)} %get-tuple-element.36.refs_1_), channel_id=1, source_target_pairs={{0,4},{1,5},{2,6},{3,7},{4,0},{5,1},{6,2},{7,3},{8,12},{9,13},{10,... | collective-permute-start | bytes 2924552 | tf_op jit(solution)/shard_map/ppermute | solution.py:19
  199.3 65.9 %collective-permute-start.15 = (bf16[136,3584]{1,0:T(8,128)(2,1)}, bf16[136,3584]{1,0:T(8,128)(2,1)}, u32[]{:S(2)}, u32[]{:S(2)}) collective-permute-start(bf16[136,3584]{1,0:T(8,128)(2,1)} %get-tuple-element.40), channel_id=1, source_target_pairs={{0,8},{1,9},{2,10},{3,11},{4,12},{5,13},{6,14},{7,15},{8,0},{9,1},... | collective-permute-start | bytes 2924552 | tf_op jit(solution)/shard_map/ppermute | solution.py:19
  201.1 84.5 %collective-permute-start.16 = (bf16[136,3584]{1,0:T(8,128)(2,1)}, bf16[136,3584]{1,0:T(8,128)(2,1)}, u32[]{:S(2)}, u32[]{:S(2)}) collective-permute-start(bf16[136,3584]{1,0:T(8,128)(2,1)} %get-tuple-element.41), channel_id=1, source_target_pairs={{0,12},{1,13},{2,14},{3,15},{4,8},{5,9},{6,10},{7,11},{8,4},{9,5},... | collective-permute-start | bytes 2924552 | tf_op jit(solution)/shard_map/ppermute | solution.py:19
  249.6 46.3 %collective-permute-start.13 = (bf16[256,576]{1,0:T(8,128)(2,1)}, bf16[256,576]{1,0:T(8,128)(2,1)S(1)}, u32[]{:S(2)}, u32[]{:S(2)}) collective-permute-start(bf16[256,576]{1,0:T(8,128)(2,1)} %get-tuple-element.38), channel_id=1, source_target_pairs={{0,1},{1,0},{2,3},{3,2},{4,5},{5,4},{6,7},{7,6},{8,9},{9,8},{10,11... | collective-permute-start | bytes 884744 | tf_op jit(solution)/shard_map/ppermute | solution.py:19
  285.5 10.4 %copy-start.10 = (f32[256,576]{1,0:T(8,128)S(1)}, f32[256,576]{1,0:T(8,128)}, u32[]{:S(2)}) copy-start(f32[256,576]{1,0:T(8,128)} %copy-done.9) | copy-start | bytes 1769476
  (12 other events, 48.4 us)

commit v3 on v2

--- a/solution.py
+++ b/solution.py
@@ -87,43 +87,43 @@
     )(meta, ids, ids.reshape(1, rows), tokens, tokens)
 
 
-def unpack_body(chunks, pieces, meta_ref, column_ref, row_ref, gate_ref, *refs):
-    parts, out_ref = refs[:-1], refs[-1]
+def unpack_body(size, meta_ref, column_ref, row_ref, gate_ref, near_ref, *refs):
+    far_refs, out_ref = refs[:-1], refs[-1]
     expert_column, place_column = chosen_slots(meta_ref, column_ref[...], row_ref[...])
     my_expert = meta_ref[0] // GROUP
     gate = gate_ref[...]
 
-    def blend(side):
+    def blend(parts):
         total = jnp.zeros(out_ref.shape, jnp.float32)
-        for number, (start, size) in enumerate(chunks):
-            for far in range(pieces // 2):
-                picks = selector(expert_column, place_column, my_expert ^ far, start, size)
-                part = parts[number * pieces + 2 * far + side]
-                total = total + jnp.dot(picks, part[...], preferred_element_type=jnp.float32)
+        for expert, part in parts:
+            picks = selector(expert_column, place_column, expert, 0, size)
+            total = total + jnp.dot(picks, part, preferred_element_type=jnp.float32)
         out_ref[...] = (total * gate).astype(jnp.bfloat16)
 
-    for side in range(2):
-        pl.when(pl.program_id(0) == side)(functools.partial(blend, side))
-
-
-def unpack(meta, ids, gates, returned, chunks, pieces, width):
+    @pl.when(pl.program_id(0) == 0)
+    def _():
+        blend([(expert, near_ref[expert]) for expert in range(near_ref.shape[0])])
+
+    @pl.when(pl.program_id(0) == 1)
+    def _():
+        blend([(my_expert ^ number, ref[...]) for number, ref in enumerate(far_refs)])
+
+
+def unpack(meta, ids, gates, near, far, width):
     rows = ids.shape[0]
     part = width // GROUP
+    experts, size, _ = near.shape
 
     def out_index(side, k, meta_ref):
         quarter = meta_ref[0] % QUAD
         high = (meta_ref[0] // QUAD) % 2
         return (0, (high ^ side) * QUAD + (quarter ^ k))
 
-    near = lambda side, k, meta_ref: (0, jnp.where(side == 0, k, QUAD - 1))
-    far = lambda side, k, meta_ref: (0, jnp.where(side == 1, k, 0))
+    near_index = lambda side, k, meta_ref: (0, 0, jnp.where(side == 0, k, QUAD - 1))
+    far_index = lambda side, k, meta_ref: (0, jnp.where(side == 1, k, 0))
     whole = lambda side, k, meta_ref: (0, 0)
-    specs = []
-    for _, size in chunks:
-        for piece in range(pieces):
-            specs.append(pl.BlockSpec((size, part), far if piece % 2 else near))
-    return pl.pallas_call(
-        functools.partial(unpack_body, chunks, pieces),
+    return pl.pallas_call(
+        functools.partial(unpack_body, size),
         grid_spec=pltpu.PrefetchScalarGridSpec(
             num_scalar_prefetch=1,
             grid=(2, QUAD),
@@ -131,8 +131,9 @@
                 pl.BlockSpec((rows, 1), whole),
                 pl.BlockSpec((1, rows), whole),
                 pl.BlockSpec((rows, 1), whole),
+                pl.BlockSpec((experts, size, part), near_index),
             ]
-            + specs,
+            + [pl.BlockSpec((size, part), far_index) for _ in far],
             out_specs=pl.BlockSpec((rows, part), out_index),
         ),
         out_shape=jax.ShapeDtypeStruct((rows, width), jnp.bfloat16),
@@ -141,7 +142,7 @@
             flops=4 * rows * rows * width, bytes_accessed=4 * rows * width, transcendentals=0
         ),
         name="unpack_rows",
-    )(meta, ids, ids.reshape(1, rows), gates, *returned)
+    )(meta, ids, ids.reshape(1, rows), gates, near, *far)
 
 
 def idle_body(*refs):
@@ -172,34 +173,32 @@
     )(*values)
 
 
-def gate_up_body(count, first, meta_ref, *refs):
+def gate_up_body(count, meta_ref, *refs):
     del meta_ref
-    parts, rest, out_ref, joined = refs[:count], refs[count:-2], refs[-2], refs[-1]
+    parts, shares, out_ref, joined = refs[:count], refs[count:-2], refs[-2], refs[-1]
     size = parts[0].shape[1]
+    depth = shares[0].shape[0]
 
     @pl.when(pl.program_id(0) == 0)
     def _():
         for number, part in enumerate(parts):
             joined[pl.ds(number * size, size), :] = part[0]
 
-    shares, start = rest, first
-    total = jnp.zeros(out_ref.shape, jnp.float32)
-    if first:
-        shares, total = rest[1:], rest[0][...]
-    for share in shares:
-        depth = share.shape[0]
+    total = jnp.dot(joined[:, :depth], shares[0][...], preferred_element_type=jnp.float32)
+    for k in range(1, QUAD):
         total += jnp.dot(
-            joined[:, start : start + depth], share[...], preferred_element_type=jnp.float32
+            joined[:, k * depth : (k + 1) * depth],
+            shares[k][...],
+            preferred_element_type=jnp.float32,
         )
-        start += depth
     out_ref[...] = total.astype(out_ref.dtype)
 
 
-def gate_up_product(meta, arrived, shares, side, dtype, first=0, base=()):
+def gate_up_product(meta, arrived, shares, side, dtype):
     pieces, size, width = arrived.shape
     count = pieces // 2
     rows = size * count
-    columns = shares[0].shape[1]
+    depth, columns = shares[0].shape
     tile = columns // 4
 
     def source(number):
@@ -211,13 +210,12 @@
 
     across = lambda n, meta_ref: (0, n)
     return pl.pallas_call(
-        functools.partial(gate_up_body, count, first),
+        functools.partial(gate_up_body, count),
         grid_spec=pltpu.PrefetchScalarGridSpec(
             num_scalar_prefetch=1,
             grid=(columns // tile,),
             in_specs=[pl.BlockSpec((1, size, width), source(number)) for number in range(count)]
-            + [pl.BlockSpec((rows, tile), across) for _ in base]
-            + [pl.BlockSpec((share.shape[0], tile), across) for share in shares],
+            + [pl.BlockSpec((depth, tile), across) for _ in shares],
             out_specs=pl.BlockSpec((rows, tile), across),
             scratch_shapes=[pltpu.VMEM((rows, width), jnp.bfloat16)],
         ),
@@ -229,13 +227,15 @@
             transcendentals=0,
         ),
         name="gate_up_product",
-    )(meta, *[arrived] * count, *base, *shares)
-
-
-def down_body(hidden_ref, *refs):
+    )(meta, *[arrived] * count, *shares)
+
+
+def down_body(joined, meta_ref, hidden_ref, *refs):
     k = pl.program_id(0)
     shares, outs = refs[:QUAD], refs[QUAD:]
-    size = outs[0].shape[0]
+    count = outs[0].shape[0] if joined else len(outs)
+    size = hidden_ref.shape[0] // count
+    mine = meta_ref[0] // GROUP
     for turn in range(QUAD):
 
         @pl.when(k == turn)
@@ -243,21 +243,35 @@
             made = jnp.dot(
                 hidden_ref[...], shares[turn][...], preferred_element_type=jnp.float32
             )
-            for number, out_ref in enumerate(outs):
-                out_ref[...] = made[number * size : (number + 1) * size].astype(jnp.bfloat16)
-
-
-def down_product(hidden, shares, count):
+            for number in range(count):
+                rows = made[number * size : (number + 1) * size].astype(jnp.bfloat16)
+                if joined:
+                    outs[0][mine ^ number] = rows
+                else:
+                    outs[number][...] = rows
+
+
+def down_product(meta, hidden, shares, count, joined):
     rows, depth = hidden.shape
     part = shares[0].shape[1]
     size = rows // count
-    return pl.pallas_call(
-        down_body,
-        grid=(QUAD,),
-        in_specs=[pl.BlockSpec((rows, depth), lambda k: (0, 0))]
-        + [pl.BlockSpec((depth, part), lambda k: (0, 0)) for _ in shares],
-        out_specs=[pl.BlockSpec((size, part), lambda k: (0, k)) for _ in range(count)],
-        out_shape=[jax.ShapeDtypeStruct((size, QUAD * part), jnp.bfloat16) for _ in range(count)],
+    whole = lambda k, meta_ref: (0, 0)
+    if joined:
+        out_specs = [pl.BlockSpec((count, size, part), lambda k, meta_ref: (0, 0, k))]
+        shapes = [(count, size, QUAD * part)]
+    else:
+        out_specs = [pl.BlockSpec((size, part), lambda k, meta_ref: (0, k))] * count
+        shapes = [(size, QUAD * part)] * count
+    return pl.pallas_call(
+        functools.partial(down_body, joined),
+        grid_spec=pltpu.PrefetchScalarGridSpec(
+            num_scalar_prefetch=1,
+            grid=(QUAD,),
+            in_specs=[pl.BlockSpec((rows, depth), whole)]
+            + [pl.BlockSpec((depth, part), whole) for _ in shares],
+            out_specs=out_specs,
+        ),
+        out_shape=[jax.ShapeDtypeStruct(shape, jnp.bfloat16) for shape in shapes],
         compiler_params=pltpu.CompilerParams(vmem_limit_bytes=58 << 20),
         cost_estimate=pl.CostEstimate(
             flops=2 * rows * depth * QUAD * part,
@@ -265,7 +279,7 @@
             transcendentals=0,
         ),
         name="down_product",
-    )(hidden, *shares)
+    )(meta, hidden, *shares)
 
 
 def latent_finish(projected, gain, length):
@@ -305,12 +319,19 @@
     for move in moves:
         move.wait()
     for tokens_ref, sum_ref in zip((other_ref, mine_ref), sums):
-        product = jnp.dot(tokens_ref[...], weight[...], preferred_element_type=jnp.float32)
+        product = jnp.dot(tokens_ref[0], weight[:size, :], preferred_element_type=jnp.float32)
+        for number in range(1, tokens_ref.shape[0]):
+            product += jnp.dot(
+                tokens_ref[number],
+                weight[number * size : (number + 1) * size, :],
+                preferred_element_type=jnp.float32,
+            )
         sum_ref[...] = product.astype(sum_ref.dtype)
 
 
 def latent_product(meta, mine, other, parts, codes):
-    rows, width = mine.shape
+    count, rows, size = mine.shape
+    width = count * size
     columns = parts[0].shape[2]
     total = sum(len(group) for group in codes)
     inside = pl.BlockSpec(memory_space=pltpu.VMEM)
@@ -343,16 +364,51 @@
     joined = jnp.concatenate(parts, axis=0)
     flat = jnp.array([code for group in codes for code in group], jnp.int32)
     order = jnp.argsort((flat ^ meta[0]) // 2)
-    weight = joined[order].reshape(mine.shape[1], joined.shape[2])
-    theirs = jnp.dot(other, weight, preferred_element_type=jnp.float32)
-    return theirs.astype(jnp.bfloat16), jnp.dot(mine, weight, preferred_element_type=jnp.float32)
-
-
-def core_columns(tokens, size, core):
+    weight = joined[order]
+    theirs, kept = [
+        jnp.einsum("crs,csf->rf", half, weight, preferred_element_type=jnp.float32)
+        for half in (other, mine)
+    ]
+    return theirs.astype(jnp.bfloat16), kept
+
+
+def core_split_body(meta_ref, tokens_ref, mine_ref, other_ref):
+    half = mine_ref.shape[2]
+    low, high = tokens_ref[:, :half], tokens_ref[:, half:]
+
+    @pl.when(meta_ref[0] % 2 == 0)
+    def _():
+        mine_ref[0], other_ref[0] = low, high
+
+    @pl.when(meta_ref[0] % 2 == 1)
+    def _():
+        mine_ref[0], other_ref[0] = high, low
+
+
+def core_split(meta, tokens, size):
     rows, width = tokens.shape
-    both = tokens.reshape(rows, width // size // 2, 2, size)
-    picked = lax.dynamic_index_in_dim(both, core, axis=2, keepdims=False)
-    return picked.reshape(rows, width // 2)
+    count = width // size // 2
+    out = pl.BlockSpec((1, rows, size), lambda n, meta_ref: (n, 0, 0))
+    return pl.pallas_call(
+        core_split_body,
+        grid_spec=pltpu.PrefetchScalarGridSpec(
+            num_scalar_prefetch=1,
+            grid=(count,),
+            in_specs=[pl.BlockSpec((rows, 2 * size), lambda n, meta_ref: (0, n))],
+            out_specs=[out, out],
+        ),
+        out_shape=[jax.ShapeDtypeStruct((count, rows, size), jnp.bfloat16)] * 2,
+        name="core_split",
+    )(meta, tokens)
+
+
+def token_halves(meta, tokens, size):
+    if size % 64 == 0:
+        return core_split(meta, tokens, size)
+    rows, width = tokens.shape
+    both = tokens.reshape(rows, width // size // 2, 2, size).transpose(2, 1, 0, 3)
+    core = meta[0] % 2
+    return both[core], both[1 - core]
 
 
 def shards(
@@ -371,60 +427,65 @@
 
     (packed,) = pack(meta, expert_ids, tokens, chunks, pieces)
     columns = [[QUAD * s + low for s in range(pieces)] for low in range(QUAD)]
-
-    core = rank % 2
-    size = latent_weight.shape[0]
-    arrived, gate_1, gate_2, down_1, latent_1, mine, other = together(
+    mine, other = token_halves(meta, tokens, latent_weight.shape[0])
+
+    gate_2 = swapped(gate_up, 2)
+    latent_1 = swapped(latent_weight[None], QUAD)
+    packed = after(packed, latent_1)
+    down_1 = swapped(down_weight, 1)
+    arrived, gate_1, gate_3, mine, other = together(
         lax.all_to_all(packed, "dp", 0, 0, axis_index_groups=columns, tiled=True),
         swapped(gate_up, 1),
-        swapped(gate_up, 2),
-        swapped(down_weight, 1),
-        swapped(latent_weight[None], QUAD),
-        core_columns(tokens, size, core),
-        swapped(core_columns(tokens, size, 1 - core), 1),
+        swapped(gate_2, 1),
+        mine,
+        swapped(other, 1),
     )
-    gate_3 = swapped(gate_2, 1)
+    down_1 = after(down_1, gate_2)
     down_3 = swapped(down_1, 2)
     held, codes = jnp.concatenate([latent_weight[None], latent_1], axis=0), [0, QUAD]
-    for level in range(3, rank_count.bit_length() - 2):
-        held = jnp.concatenate([held, swapped(held, 1 << level)], axis=0)
-        codes = codes + [code ^ (1 << level) for code in codes]
-    bit = rank_count // 2
-    half = held.shape[1] // 2
-    halved = lax.axis_size("groups") == 2 and half % 16 == 0
-    group = lax.axis_index("groups")
-    sent = lax.dynamic_slice_in_dim(held, group * half, half, 1) if halved else held
-    cut = swapped(sent, bit)
-
-    begun = gate_up_product(meta, arrived, [gate_up, gate_1, gate_2], 1, jnp.float32)
-    theirs = gate_up_product(
-        meta, arrived, [gate_3], 1, jnp.bfloat16, 3 * gate_up.shape[0], [begun]
-    )
-    ours = gate_up_product(meta, arrived, [gate_up, gate_1, gate_2, gate_3], 0, jnp.float32)
-    came, ours, down_3, cut = together(swapped(theirs, QUAD), ours, down_3, cut)
+    middle = pieces == 4
+    if not middle:
+        for level in range(3, rank_count.bit_length() - 1):
+            held = jnp.concatenate([held, swapped(held, 1 << level)], axis=0)
+            codes = codes + [code ^ (1 << level) for code in codes]
+    cut = held
+    if middle:
+        cut = lax.ppermute(held, "dp", [(low, low ^ 12) for low in range(QUAD, 3 * QUAD)])
+
+    weight_in = [gate_up, gate_1, gate_2, gate_3]
+    theirs = gate_up_product(meta, arrived, weight_in, 1, jnp.bfloat16)
+    ours = gate_up_product(meta, arrived, weight_in, 0, jnp.float32)
+    down_3 = after(down_3, ours)
+    split = down_3.shape[0] // 2
+    down_2 = [swapped(piece, 1) for piece in (down_3[:split], down_3[split:])]
+    came, ours, cut, *down_2 = together(swapped(theirs, QUAD), ours, cut, *down_2)
+    down_2 = jnp.concatenate(down_2, axis=0)
     summed = ours + came.astype(jnp.float32)
     hidden = (jax.nn.silu(summed[:, :hidden_units]) * summed[:, hidden_units:]).astype(jnp.bfloat16)
 
-    partner, down_2, other_half = together(
-        swapped(hidden, QUAD),
-        swapped(down_3, 1),
-        lax.ppermute(cut, "groups", [(0, 1), (1, 0)]) if halved else cut,
-    )
+    held = after(held, hidden)
+    latent_parts, latent_codes = [held, swapped(held, 2)], [codes, [code ^ 2 for code in codes]]
+    partner = swapped(hidden, QUAD)
+    forward = cut
+    if middle:
+        forward = lax.ppermute(
+            cut, "dp", [(low, low ^ QUAD) for low in range(QUAD, 3 * QUAD)]
+        )
+
     weight_out = [down_weight, down_1, down_2, down_3]
-    made = [down_product(block, weight_out, pieces // 2) for block in (hidden, partner)]
-    if halved:
-        first = group == 0
-        cut = jnp.where(
-            first,
-            jnp.concatenate([cut, other_half], axis=1),
-            jnp.concatenate([other_half, cut], axis=1),
-        )
-    held = after(jnp.concatenate([held, cut], axis=0), made[1][0])
-    codes = codes + [code ^ bit for code in codes]
-    latent_parts, latent_codes = [held, swapped(held, 2)], [codes, [code ^ 2 for code in codes]]
-
-    returned = [made[0][0]] + [swapped(made[t % 2][t // 2], QUAD * t) for t in range(1, pieces)]
-    moe_out = unpack(meta, expert_ids, gate_weights, returned, chunks, pieces, width)
+    (made_own,) = down_product(meta, hidden, weight_out, experts, True)
+    halves = [[GROUP * e + low for e in range(experts)] for low in range(GROUP)]
+    near = lax.all_to_all(made_own, "dp", 0, 0, axis_index_groups=halves, tiled=True)
+    partner, forward = together(partner, forward)
+    partner = after(partner, made_own)
+    made = down_product(meta, partner, weight_out, experts, False)
+    far = [swapped(made[n], QUAD * (2 * n + 1)) for n in range(experts)]
+    if middle:
+        inner = (rank >> 2 & 1) != (rank >> 3 & 1)
+        part = after(jnp.where(inner, cut[::-1], forward), partner)
+        latent_parts += [part, swapped(part, 2)]
+        latent_codes += [[8, 12], [8 ^ 2, 12 ^ 2]]
+    moe_out = unpack(meta, expert_ids, gate_weights, near, far, width)
     given, kept = latent_sums(meta, mine, other, latent_parts, latent_codes)
     projected = kept + swapped(given, 1).astype(jnp.float32)
     latent_cache = latent_finish(projected, latent_gain, length)

time: 299 us -> 269 us (0.90)
  waiting for transfers between devices: 177 us -> 131 us
  starting transfers between devices: 19.6 us -> 32.2 us
  Pallas kernels: 60.3 us -> 64.6 us
    ppermute x16, waiting for transfers between devices: 162 us -> 127 us  [swapped(): lax.ppermute(block, 'dp', [(low, low ^ bits) for low in range(count)])]
    ppermute x1 -> x2, waiting for transfers between devices: 13.9 us -> 0.01 us  [the longest x1 0.01 us: shards(): lax.ppermute(cut, 'dp', [(low, low ^ QUAD) for low in range(QUAD, 3 * QUA...]
    reshape x2 -> x0, local copies, waits for them, and re-layouts: 6.38 us -> none  [core_columns(): return picked.reshape(rows, width // 2)]
    ppermute x1 -> x2, starting transfers between devices: 1.49 us -> 7.19 us  [the longest x1 3.7 us: shards(): lax.ppermute(cut, 'dp', [(low, low ^ QUAD) for low in range(QUAD, 3 * QUA...]
    all_to_all x0 -> x1, starting transfers between devices: none -> 4.95 us  [shards(): lax.all_to_all(made_own, 'dp', 0, 0, axis_index_groups=halves, tiled=True)]
    pallas_call x6, Pallas kernels: 47.2 us -> 52 us  [the longest x2 18.4 us: gate_up_product(): pl.pallas_call(functools.partial(gate_up_body, count), grid_spec=pltpu.Pr...]
    pallas_call x0 -> x1, local copies, waits for them, and re-layouts: none -> 3.9 us  [core_split(): pl.pallas_call(core_split_body, grid_spec=pltpu.PrefetchScalarGridSpec(nu...]
    ppermute x0 -> x1, local copies, waits for them, and re-layouts: none -> 3.83 us  [swapped(): lax.ppermute(block, 'dp', [(low, low ^ bits) for low in range(count)])]
  transfers between devices with their start and end apart: 18 -> 20, of which waited for: 8 -> 11; matrix products, arithmetic and copies ran while one was open for 7% -> 9% of each run, Pallas kernels for 16% -> 24%
where the time goes in v3:
time: 269 us; the launch traced here: 265 us
  waiting for transfers between devices  131 us (49%)
  Pallas kernels  64.6 us (24%)
  starting transfers between devices  32.2 us (12%)
  local copies, waits for them, and re-layouts  28.9 us (11%)
  other arithmetic  8.24 us (3%)
    ppermute x16, waiting for transfers between devices, swapped(): lax.ppermute(block, 'dp', [(low, low ^ bits) for low in range(count)])  127 us
    pallas_call x2, Pallas kernels, gate_up_product(): pl.pallas_call(functools.partial(gate_up_body, count), grid_spec=pltpu.Pr...  18.4 us
    unnamed x46, local copies, waits for them, and re-layouts  17 us
    pallas_call x2, Pallas kernels, down_product(): pl.pallas_call(functools.partial(down_body, joined), grid_spec=pltpu.Pref...  15.8 us
    ppermute x16, starting transfers between devices, swapped(): lax.ppermute(block, 'dp', [(low, low ^ bits) for low in range(count)])  14.7 us
    pallas_call x1, Pallas kernels, unpack(): pl.pallas_call(functools.partial(unpack_body, size), grid_spec=pltpu.Pref...  10.1 us
    pallas_call x1, Pallas kernels, core_split(): pl.pallas_call(core_split_body, grid_spec=pltpu.PrefetchScalarGridSpec(nu...  7.7 us
    pallas_call x1, Pallas kernels, pack(): pl.pallas_call(functools.partial(pack_body, chunks), grid_spec=pltpu.Pref...  6.6 us
  transfers between devices with their start and end apart: 20, of which 11 were waited for; matrix products, arithmetic and copies ran while one was open for 9% of the time, Pallas kernels for 24%

profile of v3, /device:TPU:8, one launch (start us, length us, event | category | flops | bytes accessed | tf_op | source)
XLA Modules:
  0.0 265.5 jit_solution(6043351947239223439)
XLA Ops:
  6.7 6.6 %pack_rows.1.refs_0_ = bf16[4,136,3584]{2,1,0:T(8,128)(2,1)} custom-call(s32[2]{0:T(128)} %pad_add_fusion.meta_ref, s32[256,1]{1,0:T(8,128)} %copy.38.column_ref, s32[1,256]{1,0:T(1,128)} %bitcast.6, bf16[256,7168]{1,0:T(8,128)(2,1)} %tokens_ref.1, bf16[256,7168]{1,0:T(8,128)(2,1)} %tokens_ref.1), custom_call_target="tpu_custom_call" | custom-call | flops 1879048192 | bytes 7340032 | tf_op jit(solution)/shard_map/pack_rows/pallas_call | solution.py:63
  13.3 3.6 %collective-permute-done.refs_1_ = bf16[1,448,576]{2,1,0:T(8,128)(2,1)S(1)} collective-permute-done((bf16[1,448,576]{2,1,0:T(8,128)(2,1)}, bf16[1,448,576]{2,1,0:T(8,128)(2,1)S(1)}, u32[]{:S(2)}, u32[]{:S(2)}) %collective-permute-start) | collective-permute-done | bytes 516128 | tf_op jit(solution)/shard_map/ppermute | solution.py:19
  17.7 5.3 %all-to-all-start = ((bf16[4,136,3584]{2,1,0:T(8,128)(2,1)}), bf16[4,136,3584]{2,1,0:T(8,128)(2,1)}, u32[]{:S(2)}, u32[]{:S(2)}) async-start(bf16[4,136,3584]{2,1,0:T(8,128)(2,1)} %after.6), calls=%async_computation | async-start | bytes 7798784 | tf_op jit(solution)/shard_map/all_to_all | solution.py:437
  23.0 59.1 %collective-permute-done.2.refs_4_.refs_1_ = bf16[896,2048]{1,0:T(8,128)(2,1)} collective-permute-done((bf16[896,2048]{1,0:T(8,128)(2,1)}, bf16[896,2048]{1,0:T(8,128)(2,1)}, u32[]{:S(2)}, u32[]{:S(2)}) %collective-permute-start.2) | collective-permute-done | bytes 3670048 | tf_op jit(solution)/shard_map/ppermute | solution.py:19
  82.6 7.7 %core_split.1 = (bf16[8,256,448]{2,1,0:T(8,128)(2,1)}, bf16[8,256,448]{2,1,0:T(8,128)(2,1)}) custom-call(s32[2]{0:T(128)} %pad_add_fusion.meta_ref, bf16[256,7168]{1,0:T(8,128)(2,1)} %tokens_ref.1), custom_call_target="tpu_custom_call" | custom-call | tf_op jit(solution)/shard_map/core_split/pallas_call | solution.py:392
  90.3 3.9 %copy.39 = bf16[8,256,448]{1,2,0:T(8,128)(2,1)} copy(bf16[8,256,448]{2,1,0:T(8,128)(2,1)} %get-tuple-element.21) | data formatting | bytes 3670016 | tf_op jit(solution)/shard_map/core_split/pallas_call | solution.py:392
  97.1 3.5 %collective-permute-start.6 = (bf16[2,448,576]{2,1,0:T(8,128)(2,1)S(1)}, bf16[2,448,576]{2,1,0:T(8,128)(2,1)S(1)}, u32[]{:S(2)}, u32[]{:S(2)}) collective-permute-start(bf16[2,448,576]{2,1,0:T(8,128)(2,1)S(1)} %pad_maximum_fusion.refs_0_), channel_id=1, source_target_pairs={{4,8},{5,9},{6,10},{7,11},{8,4},{9,5},{10,6},{11,7},{20,24},{21,25... | collective-permute-start | bytes 3096584 | tf_op jit(solution)/shard_map/ppermute | solution.py:453
  100.6 3.8 %copy.40.refs_4_ = bf16[8,256,448]{2,1,0:T(8,128)(2,1)} copy(bf16[8,256,448]{1,2,0:T(8,128)(2,1)} %collective-permute-done.4) | data formatting | bytes 3670016 | tf_op jit(solution)/shard_map/ppermute | solution.py:19
  104.5 3.6 %all-to-all-done.refs_0_ = bf16[4,136,3584]{2,1,0:T(8,128)(2,1)} async-done(((bf16[4,136,3584]{2,1,0:T(8,128)(2,1)}), bf16[4,136,3584]{2,1,0:T(8,128)(2,1)}, u32[]{:S(2)}, u32[]{:S(2)}) %all-to-all-start) | async-done | bytes 3899424 | tf_op jit(solution)/shard_map/all_to_all | solution.py:437
  110.7 9.2 %gate_up_product.2 = bf16[272,2048]{1,0:T(8,128)(2,1)S(1)} custom-call(s32[2]{0:T(128)S(1)} %copy-done.7, bf16[4,136,3584]{2,1,0:T(8,128)(2,1)} %get-tuple-element.24.refs_0_.refs_1_, bf16[4,136,3584]{2,1,0:T(8,128)(2,1)} %get-tuple-element.24.refs_0_.refs_1_, bf16[896,2048]{1,0:T(8,128)(2,1)S(1)} %copy-done.2, bf16[896,2048]{1,0:T(8,128)(2,1)} %get-tuple-element.25.refs_3_, ...), custom_call_target="tpu_custom_call" | custom-call | flops 3992977408 | bytes 16629760 | tf_op jit(solution)/shard_map/gate_up_product/pallas_call | solution.py:212
  122.0 9.2 %gate_up_product.3.refs_1_ = f32[272,2048]{1,0:T(8,128)S(1)} custom-call(s32[2]{0:T(128)S(1)} %copy-done.7, bf16[4,136,3584]{2,1,0:T(8,128)(2,1)} %get-tuple-element.24.refs_0_.refs_1_, bf16[4,136,3584]{2,1,0:T(8,128)(2,1)} %get-tuple-element.24.refs_0_.refs_1_, bf16[896,2048]{1,0:T(8,128)(2,1)S(1)} %copy-done.2, ...), custom_call_target="tpu_custom_call" | custom-call | flops 3992977408 | bytes 16629760 | tf_op jit(solution)/shard_map/gate_up_product/pallas_call | solution.py:212
  132.6 5.5 %collective-permute-done.8.refs_0_ = bf16[1024,896]{1,0:T(8,128)(2,1)} collective-permute-done((bf16[1024,896]{1,0:T(8,128)(2,1)}, bf16[1024,896]{1,0:T(8,128)(2,1)}, u32[]{:S(2)}, u32[]{:S(2)}) %collective-permute-start.8) | collective-permute-done | bytes 1835040 | tf_op jit(solution)/shard_map/ppermute | solution.py:19
  144.8 3.7 %collective-permute-start.13 = (bf16[2,448,576]{2,1,0:T(8,128)(2,1)}, bf16[2,448,576]{2,1,0:T(8,128)(2,1)S(1)}, u32[]{:S(2)}, u32[]{:S(2)}) collective-permute-start(bf16[2,448,576]{2,1,0:T(8,128)(2,1)} %get-tuple-element.29), channel_id=1, source_target_pairs={{4,0},{5,1},{6,2},{7,3},{8,12},{9,13},{10,14},{11,15},{20,16},{21,... | collective-permute-start | bytes 3096584 | tf_op jit(solution)/shard_map/ppermute | solution.py:471
  155.1 7.9 %down_product.2.refs_1_ = bf16[2,136,3584]{2,1,0:T(8,128)(2,1)} custom-call(s32[2]{0:T(128)} %pad_add_fusion.meta_ref, bf16[272,1024]{1,0:T(8,128)(2,1)} %copy-done.12, bf16[1024,896]{1,0:T(8,128)(2,1)} %refs_0_.3, bf16[1024,896]{1,0:T(8,128)(2,1)} %after.7.refs_1_, bf16[1024,896]{1,0:T(8,128)(2,1)} %copy-done.10, bf16[1024,896]{1,0:T(8,128)(2,1)} %after.8.refs_3_), custom_call_target="tpu_custom_call" | custom-call | flops 1996488704 | bytes 9846784 | tf_op jit(solution)/shard_map/down_product/pallas_call | solution.py:265
  162.9 4.9 %all-to-all-start.1 = ((bf16[2,136,3584]{2,1,0:T(8,128)(2,1)}), bf16[2,136,3584]{2,1,0:T(8,128)(2,1)}, u32[]{:S(2)}, u32[]{:S(2)}) async-start(bf16[2,136,3584]{2,1,0:T(8,128)(2,1)} %down_product.2.refs_1_), calls=%async_computation.1 | async-start | bytes 3899392 | tf_op jit(solution)/shard_map/all_to_all | solution.py:478
  168.7 15.2 %collective-permute-done.12.refs_0_ = bf16[272,1024]{1,0:T(8,128)(2,1)S(1)} collective-permute-done((bf16[272,1024]{1,0:T(8,128)(2,1)S(1)}, bf16[272,1024]{1,0:T(8,128)(2,1)S(1)}, u32[]{:S(2)}, u32[]{:S(2)}) %collective-permute-start.12) | collective-permute-done | bytes 557088 | tf_op jit(solution)/shard_map/ppermute | solution.py:19
  187.0 2.6 reverse_select_fusion.refs_0_
  191.4 7.9 %down_product.3 = (bf16[136,3584]{1,0:T(8,128)(2,1)}, bf16[136,3584]{1,0:T(8,128)(2,1)}) custom-call(s32[2]{0:T(128)} %pad_add_fusion.meta_ref, bf16[272,1024]{1,0:T(8,128)(2,1)} %after.10.refs_1_.hidden_ref, bf16[1024,896]{1,0:T(8,128)(2,1)} %refs_0_.3, bf16[1024,896]{1,0:T(8,128)(2,1)} %after.7.refs_1_, bf16[1024,896]{1,0:T(8,128)(2,1)} %copy-done.10, ...), custom_call_target="tpu_custom_call" | custom-call | flops 1996488704 | bytes 9846784 | tf_op jit(solution)/shard_map/down_product/pallas_call | solution.py:265
  199.3 2.5 collective-permute-start.16
  201.8 2.7 %collective-permute-start.17 = (bf16[136,3584]{1,0:T(8,128)(2,1)}, bf16[136,3584]{1,0:T(8,128)(2,1)}, u32[]{:S(2)}, u32[]{:S(2)}) collective-permute-start(bf16[136,3584]{1,0:T(8,128)(2,1)} %get-tuple-element.37), channel_id=1, source_target_pairs={{0,12},{1,13},{2,14},{3,15},{4,8},{5,9},{6,10},{7,11},{8,4},{9,5},... | collective-permute-start | bytes 2924552 | tf_op jit(solution)/shard_map/ppermute | solution.py:19
  204.5 12.8 %collective-permute-done.14.refs_3_ = bf16[2,448,576]{2,1,0:T(8,128)(2,1)} collective-permute-done((bf16[2,448,576]{2,1,0:T(8,128)(2,1)}, bf16[2,448,576]{2,1,0:T(8,128)(2,1)}, u32[]{:S(2)}, u32[]{:S(2)}) %collective-permute-start.14) | collective-permute-done | bytes 1032224 | tf_op jit(solution)/shard_map/ppermute | solution.py:19
  219.0 5.9 %latent_product.1 = (bf16[256,576]{1,0:T(8,128)(2,1)}, f32[256,576]{1,0:T(8,128)S(1)}) custom-call(s32[2]{0:T(128)S(1)} %copy-done.8, bf16[8,256,448]{2,1,0:T(8,128)(2,1)S(1)} %copy-done.6, bf16[8,256,448]{2,1,0:T(8,128)(2,1)S(1)} %copy-done.1, bf16[2,448,576]{2,1,0:T(8,128)(2,1)S(1)} %copy-done.4, bf16[2,448,576]{2,1,0:T(8,128)(2,1)S(1)} %collective-permute-done.11.refs_1_, ...), custom_call_target="tpu_custom_call" | custom-call | flops 2113929216 | bytes 7798784 | tf_op jit(solution)/shard_map/latent_product/pallas_call | solution.py:338
  226.5 25.3 %collective-permute-done.16.refs_0_ = bf16[136,3584]{1,0:T(8,128)(2,1)} collective-permute-done((bf16[136,3584]{1,0:T(8,128)(2,1)}, bf16[136,3584]{1,0:T(8,128)(2,1)}, u32[]{:S(2)}, u32[]{:S(2)}) %collective-permute-start.16) | collective-permute-done | bytes 974880 | tf_op jit(solution)/shard_map/ppermute | solution.py:19
  252.9 10.1 %unpack_rows.1 = bf16[256,7168]{1,0:T(8,128)(2,1)} custom-call(s32[2]{0:T(128)} %pad_add_fusion.meta_ref, s32[256,1]{1,0:T(8,128)} %copy.38.column_ref, s32[1,256]{1,0:T(1,128)} %bitcast.7, f32[256,1]{1,0:T(8,128)} %copy.43.gate_ref, bf16[2,136,3584]{2,1,0:T(8,128)(2,1)} %all-to-all-done.1.near_ref, bf16[136,3584]{1,0:T(8,128)(2,1)} %collective-permute-done.16.refs_0_, ...), custom_call_target="tpu_custom_call" | custom-call | flops 1879048192 | bytes 7340032 | tf_op jit(solution)/shard_map/unpack_rows/pallas_call | solution.py:125
  (98 shorter events, 41.9 us)
Async XLA Ops:
  0.6 81.5 %collective-permute-start.2 = (bf16[896,2048]{1,0:T(8,128)(2,1)}, bf16[896,2048]{1,0:T(8,128)(2,1)}, u32[]{:S(2)}, u32[]{:S(2)}) collective-permute-start(bf16[896,2048]{1,0:T(8,128)(2,1)} %refs_2_.3), channel_id=1, source_target_pairs={{0,2},{1,3},{2,0},{3,1},{4,6},{5,7},{6,4},{7,5},{8,10},{9,11},{10,... | collective-permute-start | bytes 11010056 | tf_op jit(solution)/shard_map/ppermute | solution.py:19
  2.2 14.6 %collective-permute-start = (bf16[1,448,576]{2,1,0:T(8,128)(2,1)}, bf16[1,448,576]{2,1,0:T(8,128)(2,1)S(1)}, u32[]{:S(2)}, u32[]{:S(2)}) collective-permute-start(bf16[1,448,576]{2,1,0:T(8,128)(2,1)} %bitcast.4), channel_id=1, source_target_pairs={{0,4},{1,5},{2,6},{3,7},{4,0},{5,1},{6,2},{7,3},{8,12},{9,13},{10,... | collective-permute-start | bytes 1548296 | tf_op jit(solution)/shard_map/ppermute | solution.py:19
  17.7 90.3 %all-to-all-start = ((bf16[4,136,3584]{2,1,0:T(8,128)(2,1)}), bf16[4,136,3584]{2,1,0:T(8,128)(2,1)}, u32[]{:S(2)}, u32[]{:S(2)}) async-start(bf16[4,136,3584]{2,1,0:T(8,128)(2,1)} %after.6), calls=%async_computation | async-start | bytes 7798784 | tf_op jit(solution)/shard_map/all_to_all | solution.py:437
  23.0 81.5 %collective-permute-start.1 = (bf16[896,2048]{1,0:T(8,128)(2,1)}, bf16[896,2048]{1,0:T(8,128)(2,1)}, u32[]{:S(2)}, u32[]{:S(2)}) collective-permute-start(bf16[896,2048]{1,0:T(8,128)(2,1)} %refs_2_.3), channel_id=1, source_target_pairs={{0,1},{1,0},{2,3},{3,2},{4,5},{5,4},{6,7},{7,6},{8,9},{9,8},{10,11... | collective-permute-start | bytes 11010056 | tf_op jit(solution)/shard_map/ppermute | solution.py:19
  82.1 26.0 %collective-permute-start.3 = (bf16[896,2048]{1,0:T(8,128)(2,1)}, bf16[896,2048]{1,0:T(8,128)(2,1)}, u32[]{:S(2)}, u32[]{:S(2)}) collective-permute-start(bf16[896,2048]{1,0:T(8,128)(2,1)} %collective-permute-done.2.refs_4_.refs_1_), channel_id=1, source_target_pairs={{0,1},{1,0},{2,3},{3,2},{4,5},{5,4},{6,7},{7,6},{8,9},{9,8},{10,11... | collective-permute-start | bytes 11010056 | tf_op jit(solution)/shard_map/ppermute | solution.py:19
  82.1 12.1 %collective-permute-start.7 = (bf16[1024,896]{1,0:T(8,128)(2,1)}, bf16[1024,896]{1,0:T(8,128)(2,1)S(1)}, u32[]{:S(2)}, u32[]{:S(2)}) collective-permute-start(bf16[1024,896]{1,0:T(8,128)(2,1)} %refs_0_.3), channel_id=1, source_target_pairs={{0,1},{1,0},{2,3},{3,2},{4,5},{5,4},{6,7},{7,6},{8,9},{9,8},{10,11... | collective-permute-start | bytes 5505032 | tf_op jit(solution)/shard_map/ppermute | solution.py:19
  94.2 6.4 %collective-permute-start.4 = (bf16[8,256,448]{1,2,0:T(8,128)(2,1)}, bf16[8,256,448]{1,2,0:T(8,128)(2,1)}, u32[]{:S(2)}, u32[]{:S(2)}) collective-permute-start(bf16[8,256,448]{1,2,0:T(8,128)(2,1)} %copy.39), channel_id=1, source_target_pairs={{0,1},{1,0},{2,3},{3,2},{4,5},{5,4},{6,7},{7,6},{8,9},{9,8},{10,11... | collective-permute-start | bytes 5505032 | tf_op jit(solution)/shard_map/ppermute | solution.py:19
  95.4 42.7 %collective-permute-start.8 = (bf16[1024,896]{1,0:T(8,128)(2,1)}, bf16[1024,896]{1,0:T(8,128)(2,1)}, u32[]{:S(2)}, u32[]{:S(2)}) collective-permute-start(bf16[1024,896]{1,0:T(8,128)(2,1)} %after.7.refs_1_), channel_id=1, source_target_pairs={{0,2},{1,3},{2,0},{3,1},{4,6},{5,7},{6,4},{7,5},{8,10},{9,11},{10,... | collective-permute-start | bytes 5505032 | tf_op jit(solution)/shard_map/ppermute | solution.py:19
  97.1 43.2 %collective-permute-start.6 = (bf16[2,448,576]{2,1,0:T(8,128)(2,1)S(1)}, bf16[2,448,576]{2,1,0:T(8,128)(2,1)S(1)}, u32[]{:S(2)}, u32[]{:S(2)}) collective-permute-start(bf16[2,448,576]{2,1,0:T(8,128)(2,1)S(1)} %pad_maximum_fusion.refs_0_), channel_id=1, source_target_pairs={{4,8},{5,9},{6,10},{7,11},{8,4},{9,5},{10,6},{11,7},{20,24},{21,25... | collective-permute-start | bytes 3096584 | tf_op jit(solution)/shard_map/ppermute | solution.py:453
  119.9 24.9 %collective-permute-start.5 = (bf16[272,2048]{1,0:T(8,128)(2,1)S(1)}, bf16[272,2048]{1,0:T(8,128)(2,1)}, u32[]{:S(2)}, u32[]{:S(2)}) collective-permute-start(bf16[272,2048]{1,0:T(8,128)(2,1)S(1)} %gate_up_product.2), channel_id=1, source_target_pairs={{0,4},{1,5},{2,6},{3,7},{4,0},{5,1},{6,2},{7,3},{8,12},{9,13},{10,... | collective-permute-start | bytes 3342344 | tf_op jit(solution)/shard_map/ppermute | solution.py:19
  139.8 2.7 %collective-permute-start.10 = (bf16[512,896]{1,0:T(8,128)(2,1)S(1)}, bf16[512,896]{1,0:T(8,128)(2,1)}, u32[]{:S(2)}, u32[]{:S(2)}) collective-permute-start(bf16[512,896]{1,0:T(8,128)(2,1)S(1)} %get-tuple-element.44), channel_id=1, source_target_pairs={{0,1},{1,0},{2,3},{3,2},{4,5},{5,4},{6,7},{7,6},{8,9},{9,8},{10,11... | collective-permute-start | bytes 2752520 | tf_op jit(solution)/shard_map/ppermute | solution.py:19
  139.8 3.9 %collective-permute-start.9 = (bf16[512,896]{1,0:T(8,128)(2,1)S(1)}, bf16[512,896]{1,0:T(8,128)(2,1)}, u32[]{:S(2)}, u32[]{:S(2)}) collective-permute-start(bf16[512,896]{1,0:T(8,128)(2,1)S(1)} %get-tuple-element.45), channel_id=1, source_target_pairs={{0,1},{1,0},{2,3},{3,2},{4,5},{5,4},{6,7},{7,6},{8,9},{9,8},{10,11... | collective-permute-start | bytes 2752520 | tf_op jit(solution)/shard_map/ppermute | solution.py:19
  144.8 39.2 %collective-permute-start.13 = (bf16[2,448,576]{2,1,0:T(8,128)(2,1)}, bf16[2,448,576]{2,1,0:T(8,128)(2,1)S(1)}, u32[]{:S(2)}, u32[]{:S(2)}) collective-permute-start(bf16[2,448,576]{2,1,0:T(8,128)(2,1)} %get-tuple-element.29), channel_id=1, source_target_pairs={{4,0},{5,1},{6,2},{7,3},{8,12},{9,13},{10,14},{11,15},{20,16},{21,... | collective-permute-start | bytes 3096584 | tf_op jit(solution)/shard_map/ppermute | solution.py:471
  151.0 32.9 %collective-permute-start.12 = (bf16[272,1024]{1,0:T(8,128)(2,1)S(1)}, bf16[272,1024]{1,0:T(8,128)(2,1)S(1)}, u32[]{:S(2)}, u32[]{:S(2)}) collective-permute-start(bf16[272,1024]{1,0:T(8,128)(2,1)S(1)} %fusion.refs_1_.hidden_ref), channel_id=1, source_target_pairs={{0,4},{1,5},{2,6},{3,7},{4,0},{5,1},{6,2},{7,3},{8,12},{9,13},{10,... | collective-permute-start | bytes 1671176 | tf_op jit(solution)/shard_map/ppermute | solution.py:19
  162.9 63.6 %all-to-all-start.1 = ((bf16[2,136,3584]{2,1,0:T(8,128)(2,1)}), bf16[2,136,3584]{2,1,0:T(8,128)(2,1)}, u32[]{:S(2)}, u32[]{:S(2)}) async-start(bf16[2,136,3584]{2,1,0:T(8,128)(2,1)} %down_product.2.refs_1_), calls=%async_computation.1 | async-start | bytes 3899392 | tf_op jit(solution)/shard_map/all_to_all | solution.py:478
  167.9 36.6 %collective-permute-start.11 = (bf16[2,448,576]{2,1,0:T(8,128)(2,1)}, bf16[2,448,576]{2,1,0:T(8,128)(2,1)S(1)}, u32[]{:S(2)}, u32[]{:S(2)}) collective-permute-start(bf16[2,448,576]{2,1,0:T(8,128)(2,1)} %after.9.refs_0_), channel_id=1, source_target_pairs={{0,2},{1,3},{2,0},{3,1},{4,6},{5,7},{6,4},{7,5},{8,10},{9,11},{10,... | collective-permute-start | bytes 3096584 | tf_op jit(solution)/shard_map/ppermute | solution.py:19
  189.6 27.8 %copy-start.1 = (bf16[8,256,448]{2,1,0:T(8,128)(2,1)S(1)}, bf16[8,256,448]{2,1,0:T(8,128)(2,1)}, u32[]{:S(2)}) copy-start(bf16[8,256,448]{2,1,0:T(8,128)(2,1)} %get-tuple-element.23.other_ref) | copy-start | bytes 5505028
  189.6 27.8 %copy-start.4 = (bf16[2,448,576]{2,1,0:T(8,128)(2,1)S(1)}, bf16[2,448,576]{2,1,0:T(8,128)(2,1)}, u32[]{:S(2)}) copy-start(bf16[2,448,576]{2,1,0:T(8,128)(2,1)} %after.9.refs_0_) | copy-start | bytes 3096580
  189.6 27.8 %copy-start.5 = (bf16[2,448,576]{2,1,0:T(8,128)(2,1)S(1)}, bf16[2,448,576]{2,1,0:T(8,128)(2,1)}, u32[]{:S(2)}) copy-start(bf16[2,448,576]{2,1,0:T(8,128)(2,1)} %after.11.refs_2_) | copy-start | bytes 3096580
  189.6 27.8 %copy-start.8 = (s32[2]{0:T(128)S(1)}, s32[2]{0:T(128)}, u32[]{:S(2)}) copy-start(s32[2]{0:T(128)} %pad_add_fusion.meta_ref) | copy-start | bytes 28
  189.6 27.8 %collective-permute-start.14 = (bf16[2,448,576]{2,1,0:T(8,128)(2,1)}, bf16[2,448,576]{2,1,0:T(8,128)(2,1)}, u32[]{:S(2)}, u32[]{:S(2)}) collective-permute-start(bf16[2,448,576]{2,1,0:T(8,128)(2,1)} %after.11.refs_2_), channel_id=1, source_target_pairs={{0,2},{1,3},{2,0},{3,1},{4,6},{5,7},{6,4},{7,5},{8,10},{9,11},{10,... | collective-permute-start | bytes 3096584 | tf_op jit(solution)/shard_map/ppermute | solution.py:19
  199.3 52.5 %collective-permute-start.16 = (bf16[136,3584]{1,0:T(8,128)(2,1)}, bf16[136,3584]{1,0:T(8,128)(2,1)}, u32[]{:S(2)}, u32[]{:S(2)}) collective-permute-start(bf16[136,3584]{1,0:T(8,128)(2,1)} %get-tuple-element.36), channel_id=1, source_target_pairs={{0,4},{1,5},{2,6},{3,7},{4,0},{5,1},{6,2},{7,3},{8,12},{9,13},{10,... | collective-permute-start | bytes 2924552 | tf_op jit(solution)/shard_map/ppermute | solution.py:19
  201.8 51.1 %collective-permute-start.17 = (bf16[136,3584]{1,0:T(8,128)(2,1)}, bf16[136,3584]{1,0:T(8,128)(2,1)}, u32[]{:S(2)}, u32[]{:S(2)}) collective-permute-start(bf16[136,3584]{1,0:T(8,128)(2,1)} %get-tuple-element.37), channel_id=1, source_target_pairs={{0,12},{1,13},{2,14},{3,15},{4,8},{5,9},{6,10},{7,11},{8,4},{9,5},... | collective-permute-start | bytes 2924552 | tf_op jit(solution)/shard_map/ppermute | solution.py:19
  224.9 38.1 %collective-permute-start.15 = (bf16[256,576]{1,0:T(8,128)(2,1)}, bf16[256,576]{1,0:T(8,128)(2,1)S(1)}, u32[]{:S(2)}, u32[]{:S(2)}) collective-permute-start(bf16[256,576]{1,0:T(8,128)(2,1)} %get-tuple-element.35), channel_id=1, source_target_pairs={{0,1},{1,0},{2,3},{3,2},{4,5},{5,4},{6,7},{7,6},{8,9},{9,8},{10,11... | collective-permute-start | bytes 884744 | tf_op jit(solution)/shard_map/ppermute | solution.py:19
  (17 other events, 39.4 us)

commit v4 on v3

--- a/solution.py
+++ b/solution.py
@@ -19,130 +19,149 @@
     return lax.ppermute(block, "dp", [(low, low ^ bits) for low in range(count)])
 
 
-def chosen_slots(meta_ref, column_ids, row_ids):
-    rows = column_ids.shape[0]
-    length = meta_ref[1]
-    own = lax.broadcasted_iota(jnp.int32, (rows, rows), 0)
-    other = lax.broadcasted_iota(jnp.int32, (rows, rows), 1)
-    earlier = (column_ids == row_ids) & (other < own) & (other < length)
+def slots_of_rows(rank_ref, lengths_ref, ids_row):
+    rows = ids_row.shape[1]
+    length = lengths_ref[rank_ref[0]]
+    down = lax.broadcasted_iota(jnp.int32, (rows, rows), 0)
+    along = lax.broadcasted_iota(jnp.int32, (rows, rows), 1)
+    ids_column = jnp.sum(
+        jnp.where(down == along, ids_row.astype(jnp.float32), 0.0), axis=1, keepdims=True
+    ).astype(jnp.int32)
+    return length, down, along, ids_column, ids_column == ids_row
+
+
+def picks_by_slot(rank_ref, lengths_ref, ids_row, experts, size, picks_ref):
+    rows = ids_row.shape[1]
+    length, down, along, _, same = slots_of_rows(rank_ref, lengths_ref, ids_row)
+    earlier = same & (down < along) & (down < length)
+    place = jnp.sum(earlier.astype(jnp.float32), axis=0, keepdims=True).astype(jnp.int32)
+    live = lax.broadcasted_iota(jnp.int32, (1, rows), 1) < length
+    chosen = jnp.where(live, ids_row, -1)
+    slot = lax.broadcasted_iota(jnp.int32, (size, rows), 0)
+    for expert in range(experts):
+        hit = (place == slot) & (chosen == expert)
+        picks_ref[expert] = hit.astype(jnp.float32).astype(jnp.bfloat16)
+
+
+def picks_by_row(rank_ref, lengths_ref, ids_row, experts, size, picks_ref):
+    rows = ids_row.shape[1]
+    length, down, along, ids_column, same = slots_of_rows(rank_ref, lengths_ref, ids_row)
+    earlier = same & (along < down) & (along < length)
     place = jnp.sum(earlier.astype(jnp.float32), axis=1, keepdims=True).astype(jnp.int32)
     live = lax.broadcasted_iota(jnp.int32, (rows, 1), 0) < length
-    return jnp.where(live, column_ids, -1), place
-
-
-def selector(expert_column, place_column, expert, start, size):
-    rows = expert_column.shape[0]
-    slot = lax.broadcasted_iota(jnp.int32, (rows, size), 1) + start
-    hit = (place_column == slot) & (expert_column == expert)
-    return hit.astype(jnp.float32).astype(jnp.bfloat16)
-
-
-def pack_body(chunks, meta_ref, column_ref, row_ref, low_ref, high_ref, *outs):
-    expert_column, place_column = chosen_slots(meta_ref, column_ref[...], row_ref[...])
-    sources = (low_ref[...], high_ref[...])
-    for (start, size), out_ref in zip(chunks, outs):
-        for expert in range(out_ref.shape[0] // 2):
-            picks = selector(expert_column, place_column, expert, start, size)
-            for side, source in enumerate(sources):
-                out_ref[2 * expert + side] = lax.dot_general(
-                    picks,
-                    source,
-                    (((0,), (0,)), ((), ())),
-                    preferred_element_type=jnp.float32,
-                ).astype(jnp.bfloat16)
-
-
-def pack(meta, ids, tokens, chunks, pieces):
+    chosen = jnp.where(live, ids_column, -1)
+    slot = lax.broadcasted_iota(jnp.int32, (rows, size), 1)
+    for expert in range(experts):
+        hit = (place == slot) & (chosen == expert)
+        picks_ref[expert] = hit.astype(jnp.float32).astype(jnp.bfloat16)
+
+
+def pack_body(rank_ref, lengths_ref, ids_ref, low_ref, high_ref, out_ref, picks_ref):
+    experts, size, _ = picks_ref.shape
+
+    @pl.when(pl.program_id(0) == 0)
+    def _():
+        picks_by_slot(rank_ref, lengths_ref, ids_ref[...], experts, size, picks_ref)
+
+    for side, source_ref in enumerate((low_ref, high_ref)):
+        for expert in range(experts):
+            out_ref[2 * expert + side] = jnp.dot(
+                picks_ref[expert], source_ref[...], preferred_element_type=jnp.float32
+            ).astype(jnp.bfloat16)
+
+
+def pack(rank_array, lengths, ids, tokens, experts, size):
     rows, width = tokens.shape
     part = width // GROUP
 
     def column_of(side):
-        return lambda k, meta_ref: (0, side * QUAD + ((meta_ref[0] % QUAD) ^ k))
-
-    whole = lambda k, meta_ref: (0, 0)
-    return pl.pallas_call(
-        functools.partial(pack_body, chunks),
+        return lambda k, rank_ref, lengths_ref: (0, side * QUAD + ((rank_ref[0] % QUAD) ^ k))
+
+    whole = lambda k, rank_ref, lengths_ref: (0, 0)
+    return pl.pallas_call(
+        pack_body,
         grid_spec=pltpu.PrefetchScalarGridSpec(
-            num_scalar_prefetch=1,
+            num_scalar_prefetch=2,
             grid=(QUAD,),
             in_specs=[
-                pl.BlockSpec((rows, 1), whole),
                 pl.BlockSpec((1, rows), whole),
                 pl.BlockSpec((rows, part), column_of(0)),
                 pl.BlockSpec((rows, part), column_of(1)),
             ],
-            out_specs=[
-                pl.BlockSpec((pieces, size, part), lambda k, meta_ref: (0, 0, k))
-                for _, size in chunks
-            ],
-        ),
-        out_shape=[
-            jax.ShapeDtypeStruct((pieces, size, QUAD * part), jnp.bfloat16) for _, size in chunks
-        ],
+            out_specs=pl.BlockSpec(
+                (2 * experts, size, part), lambda k, rank_ref, lengths_ref: (0, 0, k)
+            ),
+            scratch_shapes=[pltpu.VMEM((experts, size, rows), jnp.bfloat16)],
+        ),
+        out_shape=jax.ShapeDtypeStruct((2 * experts, size, QUAD * part), jnp.bfloat16),
         compiler_params=pltpu.CompilerParams(vmem_limit_bytes=58 << 20),
         cost_estimate=pl.CostEstimate(
             flops=4 * rows * rows * width, bytes_accessed=4 * rows * width, transcendentals=0
         ),
         name="pack_rows",
-    )(meta, ids, ids.reshape(1, rows), tokens, tokens)
-
-
-def unpack_body(size, meta_ref, column_ref, row_ref, gate_ref, near_ref, *refs):
-    far_refs, out_ref = refs[:-1], refs[-1]
-    expert_column, place_column = chosen_slots(meta_ref, column_ref[...], row_ref[...])
-    my_expert = meta_ref[0] // GROUP
-    gate = gate_ref[...]
-
-    def blend(parts):
-        total = jnp.zeros(out_ref.shape, jnp.float32)
-        for expert, part in parts:
-            picks = selector(expert_column, place_column, expert, 0, size)
-            total = total + jnp.dot(picks, part, preferred_element_type=jnp.float32)
-        out_ref[...] = (total * gate).astype(jnp.bfloat16)
+    )(rank_array, lengths, ids.reshape(1, rows), tokens, tokens)
+
+
+def unpack_body(near, rank_ref, lengths_ref, ids_ref, gate_ref, *refs):
+    out_ref, picks_ref, gate_column_ref = refs[-3:]
+    experts, rows, size = picks_ref.shape
+    my_expert = rank_ref[0] // GROUP
 
     @pl.when(pl.program_id(0) == 0)
     def _():
-        blend([(expert, near_ref[expert]) for expert in range(near_ref.shape[0])])
-
-    @pl.when(pl.program_id(0) == 1)
-    def _():
-        blend([(my_expert ^ number, ref[...]) for number, ref in enumerate(far_refs)])
-
-
-def unpack(meta, ids, gates, near, far, width):
+        picks_by_row(rank_ref, lengths_ref, ids_ref[...], experts, size, picks_ref)
+        down = lax.broadcasted_iota(jnp.int32, (rows, rows), 0)
+        along = lax.broadcasted_iota(jnp.int32, (rows, rows), 1)
+        gate_column_ref[...] = jnp.sum(
+            jnp.where(down == along, gate_ref[...], 0.0), axis=1, keepdims=True
+        )
+
+    total = jnp.zeros(out_ref.shape, jnp.float32)
+    for number in range(experts):
+        part = refs[0][number] if near else refs[number][...]
+        picks = picks_ref[number if near else my_expert ^ number]
+        total += jnp.dot(picks, part, preferred_element_type=jnp.float32)
+    out_ref[...] = (total * gate_column_ref[...]).astype(jnp.bfloat16)
+
+
+def unpack(rank_array, lengths, ids, gates, parts, width, near, base=()):
     rows = ids.shape[0]
     part = width // GROUP
-    experts, size, _ = near.shape
-
-    def out_index(side, k, meta_ref):
-        quarter = meta_ref[0] % QUAD
-        high = (meta_ref[0] // QUAD) % 2
-        return (0, (high ^ side) * QUAD + (quarter ^ k))
-
-    near_index = lambda side, k, meta_ref: (0, 0, jnp.where(side == 0, k, QUAD - 1))
-    far_index = lambda side, k, meta_ref: (0, jnp.where(side == 1, k, 0))
-    whole = lambda side, k, meta_ref: (0, 0)
-    return pl.pallas_call(
-        functools.partial(unpack_body, size),
+    size = parts[0].shape[-2]
+    experts = parts[0].shape[0] if near else len(parts)
+
+    def out_index(k, rank_ref, lengths_ref):
+        quarter = rank_ref[0] % QUAD
+        high = (rank_ref[0] // QUAD) % 2
+        return (0, (high if near else 1 - high) * QUAD + (quarter ^ k))
+
+    whole = lambda k, rank_ref, lengths_ref: (0, 0)
+    if near:
+        specs = [pl.BlockSpec((experts, size, part), lambda k, rank_ref, lengths_ref: (0, 0, k))]
+    else:
+        specs = [pl.BlockSpec((size, part), lambda k, rank_ref, lengths_ref: (0, k))] * experts
+    return pl.pallas_call(
+        functools.partial(unpack_body, near),
         grid_spec=pltpu.PrefetchScalarGridSpec(
-            num_scalar_prefetch=1,
-            grid=(2, QUAD),
-            in_specs=[
-                pl.BlockSpec((rows, 1), whole),
-                pl.BlockSpec((1, rows), whole),
-                pl.BlockSpec((rows, 1), whole),
-                pl.BlockSpec((experts, size, part), near_index),
-            ]
-            + [pl.BlockSpec((size, part), far_index) for _ in far],
+            num_scalar_prefetch=2,
+            grid=(QUAD,),
+            in_specs=[pl.BlockSpec((1, rows), whole), pl.BlockSpec((1, rows), whole)]
+            + specs
+            + [pl.BlockSpec(memory_space=pl.ANY)] * len(base),
             out_specs=pl.BlockSpec((rows, part), out_index),
+            scratch_shapes=[
+                pltpu.VMEM((experts, rows, size), jnp.bfloat16),
+                pltpu.VMEM((rows, 1), jnp.float32),
+            ],
         ),
         out_shape=jax.ShapeDtypeStruct((rows, width), jnp.bfloat16),
+        input_output_aliases={4 + len(specs): 0} if base else {},
         compiler_params=pltpu.CompilerParams(vmem_limit_bytes=58 << 20),
         cost_estimate=pl.CostEstimate(
-            flops=4 * rows * rows * width, bytes_accessed=4 * rows * width, transcendentals=0
+            flops=2 * rows * rows * width, bytes_accessed=2 * rows * width, transcendentals=0
         ),
         name="unpack_rows",
-    )(meta, ids, ids.reshape(1, rows), gates, near, *far)
+    )(rank_array, lengths, ids.reshape(1, rows), gates.reshape(1, rows), *parts, *base)
 
 
 def idle_body(*refs):
@@ -230,31 +249,48 @@
     )(meta, *[arrived] * count, *shares)
 
 
-def down_body(joined, meta_ref, hidden_ref, *refs):
+def down_body(places, joined, meta_ref, hidden_ref, *refs):
     k = pl.program_id(0)
-    shares, outs = refs[:QUAD], refs[QUAD:]
+    weight, done = refs[-2:]
+    pieces, outs = refs[: len(places)], refs[len(places) : -2]
     count = outs[0].shape[0] if joined else len(outs)
     size = hidden_ref.shape[0] // count
     mine = meta_ref[0] // GROUP
+    moves = []
+    for number, (piece, (turn, start)) in enumerate(zip(pieces, places)):
+        target = weight.at[turn, pl.ds(start, piece.shape[0]), :]
+        moves.append(pltpu.make_async_copy(piece, target, done.at[number]))
+
+    @pl.when(k == 0)
+    def _():
+        for move in moves:
+            move.start()
+
     for turn in range(QUAD):
 
         @pl.when(k == turn)
         def _(turn=turn):
-            made = jnp.dot(
-                hidden_ref[...], shares[turn][...], preferred_element_type=jnp.float32
-            )
-            for number in range(count):
-                rows = made[number * size : (number + 1) * size].astype(jnp.bfloat16)
-                if joined:
-                    outs[0][mine ^ number] = rows
-                else:
-                    outs[number][...] = rows
+            for move, place in zip(moves, places):
+                if place[0] == turn:
+                    move.wait()
+
+    made = jnp.dot(hidden_ref[...], weight[k], preferred_element_type=jnp.float32)
+    for number in range(count):
+        rows = made[number * size : (number + 1) * size].astype(jnp.bfloat16)
+        if joined:
+            outs[0][mine ^ number] = rows
+        else:
+            outs[number][...] = rows
 
 
 def down_product(meta, hidden, shares, count, joined):
     rows, depth = hidden.shape
     part = shares[0].shape[1]
     size = rows // count
+    places, filled = [], 0
+    for share in shares:
+        places.append((filled // depth, filled % depth))
+        filled += share.shape[0]
     whole = lambda k, meta_ref: (0, 0)
     if joined:
         out_specs = [pl.BlockSpec((count, size, part), lambda k, meta_ref: (0, 0, k))]
@@ -263,13 +299,17 @@
         out_specs = [pl.BlockSpec((size, part), lambda k, meta_ref: (0, k))] * count
         shapes = [(size, QUAD * part)] * count
     return pl.pallas_call(
-        functools.partial(down_body, joined),
+        functools.partial(down_body, places, joined),
         grid_spec=pltpu.PrefetchScalarGridSpec(
             num_scalar_prefetch=1,
             grid=(QUAD,),
             in_specs=[pl.BlockSpec((rows, depth), whole)]
-            + [pl.BlockSpec((depth, part), whole) for _ in shares],
+            + [pl.BlockSpec(memory_space=pl.ANY)] * len(shares),
             out_specs=out_specs,
+            scratch_shapes=[
+                pltpu.VMEM((QUAD, depth, part), jnp.bfloat16),
+                pltpu.SemaphoreType.DMA((len(shares),)),
+            ],
         ),
         out_shape=[jax.ShapeDtypeStruct(shape, jnp.bfloat16) for shape in shapes],
         compiler_params=pltpu.CompilerParams(vmem_limit_bytes=58 << 20),
@@ -421,74 +461,84 @@
     pieces = rank_count // QUAD
     hidden_units = gate_up.shape[1] // 2
     length = lengths[rank]
-    meta = jnp.stack([rank.astype(jnp.int32), length])
+    meta = rank.astype(jnp.int32).reshape(1)
     capacity = rows // experts + 2
-    chunks = [(0, -(-capacity // 8) * 8)]
-
-    (packed,) = pack(meta, expert_ids, tokens, chunks, pieces)
+    slots = -(-capacity // 8) * 8
+
+    packed = pack(meta, lengths, expert_ids, tokens, experts, slots)
     columns = [[QUAD * s + low for s in range(pieces)] for low in range(QUAD)]
     mine, other = token_halves(meta, tokens, latent_weight.shape[0])
 
-    gate_2 = swapped(gate_up, 2)
-    latent_1 = swapped(latent_weight[None], QUAD)
+    half = latent_weight.shape[0] // 2
+    middle = pieces == 4 and lax.axis_size("groups") == 2 and half % 16 == 0
+    group = lax.axis_index("groups")
+    first_group = group == 0
+    sent = latent_weight[None]
+    if middle:
+        sent = lax.dynamic_slice_in_dim(sent, group * half, half, 1)
+    latent_1 = swapped(sent, QUAD)
     packed = after(packed, latent_1)
+    gate_2, mine, other = together(swapped(gate_up, 2), mine, swapped(other, 1))
     down_1 = swapped(down_weight, 1)
-    arrived, gate_1, gate_3, mine, other = together(
+    arrived, gate_1, gate_3 = together(
         lax.all_to_all(packed, "dp", 0, 0, axis_index_groups=columns, tiled=True),
         swapped(gate_up, 1),
         swapped(gate_2, 1),
-        mine,
-        swapped(other, 1),
     )
     down_1 = after(down_1, gate_2)
-    down_3 = swapped(down_1, 2)
-    held, codes = jnp.concatenate([latent_weight[None], latent_1], axis=0), [0, QUAD]
-    middle = pieces == 4
-    if not middle:
+    split = down_1.shape[0] // 2
+    down_3 = [swapped(piece, 2) for piece in (down_1[:split], down_1[split:])]
+    if middle:
+        cut = swapped(after(jnp.concatenate([sent, latent_1], axis=0), arrived), 2 * QUAD)
+    else:
+        held, codes = jnp.concatenate([latent_weight[None], latent_1], axis=0), [0, QUAD]
         for level in range(3, rank_count.bit_length() - 1):
             held = jnp.concatenate([held, swapped(held, 1 << level)], axis=0)
             codes = codes + [code ^ (1 << level) for code in codes]
-    cut = held
-    if middle:
-        cut = lax.ppermute(held, "dp", [(low, low ^ 12) for low in range(QUAD, 3 * QUAD)])
 
     weight_in = [gate_up, gate_1, gate_2, gate_3]
     theirs = gate_up_product(meta, arrived, weight_in, 1, jnp.bfloat16)
     ours = gate_up_product(meta, arrived, weight_in, 0, jnp.float32)
-    down_3 = after(down_3, ours)
-    split = down_3.shape[0] // 2
-    down_2 = [swapped(piece, 1) for piece in (down_3[:split], down_3[split:])]
-    came, ours, cut, *down_2 = together(swapped(theirs, QUAD), ours, cut, *down_2)
-    down_2 = jnp.concatenate(down_2, axis=0)
+    if middle:
+        ours, cut = together(ours, cut)
+    down_3 = [after(piece, ours) for piece in down_3]
+    down_2 = [swapped(piece, 1) for piece in down_3]
+    came, *down_2 = together(swapped(theirs, QUAD), *down_2)
     summed = ours + came.astype(jnp.float32)
     hidden = (jax.nn.silu(summed[:, :hidden_units]) * summed[:, hidden_units:]).astype(jnp.bfloat16)
 
-    held = after(held, hidden)
-    latent_parts, latent_codes = [held, swapped(held, 2)], [codes, [code ^ 2 for code in codes]]
     partner = swapped(hidden, QUAD)
-    forward = cut
     if middle:
-        forward = lax.ppermute(
-            cut, "dp", [(low, low ^ QUAD) for low in range(QUAD, 3 * QUAD)]
-        )
-
-    weight_out = [down_weight, down_1, down_2, down_3]
+        mixed = jnp.concatenate([latent_1, cut], axis=0)
+        swap = lax.ppermute(mixed, "groups", [(0, 1), (1, 0)])
+    weight_out = [down_weight, down_1, *down_2, *down_3]
     (made_own,) = down_product(meta, hidden, weight_out, experts, True)
     halves = [[GROUP * e + low for e in range(experts)] for low in range(GROUP)]
     near = lax.all_to_all(made_own, "dp", 0, 0, axis_index_groups=halves, tiled=True)
-    partner, forward = together(partner, forward)
+    if middle:
+        partner, swap = together(partner, swap)
     partner = after(partner, made_own)
     made = down_product(meta, partner, weight_out, experts, False)
     far = [swapped(made[n], QUAD * (2 * n + 1)) for n in range(experts)]
     if middle:
-        inner = (rank >> 2 & 1) != (rank >> 3 & 1)
-        part = after(jnp.where(inner, cut[::-1], forward), partner)
-        latent_parts += [part, swapped(part, 2)]
-        latent_codes += [[8, 12], [8 ^ 2, 12 ^ 2]]
-    moe_out = unpack(meta, expert_ids, gate_weights, near, far, width)
+        full = jnp.where(
+            first_group,
+            jnp.concatenate([mixed, swap], axis=1),
+            jnp.concatenate([swap, mixed], axis=1),
+        )
+        held = [jnp.concatenate([latent_weight[None], full[:1]], axis=0), full[1:]]
+        codes = [[0, 4], [8, 12]]
+    else:
+        held, codes = [held], [codes]
+    held = [after(block, partner) for block in held]
+    latent_parts = held + [swapped(block, 2) for block in held]
+    latent_codes = codes + [[code ^ 2 for code in group] for group in codes]
     given, kept = latent_sums(meta, mine, other, latent_parts, latent_codes)
-    projected = kept + swapped(given, 1).astype(jnp.float32)
+    whose = (meta, lengths, expert_ids, gate_weights)
+    moe_out = unpack(*whose, [near], width, True)
+    projected = kept + swapped(after(given, moe_out), 1).astype(jnp.float32)
     latent_cache = latent_finish(projected, latent_gain, length)
+    moe_out = unpack(*whose, far, width, False, [moe_out])
     return (latent_cache, moe_out)
 
 

time: 269 us -> 260 us (0.967)
  Pallas kernels: 64.6 us -> 59.9 us
  starting transfers between devices: 32.2 us -> 27.7 us
    ppermute x2 -> x1, starting transfers between devices: 7.19 us -> 1.49 us  [shards(): swap = lax.ppermute(mixed, 'groups', [(0, 1), (1, 0)])]
    ppermute x16 -> x18, waiting for transfers between devices: 127 us -> 130 us  [swapped(): lax.ppermute(block, 'dp', [(low, low ^ bits) for low in range(count)])]
    pallas_call x4 -> x5, Pallas kernels: 32.5 us -> 30.1 us  [the longest x2 12.9 us: down_product(): pl.pallas_call(functools.partial(down_body, places, joined), grid_spec=pl...]
    unnamed x46 -> x42, local copies, waits for them, and re-layouts: 17 us -> 15.3 us
    ppermute x16 -> x18, starting transfers between devices: 14.7 us -> 15.9 us  [swapped(): lax.ppermute(block, 'dp', [(low, low ^ bits) for low in range(count)])]
  transfers between devices with their start and end apart: 20 -> 21, of which waited for: 11 -> 13; matrix products, arithmetic and copies ran while one was open for 9% -> 9% of each run, Pallas kernels for 24% -> 23%
where the time goes in v4:
time: 260 us; the launch traced here: 259 us
  waiting for transfers between devices  133 us (51%)
  Pallas kernels  59.9 us (23%)
  local copies, waits for them, and re-layouts  30.1 us (12%)
  starting transfers between devices  27.7 us (11%)
  other arithmetic  8.02 us (3%)
    ppermute x18, waiting for transfers between devices, swapped(): lax.ppermute(block, 'dp', [(low, low ^ bits) for low in range(count)])  130 us
    pallas_call x2, Pallas kernels, gate_up_product(): pl.pallas_call(functools.partial(gate_up_body, count), grid_spec=pltpu.Pr...  17.3 us
    ppermute x18, starting transfers between devices, swapped(): lax.ppermute(block, 'dp', [(low, low ^ bits) for low in range(count)])  15.9 us
    unnamed x42, local copies, waits for them, and re-layouts  15.3 us
    pallas_call x2, Pallas kernels, down_product(): pl.pallas_call(functools.partial(down_body, places, joined), grid_spec=pl...  12.9 us
    pallas_call x2, Pallas kernels, unpack(): pl.pallas_call(functools.partial(unpack_body, near), grid_spec=pltpu.Pref...  10.8 us
    pallas_call x1, Pallas kernels, core_split(): pl.pallas_call(core_split_body, grid_spec=pltpu.PrefetchScalarGridSpec(nu...  7.03 us
    pallas_call x1, Pallas kernels, pack(): pl.pallas_call(pack_body, grid_spec=pltpu.PrefetchScalarGridSpec(num_scal...  6.33 us
  transfers between devices with their start and end apart: 21, of which 13 were waited for; matrix products, arithmetic and copies ran while one was open for 9% of the time, Pallas kernels for 23%

profile of v4, /device:TPU:8, one launch (start us, length us, event | category | flops | bytes accessed | tf_op | source)
XLA Modules:
  0.0 259.1 jit_solution(11793745460104371913)
XLA Ops:
  3.7 6.3 %pack_rows.1.refs_0_ = bf16[4,136,3584]{2,1,0:T(8,128)(2,1)} custom-call(s32[1]{0:T(128)} %bitcast.1.meta_ref.rank_ref, s32[16]{0:T(128)} %lengths_ref.5, s32[1,256]{1,0:T(1,128)} %bitcast.8, bf16[256,7168]{1,0:T(8,128)(2,1)} %high_ref.1, bf16[256,7168]{1,0:T(8,128)(2,1)} %high_ref.1), custom_call_target="tpu_custom_call" | custom-call | flops 1879048192 | bytes 7340032 | tf_op jit(solution)/shard_map/pack_rows/pallas_call | solution.py:81
  12.3 5.3 %all-to-all-start = ((bf16[4,136,3584]{2,1,0:T(8,128)(2,1)}), bf16[4,136,3584]{2,1,0:T(8,128)(2,1)}, u32[]{:S(2)}, u32[]{:S(2)}) async-start(bf16[4,136,3584]{2,1,0:T(8,128)(2,1)} %after.9), calls=%async_computation | async-start | bytes 7798784 | tf_op jit(solution)/shard_map/all_to_all | solution.py:484
  17.6 7.0 %core_split.1 = (bf16[8,256,448]{2,1,0:T(8,128)(2,1)}, bf16[8,256,448]{2,1,0:T(8,128)(2,1)}) custom-call(s32[1]{0:T(128)} %bitcast.1.meta_ref.rank_ref, bf16[256,7168]{1,0:T(8,128)(2,1)} %high_ref.1), custom_call_target="tpu_custom_call" | custom-call | tf_op jit(solution)/shard_map/core_split/pallas_call | solution.py:432
  24.6 3.3 %copy.37 = bf16[8,256,448]{1,2,0:T(8,128)(2,1)S(1)} copy(bf16[8,256,448]{2,1,0:T(8,128)(2,1)} %get-tuple-element.22) | data formatting | bytes 3670016 | tf_op jit(solution)/shard_map/core_split/pallas_call | solution.py:432
  28.5 5.2 %collective-permute-done.1 = bf16[8,256,448]{1,2,0:T(8,128)(2,1)} collective-permute-done((bf16[8,256,448]{1,2,0:T(8,128)(2,1)S(1)}, bf16[8,256,448]{1,2,0:T(8,128)(2,1)}, u32[]{:S(2)}, u32[]{:S(2)}) %collective-permute-start.1) | collective-permute-done | bytes 1835040 | tf_op jit(solution)/shard_map/ppermute | solution.py:19
  33.7 3.8 %copy.38.refs_2_ = bf16[8,256,448]{2,1,0:T(8,128)(2,1)} copy(bf16[8,256,448]{1,2,0:T(8,128)(2,1)} %collective-permute-done.1) | data formatting | bytes 3670016 | tf_op jit(solution)/shard_map/ppermute | solution.py:19
  37.5 44.6 %collective-permute-done.refs_0_ = bf16[896,2048]{1,0:T(8,128)(2,1)} collective-permute-done((bf16[896,2048]{1,0:T(8,128)(2,1)}, bf16[896,2048]{1,0:T(8,128)(2,1)}, u32[]{:S(2)}, u32[]{:S(2)}) %collective-permute-start) | collective-permute-done | bytes 3670048 | tf_op jit(solution)/shard_map/ppermute | solution.py:19
  82.6 8.4 %collective-permute-done.7.refs_0_ = bf16[1024,896]{1,0:T(8,128)(2,1)S(1)} collective-permute-done((bf16[1024,896]{1,0:T(8,128)(2,1)}, bf16[1024,896]{1,0:T(8,128)(2,1)S(1)}, u32[]{:S(2)}, u32[]{:S(2)}) %collective-permute-start.7) | collective-permute-done | bytes 1835040 | tf_op jit(solution)/shard_map/ppermute | solution.py:19
  92.3 2.9 %fusion.8 = (bf16[512,896]{1,0:T(8,128)(2,1)}, bf16[512,896]{1,0:T(8,128)(2,1)}) fusion(bf16[1024,896]{1,0:T(8,128)(2,1)} %after.11.refs_1_), kind=kLoop, calls=%fused_computation.26 | loop fusion | bytes 3670016 | tf_op jit(solution)/shard_map/slice | solution.py:490
  100.4 3.4 %collective-permute-start.5 = (bf16[2,224,576]{2,1,0:T(8,128)(2,1)}, bf16[2,224,576]{2,1,0:T(8,128)(2,1)}, u32[]{:S(2)}, u32[]{:S(2)}) collective-permute-start(bf16[2,224,576]{2,1,0:T(8,128)(2,1)} %after.10), channel_id=1, source_target_pairs={{0,8},{1,9},{2,10},{3,11},{4,12},{5,13},{6,14},{7,15},{8,0},{9,1},... | collective-permute-start | bytes 1548296 | tf_op jit(solution)/shard_map/ppermute | solution.py:19
  105.8 8.6 %gate_up_product.3 = bf16[272,2048]{1,0:T(8,128)(2,1)S(1)} custom-call(s32[1]{0:T(128)} %bitcast.1.meta_ref.rank_ref, bf16[4,136,3584]{2,1,0:T(8,128)(2,1)} %get-tuple-element.26.refs_0_.refs_1_, bf16[4,136,3584]{2,1,0:T(8,128)(2,1)} %get-tuple-element.26.refs_0_.refs_1_, bf16[896,2048]{1,0:T(8,128)(2,1)S(1)} %copy-done.3, ...), custom_call_target="tpu_custom_call" | custom-call | flops 3992977408 | bytes 16629760 | tf_op jit(solution)/shard_map/gate_up_product/pallas_call | solution.py:231
  114.5 8.7 %gate_up_product.2.refs_0_ = f32[272,2048]{1,0:T(8,128)S(1)} custom-call(s32[1]{0:T(128)} %bitcast.1.meta_ref.rank_ref, bf16[4,136,3584]{2,1,0:T(8,128)(2,1)} %get-tuple-element.26.refs_0_.refs_1_, bf16[4,136,3584]{2,1,0:T(8,128)(2,1)} %get-tuple-element.26.refs_0_.refs_1_, bf16[896,2048]{1,0:T(8,128)(2,1)S(1)} %copy-done.3, ...), custom_call_target="tpu_custom_call" | custom-call | flops 3992977408 | bytes 16629760 | tf_op jit(solution)/shard_map/gate_up_product/pallas_call | solution.py:231
  127.6 10.1 %collective-permute-done.10.refs_0_ = bf16[512,896]{1,0:T(8,128)(2,1)S(1)} collective-permute-done((bf16[512,896]{1,0:T(8,128)(2,1)}, bf16[512,896]{1,0:T(8,128)(2,1)S(1)}, u32[]{:S(2)}, u32[]{:S(2)}) %collective-permute-start.10) | collective-permute-done | bytes 917536 | tf_op jit(solution)/shard_map/ppermute | solution.py:19
  142.9 6.7 %collective-permute-done.6.refs_0_ = bf16[272,2048]{1,0:T(8,128)(2,1)} collective-permute-done((bf16[272,2048]{1,0:T(8,128)(2,1)S(1)}, bf16[272,2048]{1,0:T(8,128)(2,1)}, u32[]{:S(2)}, u32[]{:S(2)}) %collective-permute-start.6) | collective-permute-done | bytes 1114144 | tf_op jit(solution)/shard_map/ppermute | solution.py:19
  154.3 6.4 %down_product.2.refs_1_ = bf16[2,136,3584]{2,1,0:T(8,128)(2,1)} custom-call(s32[1]{0:T(128)} %bitcast.1.meta_ref.rank_ref, bf16[272,1024]{1,0:T(8,128)(2,1)} %copy-done.16, bf16[1024,896]{1,0:T(8,128)(2,1)} %refs_0_.3, bf16[1024,896]{1,0:T(8,128)(2,1)} %after.11.refs_1_, bf16[512,896]{1,0:T(8,128)(2,1)} %get-tuple-element.34.refs_2_, ...), custom_call_target="tpu_custom_call" | custom-call | flops 1996488704 | bytes 9846784 | tf_op jit(solution)/shard_map/down_product/pallas_call | solution.py:301
  160.7 5.0 %all-to-all-start.1 = ((bf16[2,136,3584]{2,1,0:T(8,128)(2,1)}), bf16[2,136,3584]{2,1,0:T(8,128)(2,1)}, u32[]{:S(2)}, u32[]{:S(2)}) async-start(bf16[2,136,3584]{2,1,0:T(8,128)(2,1)} %down_product.2.refs_1_), calls=%async_computation.1 | async-start | bytes 3899392 | tf_op jit(solution)/shard_map/all_to_all | solution.py:517
  175.4 6.5 %down_product.3 = (bf16[136,3584]{1,0:T(8,128)(2,1)}, bf16[136,3584]{1,0:T(8,128)(2,1)}) custom-call(s32[1]{0:T(128)} %bitcast.1.meta_ref.rank_ref, bf16[272,1024]{1,0:T(8,128)(2,1)} %after.14.refs_1_.hidden_ref, bf16[1024,896]{1,0:T(8,128)(2,1)} %refs_0_.3, bf16[1024,896]{1,0:T(8,128)(2,1)} %after.11.refs_1_, bf16[512,896]{1,0:T(8,128)(2,1)} %get-tuple-element.34.refs_2_, ...), custom_call_target="tpu_custom_call" | custom-call | flops 1996488704 | bytes 9846784 | tf_op jit(solution)/shard_map/down_product/pallas_call | solution.py:301
  184.9 17.0 %collective-permute-done.14.refs_2_ = bf16[2,448,576]{2,1,0:T(8,128)(2,1)} collective-permute-done((bf16[2,448,576]{2,1,0:T(8,128)(2,1)}, bf16[2,448,576]{2,1,0:T(8,128)(2,1)}, u32[]{:S(2)}, u32[]{:S(2)}) %collective-permute-start.14) | collective-permute-done | bytes 1032224 | tf_op jit(solution)/shard_map/ppermute | solution.py:19
  201.9 22.5 %collective-permute-done.15.refs_3_ = bf16[2,448,576]{2,1,0:T(8,128)(2,1)} collective-permute-done((bf16[2,448,576]{2,1,0:T(8,128)(2,1)}, bf16[2,448,576]{2,1,0:T(8,128)(2,1)}, u32[]{:S(2)}, u32[]{:S(2)}) %collective-permute-start.15) | collective-permute-done | bytes 1032224 | tf_op jit(solution)/shard_map/ppermute | solution.py:19
  227.2 5.5 %latent_product.1 = (bf16[256,576]{1,0:T(8,128)(2,1)S(1)}, f32[256,576]{1,0:T(8,128)S(1)}) custom-call(s32[1]{0:T(128)} %bitcast.1.meta_ref.rank_ref, bf16[8,256,448]{2,1,0:T(8,128)(2,1)S(1)} %copy-done.6, bf16[8,256,448]{2,1,0:T(8,128)(2,1)S(1)} %copy-done.2, bf16[2,448,576]{2,1,0:T(8,128)(2,1)S(1)} %copy-done.5, bf16[2,448,576]{2,1,0:T(8,128)(2,1)S(1)} %copy-done.4, ...), custom_call_target="tpu_custom_call" | custom-call | flops 2113929216 | bytes 7798784 | tf_op jit(solution)/shard_map/latent_product/pallas_call | solution.py:378
  234.3 5.4 %unpack_rows.2.refs_1_.refs_2_ = bf16[256,7168]{1,0:T(8,128)(2,1)} custom-call(s32[1]{0:T(128)} %bitcast.1.meta_ref.rank_ref, s32[16]{0:T(128)} %lengths_ref.5, s32[1,256]{1,0:T(1,128)} %bitcast.9, f32[1,256]{1,0:T(1,128)} %bitcast.11, bf16[2,136,3584]{2,1,0:T(8,128)(2,1)} %all-to-all-done.1.refs_0_), custom_call_target="tpu_custom_call" | custom-call | flops 939524096 | bytes 3670016 | tf_op jit(solution)/shard_map/unpack_rows/pallas_call | solution.py:143
  240.4 3.9 %collective-permute-done.17.refs_0_ = bf16[136,3584]{1,0:T(8,128)(2,1)} collective-permute-done((bf16[136,3584]{1,0:T(8,128)(2,1)}, bf16[136,3584]{1,0:T(8,128)(2,1)}, u32[]{:S(2)}, u32[]{:S(2)}) %collective-permute-start.17) | collective-permute-done | bytes 974880 | tf_op jit(solution)/shard_map/ppermute | solution.py:19
  244.2 7.5 %collective-permute-done.18.refs_1_ = bf16[136,3584]{1,0:T(8,128)(2,1)} collective-permute-done((bf16[136,3584]{1,0:T(8,128)(2,1)}, bf16[136,3584]{1,0:T(8,128)(2,1)}, u32[]{:S(2)}, u32[]{:S(2)}) %collective-permute-start.18) | collective-permute-done | bytes 974880 | tf_op jit(solution)/shard_map/ppermute | solution.py:19
  251.7 5.5 %unpack_rows.3 = bf16[256,7168]{1,0:T(8,128)(2,1)} custom-call(s32[1]{0:T(128)} %bitcast.1.meta_ref.rank_ref, s32[16]{0:T(128)} %lengths_ref.5, s32[1,256]{1,0:T(1,128)} %bitcast.10, f32[1,256]{1,0:T(1,128)} %bitcast.12, bf16[136,3584]{1,0:T(8,128)(2,1)} %collective-permute-done.17.refs_0_, ...), custom_call_target="tpu_custom_call", output_to_operand_aliasing={{}: (6, {})} | custom-call | flops 939524096 | bytes 3670016 | tf_op jit(solution)/shard_map/unpack_rows/pallas_call | solution.py:143
  (105 shorter events, 48.9 us)
Async XLA Ops:
  0.6 81.5 %collective-permute-start = (bf16[896,2048]{1,0:T(8,128)(2,1)}, bf16[896,2048]{1,0:T(8,128)(2,1)}, u32[]{:S(2)}, u32[]{:S(2)}) collective-permute-start(bf16[896,2048]{1,0:T(8,128)(2,1)} %refs_2_.3), channel_id=1, source_target_pairs={{0,2},{1,3},{2,0},{3,1},{4,6},{5,7},{6,4},{7,5},{8,10},{9,11},{10,... | collective-permute-start | bytes 11010056 | tf_op jit(solution)/shard_map/ppermute | solution.py:19
  3.2 8.4 %collective-permute-start.2 = (bf16[1,224,576]{2,1,0:T(8,128)(2,1)S(1)}, bf16[1,224,576]{2,1,0:T(8,128)(2,1)S(1)}, u32[]{:S(2)}, u32[]{:S(2)}) collective-permute-start(bf16[1,224,576]{2,1,0:T(8,128)(2,1)S(1)} %dynamic-slice_bitcast_fusion), channel_id=1, source_target_pairs={{0,4},{1,5},{2,6},{3,7},{4,0},{5,1},{6,2},{7,3},{8,12},{9,13},{10,... | collective-permute-start | bytes 774152 | tf_op jit(solution)/shard_map/ppermute | solution.py:19
  12.3 88.1 %all-to-all-start = ((bf16[4,136,3584]{2,1,0:T(8,128)(2,1)}), bf16[4,136,3584]{2,1,0:T(8,128)(2,1)}, u32[]{:S(2)}, u32[]{:S(2)}) async-start(bf16[4,136,3584]{2,1,0:T(8,128)(2,1)} %after.9), calls=%async_computation | async-start | bytes 7798784 | tf_op jit(solution)/shard_map/all_to_all | solution.py:484
  27.9 5.8 %collective-permute-start.1 = (bf16[8,256,448]{1,2,0:T(8,128)(2,1)S(1)}, bf16[8,256,448]{1,2,0:T(8,128)(2,1)}, u32[]{:S(2)}, u32[]{:S(2)}) collective-permute-start(bf16[8,256,448]{1,2,0:T(8,128)(2,1)S(1)} %copy.37), channel_id=1, source_target_pairs={{0,1},{1,0},{2,3},{3,2},{4,5},{5,4},{6,7},{7,6},{8,9},{9,8},{10,11... | collective-permute-start | bytes 5505032 | tf_op jit(solution)/shard_map/ppermute | solution.py:19
  28.0 70.2 %collective-permute-start.3 = (bf16[896,2048]{1,0:T(8,128)(2,1)}, bf16[896,2048]{1,0:T(8,128)(2,1)}, u32[]{:S(2)}, u32[]{:S(2)}) collective-permute-start(bf16[896,2048]{1,0:T(8,128)(2,1)} %refs_2_.3), channel_id=1, source_target_pairs={{0,1},{1,0},{2,3},{3,2},{4,5},{5,4},{6,7},{7,6},{8,9},{9,8},{10,11... | collective-permute-start | bytes 11010056 | tf_op jit(solution)/shard_map/ppermute | solution.py:19
  82.1 18.3 %collective-permute-start.4 = (bf16[896,2048]{1,0:T(8,128)(2,1)}, bf16[896,2048]{1,0:T(8,128)(2,1)}, u32[]{:S(2)}, u32[]{:S(2)}) collective-permute-start(bf16[896,2048]{1,0:T(8,128)(2,1)} %get-tuple-element.25.refs_4_.refs_1_), channel_id=1, source_target_pairs={{0,1},{1,0},{2,3},{3,2},{4,5},{5,4},{6,7},{7,6},{8,9},{9,8},{10,11... | collective-permute-start | bytes 11010056 | tf_op jit(solution)/shard_map/ppermute | solution.py:19
  82.1 8.9 %collective-permute-start.7 = (bf16[1024,896]{1,0:T(8,128)(2,1)}, bf16[1024,896]{1,0:T(8,128)(2,1)S(1)}, u32[]{:S(2)}, u32[]{:S(2)}) collective-permute-start(bf16[1024,896]{1,0:T(8,128)(2,1)} %refs_0_.3), channel_id=1, source_target_pairs={{0,1},{1,0},{2,3},{3,2},{4,5},{5,4},{6,7},{7,6},{8,9},{9,8},{10,11... | collective-permute-start | bytes 5505032 | tf_op jit(solution)/shard_map/ppermute | solution.py:19
  95.2 31.5 %collective-permute-start.8 = (bf16[512,896]{1,0:T(8,128)(2,1)}, bf16[512,896]{1,0:T(8,128)(2,1)S(1)}, u32[]{:S(2)}, u32[]{:S(2)}) collective-permute-start(bf16[512,896]{1,0:T(8,128)(2,1)} %get-tuple-element.47), channel_id=1, source_target_pairs={{0,2},{1,3},{2,0},{3,1},{4,6},{5,7},{6,4},{7,5},{8,10},{9,11},{10,... | collective-permute-start | bytes 2752520 | tf_op jit(solution)/shard_map/ppermute | solution.py:19
  96.7 41.0 %collective-permute-start.10 = (bf16[512,896]{1,0:T(8,128)(2,1)}, bf16[512,896]{1,0:T(8,128)(2,1)S(1)}, u32[]{:S(2)}, u32[]{:S(2)}) collective-permute-start(bf16[512,896]{1,0:T(8,128)(2,1)} %get-tuple-element.46), channel_id=1, source_target_pairs={{0,2},{1,3},{2,0},{3,1},{4,6},{5,7},{6,4},{7,5},{8,10},{9,11},{10,... | collective-permute-start | bytes 2752520 | tf_op jit(solution)/shard_map/ppermute | solution.py:19
  100.4 26.3 %collective-permute-start.5 = (bf16[2,224,576]{2,1,0:T(8,128)(2,1)}, bf16[2,224,576]{2,1,0:T(8,128)(2,1)}, u32[]{:S(2)}, u32[]{:S(2)}) collective-permute-start(bf16[2,224,576]{2,1,0:T(8,128)(2,1)} %after.10), channel_id=1, source_target_pairs={{0,8},{1,9},{2,10},{3,11},{4,12},{5,13},{6,14},{7,15},{8,0},{9,1},... | collective-permute-start | bytes 1548296 | tf_op jit(solution)/shard_map/ppermute | solution.py:19
  114.4 35.3 %collective-permute-start.6 = (bf16[272,2048]{1,0:T(8,128)(2,1)S(1)}, bf16[272,2048]{1,0:T(8,128)(2,1)}, u32[]{:S(2)}, u32[]{:S(2)}) collective-permute-start(bf16[272,2048]{1,0:T(8,128)(2,1)S(1)} %gate_up_product.3), channel_id=1, source_target_pairs={{0,4},{1,5},{2,6},{3,7},{4,0},{5,1},{6,2},{7,3},{8,12},{9,13},{10,... | collective-permute-start | bytes 3342344 | tf_op jit(solution)/shard_map/ppermute | solution.py:19
  127.6 22.1 %collective-permute-start.9 = (bf16[512,896]{1,0:T(8,128)(2,1)}, bf16[512,896]{1,0:T(8,128)(2,1)}, u32[]{:S(2)}, u32[]{:S(2)}) collective-permute-start(bf16[512,896]{1,0:T(8,128)(2,1)} %after.12.refs_4_), channel_id=1, source_target_pairs={{0,1},{1,0},{2,3},{3,2},{4,5},{5,4},{6,7},{7,6},{8,9},{9,8},{10,11... | collective-permute-start | bytes 2752520 | tf_op jit(solution)/shard_map/ppermute | solution.py:19
  138.6 11.1 %collective-permute-start.11 = (bf16[512,896]{1,0:T(8,128)(2,1)}, bf16[512,896]{1,0:T(8,128)(2,1)}, u32[]{:S(2)}, u32[]{:S(2)}) collective-permute-start(bf16[512,896]{1,0:T(8,128)(2,1)} %after.13.refs_5_), channel_id=1, source_target_pairs={{0,1},{1,0},{2,3},{3,2},{4,5},{5,4},{6,7},{7,6},{8,9},{9,8},{10,11... | collective-permute-start | bytes 2752520 | tf_op jit(solution)/shard_map/ppermute | solution.py:19
  141.5 24.3 %collective-permute-start.13 = (bf16[3,224,576]{2,1,0:T(8,128)(2,1)}, bf16[3,224,576]{2,1,0:T(8,128)(2,1)}, u32[]{:S(2)}, u32[]{:S(2)}) collective-permute-start(bf16[3,224,576]{2,1,0:T(8,128)(2,1)} %constant_dynamic-update-slice_fusion), channel_id=1, source_target_pairs={{0,16},{16,0},{1,17},{17,1},{2,18},{18,2},{3,19},{19,3},{4,20},{20... | collective-permute-start | bytes 2322440 | tf_op jit(solution)/shard_map/ppermute | solution.py:513
  151.6 15.0 %collective-permute-start.12 = (bf16[272,1024]{1,0:T(8,128)(2,1)S(1)}, bf16[272,1024]{1,0:T(8,128)(2,1)S(1)}, u32[]{:S(2)}, u32[]{:S(2)}) collective-permute-start(bf16[272,1024]{1,0:T(8,128)(2,1)S(1)} %fusion.hidden_ref), channel_id=1, source_target_pairs={{0,4},{1,5},{2,6},{3,7},{4,0},{5,1},{6,2},{7,3},{8,12},{9,13},{10,... | collective-permute-start | bytes 1671176 | tf_op jit(solution)/shard_map/ppermute | solution.py:19
  160.7 73.6 %all-to-all-start.1 = ((bf16[2,136,3584]{2,1,0:T(8,128)(2,1)}), bf16[2,136,3584]{2,1,0:T(8,128)(2,1)}, u32[]{:S(2)}, u32[]{:S(2)}) async-start(bf16[2,136,3584]{2,1,0:T(8,128)(2,1)} %down_product.2.refs_1_), calls=%async_computation.1 | async-start | bytes 3899392 | tf_op jit(solution)/shard_map/all_to_all | solution.py:517
  173.3 51.1 %copy-start.2 = (bf16[8,256,448]{2,1,0:T(8,128)(2,1)S(1)}, bf16[8,256,448]{2,1,0:T(8,128)(2,1)}, u32[]{:S(2)}) copy-start(bf16[8,256,448]{2,1,0:T(8,128)(2,1)} %get-tuple-element.24.other_ref) | copy-start | bytes 5505028
  173.3 51.1 %copy-start.4 = (bf16[2,448,576]{2,1,0:T(8,128)(2,1)S(1)}, bf16[2,448,576]{2,1,0:T(8,128)(2,1)}, u32[]{:S(2)}) copy-start(bf16[2,448,576]{2,1,0:T(8,128)(2,1)} %after.16.refs_1_) | copy-start | bytes 3096580
  173.3 28.6 %collective-permute-start.14 = (bf16[2,448,576]{2,1,0:T(8,128)(2,1)}, bf16[2,448,576]{2,1,0:T(8,128)(2,1)}, u32[]{:S(2)}, u32[]{:S(2)}) collective-permute-start(bf16[2,448,576]{2,1,0:T(8,128)(2,1)} %after.15.refs_0_), channel_id=1, source_target_pairs={{0,2},{1,3},{2,0},{3,1},{4,6},{5,7},{6,4},{7,5},{8,10},{9,11},{10,... | collective-permute-start | bytes 3096584 | tf_op jit(solution)/shard_map/ppermute | solution.py:19
  173.8 50.5 %collective-permute-start.15 = (bf16[2,448,576]{2,1,0:T(8,128)(2,1)}, bf16[2,448,576]{2,1,0:T(8,128)(2,1)}, u32[]{:S(2)}, u32[]{:S(2)}) collective-permute-start(bf16[2,448,576]{2,1,0:T(8,128)(2,1)} %after.16.refs_1_), channel_id=1, source_target_pairs={{0,2},{1,3},{2,0},{3,1},{4,6},{5,7},{6,4},{7,5},{8,10},{9,11},{10,... | collective-permute-start | bytes 3096584 | tf_op jit(solution)/shard_map/ppermute | solution.py:19
  181.8 62.4 %collective-permute-start.17 = (bf16[136,3584]{1,0:T(8,128)(2,1)}, bf16[136,3584]{1,0:T(8,128)(2,1)}, u32[]{:S(2)}, u32[]{:S(2)}) collective-permute-start(bf16[136,3584]{1,0:T(8,128)(2,1)} %get-tuple-element.38), channel_id=1, source_target_pairs={{0,4},{1,5},{2,6},{3,7},{4,0},{5,1},{6,2},{7,3},{8,12},{9,13},{10,... | collective-permute-start | bytes 2924552 | tf_op jit(solution)/shard_map/ppermute | solution.py:19
  183.6 68.1 %collective-permute-start.18 = (bf16[136,3584]{1,0:T(8,128)(2,1)}, bf16[136,3584]{1,0:T(8,128)(2,1)}, u32[]{:S(2)}, u32[]{:S(2)}) collective-permute-start(bf16[136,3584]{1,0:T(8,128)(2,1)} %get-tuple-element.39), channel_id=1, source_target_pairs={{0,12},{1,13},{2,14},{3,15},{4,8},{5,9},{6,10},{7,11},{8,4},{9,5},... | collective-permute-start | bytes 2924552 | tf_op jit(solution)/shard_map/ppermute | solution.py:19
  239.7 17.5 %collective-permute-start.16 = (bf16[256,576]{1,0:T(8,128)(2,1)}, bf16[256,576]{1,0:T(8,128)(2,1)S(1)}, u32[]{:S(2)}, u32[]{:S(2)}) collective-permute-start(bf16[256,576]{1,0:T(8,128)(2,1)} %after.17), channel_id=1, source_target_pairs={{0,1},{1,0},{2,3},{3,2},{4,5},{5,4},{6,7},{7,6},{8,9},{9,8},{10,11... | collective-permute-start | bytes 884744 | tf_op jit(solution)/shard_map/ppermute | solution.py:19
  240.4 16.8 %copy-start.8 = (f32[256,576]{1,0:T(8,128)S(1)}, f32[256,576]{1,0:T(8,128)}, u32[]{:S(2)}) copy-start(f32[256,576]{1,0:T(8,128)} %copy-done.7) | copy-start | bytes 1769476
  (17 other events, 43.4 us)

commit v5 on v4

--- a/solution.py
+++ b/solution.py
@@ -118,9 +118,9 @@
 
     total = jnp.zeros(out_ref.shape, jnp.float32)
     for number in range(experts):
-        part = refs[0][number] if near else refs[number][...]
-        picks = picks_ref[number if near else my_expert ^ number]
-        total += jnp.dot(picks, part, preferred_element_type=jnp.float32)
+        expert = my_expert ^ number
+        part = refs[1][expert] if near and number else refs[number][...]
+        total += jnp.dot(picks_ref[expert], part, preferred_element_type=jnp.float32)
     out_ref[...] = (total * gate_column_ref[...]).astype(jnp.bfloat16)
 
 
@@ -128,7 +128,7 @@
     rows = ids.shape[0]
     part = width // GROUP
     size = parts[0].shape[-2]
-    experts = parts[0].shape[0] if near else len(parts)
+    experts = parts[1].shape[0] if near else len(parts)
 
     def out_index(k, rank_ref, lengths_ref):
         quarter = rank_ref[0] % QUAD
@@ -136,10 +136,10 @@
         return (0, (high if near else 1 - high) * QUAD + (quarter ^ k))
 
     whole = lambda k, rank_ref, lengths_ref: (0, 0)
+    specs = [pl.BlockSpec((size, part), lambda k, rank_ref, lengths_ref: (0, k))] * experts
     if near:
-        specs = [pl.BlockSpec((experts, size, part), lambda k, rank_ref, lengths_ref: (0, 0, k))]
-    else:
-        specs = [pl.BlockSpec((size, part), lambda k, rank_ref, lengths_ref: (0, k))] * experts
+        both = pl.BlockSpec((experts, size, part), lambda k, rank_ref, lengths_ref: (0, 0, k))
+        specs = [specs[0], both]
     return pl.pallas_call(
         functools.partial(unpack_body, near),
         grid_spec=pltpu.PrefetchScalarGridSpec(
@@ -192,9 +192,11 @@
     )(*values)
 
 
-def gate_up_body(count, meta_ref, *refs):
+def gate_up_body(groups, meta_ref, *refs):
     del meta_ref
-    parts, shares, out_ref, joined = refs[:count], refs[count:-2], refs[-2], refs[-1]
+    count = sum(groups)
+    parts, shares = refs[:count], refs[count : count + QUAD]
+    outs, joined = refs[count + QUAD : -1], refs[-1]
     size = parts[0].shape[1]
     depth = shares[0].shape[0]
 
@@ -210,17 +212,19 @@
             shares[k][...],
             preferred_element_type=jnp.float32,
         )
-    out_ref[...] = total.astype(out_ref.dtype)
-
-
-def gate_up_product(meta, arrived, shares, side, dtype):
-    pieces, size, width = arrived.shape
-    count = pieces // 2
-    rows = size * count
+    start = 0
+    for group, out_ref in zip(groups, outs):
+        out_ref[...] = total[start : start + group * size].astype(out_ref.dtype)
+        start += group * size
+
+
+def gate_up_product(meta, arrived, shares, groups):
+    _, size, width = arrived.shape
     depth, columns = shares[0].shape
     tile = columns // 4
-
-    def source(number):
+    rows = size * sum(len(numbers) for numbers, _, _ in groups)
+
+    def source(number, side):
         def index(n, meta_ref):
             rank = meta_ref[0]
             return (2 * ((rank // GROUP) ^ number) + (((rank // QUAD) % 2) ^ side), 0, 0)
@@ -228,17 +232,22 @@
         return index
 
     across = lambda n, meta_ref: (0, n)
-    return pl.pallas_call(
-        functools.partial(gate_up_body, count),
+    picked = [source(number, side) for numbers, side, _ in groups for number in numbers]
+    heights = [size * len(numbers) for numbers, _, _ in groups]
+    return pl.pallas_call(
+        functools.partial(gate_up_body, [len(numbers) for numbers, _, _ in groups]),
         grid_spec=pltpu.PrefetchScalarGridSpec(
             num_scalar_prefetch=1,
             grid=(columns // tile,),
-            in_specs=[pl.BlockSpec((1, size, width), source(number)) for number in range(count)]
+            in_specs=[pl.BlockSpec((1, size, width), index) for index in picked]
             + [pl.BlockSpec((depth, tile), across) for _ in shares],
-            out_specs=pl.BlockSpec((rows, tile), across),
+            out_specs=[pl.BlockSpec((height, tile), across) for height in heights],
             scratch_shapes=[pltpu.VMEM((rows, width), jnp.bfloat16)],
         ),
-        out_shape=jax.ShapeDtypeStruct((rows, columns), dtype),
+        out_shape=[
+            jax.ShapeDtypeStruct((height, columns), dtype)
+            for height, (_, _, dtype) in zip(heights, groups)
+        ],
         compiler_params=pltpu.CompilerParams(vmem_limit_bytes=32 << 20),
         cost_estimate=pl.CostEstimate(
             flops=2 * rows * width * columns,
@@ -246,14 +255,14 @@
             transcendentals=0,
         ),
         name="gate_up_product",
-    )(meta, *[arrived] * count, *shares)
+    )(meta, *[arrived] * len(picked), *shares)
 
 
 def down_body(places, joined, meta_ref, hidden_ref, *refs):
     k = pl.program_id(0)
     weight, done = refs[-2:]
     pieces, outs = refs[: len(places)], refs[len(places) : -2]
-    count = outs[0].shape[0] if joined else len(outs)
+    count = outs[0].shape[0] - 1 if joined else len(outs)
     size = hidden_ref.shape[0] // count
     mine = meta_ref[0] // GROUP
     moves = []
@@ -278,7 +287,7 @@
     for number in range(count):
         rows = made[number * size : (number + 1) * size].astype(jnp.bfloat16)
         if joined:
-            outs[0][mine ^ number] = rows
+            outs[0][mine ^ (number + 1)] = rows
         else:
             outs[number][...] = rows
 
@@ -293,8 +302,8 @@
         filled += share.shape[0]
     whole = lambda k, meta_ref: (0, 0)
     if joined:
-        out_specs = [pl.BlockSpec((count, size, part), lambda k, meta_ref: (0, 0, k))]
-        shapes = [(count, size, QUAD * part)]
+        out_specs = [pl.BlockSpec((count + 1, size, part), lambda k, meta_ref: (0, 0, k))]
+        shapes = [(count + 1, size, QUAD * part)]
     else:
         out_specs = [pl.BlockSpec((size, part), lambda k, meta_ref: (0, k))] * count
         shapes = [(size, QUAD * part)] * count
@@ -486,8 +495,7 @@
         swapped(gate_2, 1),
     )
     down_1 = after(down_1, gate_2)
-    split = down_1.shape[0] // 2
-    down_3 = [swapped(piece, 2) for piece in (down_1[:split], down_1[split:])]
+    down_3 = swapped(down_1, 2)
     if middle:
         cut = swapped(after(jnp.concatenate([sent, latent_1], axis=0), arrived), 2 * QUAD)
     else:
@@ -497,30 +505,46 @@
             codes = codes + [code ^ (1 << level) for code in codes]
 
     weight_in = [gate_up, gate_1, gate_2, gate_3]
-    theirs = gate_up_product(meta, arrived, weight_in, 1, jnp.bfloat16)
-    ours = gate_up_product(meta, arrived, weight_in, 0, jnp.float32)
+    away = list(range(1, experts))
+    (theirs,) = gate_up_product(meta, arrived, weight_in, [(away, 1, jnp.bfloat16)])
+    ours, theirs_near, ours_near = gate_up_product(
+        meta,
+        arrived,
+        weight_in,
+        [(away, 0, jnp.float32), ([0], 1, jnp.bfloat16), ([0], 0, jnp.float32)],
+    )
     if middle:
         ours, cut = together(ours, cut)
-    down_3 = [after(piece, ours) for piece in down_3]
-    down_2 = [swapped(piece, 1) for piece in down_3]
+    down_3 = after(down_3, ours)
+    split = down_3.shape[0] // 4
+    down_2 = [swapped(down_3[n * split : (n + 1) * split], 1) for n in range(4)]
     came, *down_2 = together(swapped(theirs, QUAD), *down_2)
-    summed = ours + came.astype(jnp.float32)
-    hidden = (jax.nn.silu(summed[:, :hidden_units]) * summed[:, hidden_units:]).astype(jnp.bfloat16)
-
+    weight_out = [down_weight, down_1, *down_2, down_3]
+
+    def activated(own, other):
+        summed = own + other.astype(jnp.float32)
+        gate, up = summed[:, :hidden_units], summed[:, hidden_units:]
+        return (jax.nn.silu(gate) * up).astype(jnp.bfloat16)
+
+    hidden = activated(ours, came)
     partner = swapped(hidden, QUAD)
-    if middle:
-        mixed = jnp.concatenate([latent_1, cut], axis=0)
-        swap = lax.ppermute(mixed, "groups", [(0, 1), (1, 0)])
-    weight_out = [down_weight, down_1, *down_2, *down_3]
-    (made_own,) = down_product(meta, hidden, weight_out, experts, True)
+    (made_own,) = down_product(meta, hidden, weight_out, experts - 1, True)
     halves = [[GROUP * e + low for e in range(experts)] for low in range(GROUP)]
     near = lax.all_to_all(made_own, "dp", 0, 0, axis_index_groups=halves, tiled=True)
+    partner = after(partner, made_own)
+    made = down_product(meta, partner, weight_out, experts - 1, False)
+    far = [swapped(made[n - 1], QUAD * (2 * n + 1)) for n in away]
+
+    came_near = after(swapped(after(theirs_near, hidden), QUAD), made[0])
+    hidden_near = activated(ours_near, came_near)
+    both = jnp.concatenate([hidden_near, swapped(hidden_near, QUAD)], axis=0)
+    here, there = down_product(meta, both, weight_out, 2, False)
+    near = [here, near]
+    far = [swapped(there, QUAD)] + far
+
     if middle:
-        partner, swap = together(partner, swap)
-    partner = after(partner, made_own)
-    made = down_product(meta, partner, weight_out, experts, False)
-    far = [swapped(made[n], QUAD * (2 * n + 1)) for n in range(experts)]
-    if middle:
+        mixed = after(jnp.concatenate([latent_1, cut], axis=0), hidden)
+        swap = lax.ppermute(mixed, "groups", [(0, 1), (1, 0)])
         full = jnp.where(
             first_group,
             jnp.concatenate([mixed, swap], axis=1),
@@ -530,12 +554,11 @@
         codes = [[0, 4], [8, 12]]
     else:
         held, codes = [held], [codes]
-    held = [after(block, partner) for block in held]
     latent_parts = held + [swapped(block, 2) for block in held]
     latent_codes = codes + [[code ^ 2 for code in group] for group in codes]
     given, kept = latent_sums(meta, mine, other, latent_parts, latent_codes)
     whose = (meta, lengths, expert_ids, gate_weights)
-    moe_out = unpack(*whose, [near], width, True)
+    moe_out = unpack(*whose, near, width, True)
     projected = kept + swapped(after(given, moe_out), 1).astype(jnp.float32)
     latent_cache = latent_finish(projected, latent_gain, length)
     moe_out = unpack(*whose, far, width, False, [moe_out])

time: 260 us -> 257 us (0.988); the launches traced: 259 us -> 253 us
  waiting for transfers between devices: 133 us -> 121 us
  local copies, waits for them, and re-layouts: 30.1 us -> 24.2 us
  Pallas kernels: 59.9 us -> 65.8 us
  other arithmetic: 8.02 us -> 10.9 us
  starting transfers between devices: 27.7 us -> 30.4 us
    ppermute x18 -> x21, waiting for transfers between devices: 130 us -> 116 us  [swapped(): lax.ppermute(block, 'dp', [(low, low ^ bits) for low in range(count)])]
    pallas_call x2 -> x3, Pallas kernels: 12.9 us -> 17.8 us  [down_product(): pl.pallas_call(functools.partial(down_body, places, joined), grid_spec=pl...]
    concatenate x0 -> x2, other arithmetic: none -> 2.97 us  [the longest x1 2.11 us: shards(): mixed = after(jnp.concatenate([latent_1, cut], axis=0), hidden)]
    ppermute x18 -> x21, starting transfers between devices: 15.9 us -> 18.6 us  [swapped(): lax.ppermute(block, 'dp', [(low, low ^ bits) for low in range(count)])]
    unnamed x42 -> x43, local copies, waits for them, and re-layouts: 15.3 us -> 12.8 us
  transfers between devices with their start and end apart: 21 -> 24, of which waited for: 13 -> 16; matrix products, arithmetic and copies ran while one was open for 9% -> 8% of each run, Pallas kernels for 23% -> 26%
where the time goes in v5:
time: 257 us; the launch traced here: 253 us
  waiting for transfers between devices  121 us (47%)
  Pallas kernels  65.8 us (26%)
  starting transfers between devices  30.4 us (12%)
  local copies, waits for them, and re-layouts  24.2 us (9%)
  other arithmetic  10.9 us (4%)
    ppermute x21, waiting for transfers between devices, swapped(): lax.ppermute(block, 'dp', [(low, low ^ bits) for low in range(count)])  116 us
    ppermute x21, starting transfers between devices, swapped(): lax.ppermute(block, 'dp', [(low, low ^ bits) for low in range(count)])  18.6 us
    pallas_call x2, Pallas kernels, gate_up_product(): pl.pallas_call(functools.partial(gate_up_body, [len(numbers) for numbers,...  18 us
    pallas_call x3, Pallas kernels, down_product(): pl.pallas_call(functools.partial(down_body, places, joined), grid_spec=pl...  17.8 us
    unnamed x43, local copies, waits for them, and re-layouts  12.8 us
    pallas_call x2, Pallas kernels, unpack(): pl.pallas_call(functools.partial(unpack_body, near), grid_spec=pltpu.Pref...  11.1 us
    pallas_call x1, Pallas kernels, core_split(): pl.pallas_call(core_split_body, grid_spec=pltpu.PrefetchScalarGridSpec(nu...  7.06 us
    pallas_call x1, Pallas kernels, pack(): pl.pallas_call(pack_body, grid_spec=pltpu.PrefetchScalarGridSpec(num_scal...  6.28 us
  transfers between devices with their start and end apart: 24, of which 16 were waited for; matrix products, arithmetic and copies ran while one was open for 8% of the time, Pallas kernels for 26%

profile of v5, /device:TPU:8, one launch (start us, length us, event | category | flops | bytes accessed | tf_op | source)
XLA Modules:
  0.0 253.1 jit_solution(8451813387884546083)
XLA Ops:
  3.7 6.3 %pack_rows.1.refs_0_ = bf16[4,136,3584]{2,1,0:T(8,128)(2,1)} custom-call(s32[1]{0:T(128)} %bitcast.1.meta_ref.rank_ref, s32[16]{0:T(128)} %lengths_ref.5, s32[1,256]{1,0:T(1,128)} %bitcast.8, bf16[256,7168]{1,0:T(8,128)(2,1)} %high_ref.1, bf16[256,7168]{1,0:T(8,128)(2,1)} %high_ref.1), custom_call_target="tpu_custom_call" | custom-call | flops 1879048192 | bytes 7340032 | tf_op jit(solution)/shard_map/pack_rows/pallas_call | solution.py:81
  12.3 5.3 %all-to-all-start = ((bf16[4,136,3584]{2,1,0:T(8,128)(2,1)}), bf16[4,136,3584]{2,1,0:T(8,128)(2,1)}, u32[]{:S(2)}, u32[]{:S(2)}) async-start(bf16[4,136,3584]{2,1,0:T(8,128)(2,1)} %after.9), calls=%async_computation | async-start | bytes 7798784 | tf_op jit(solution)/shard_map/all_to_all | solution.py:493
  17.6 7.1 %core_split.1 = (bf16[8,256,448]{2,1,0:T(8,128)(2,1)}, bf16[8,256,448]{2,1,0:T(8,128)(2,1)}) custom-call(s32[1]{0:T(128)} %bitcast.1.meta_ref.rank_ref, bf16[256,7168]{1,0:T(8,128)(2,1)} %high_ref.1), custom_call_target="tpu_custom_call" | custom-call | tf_op jit(solution)/shard_map/core_split/pallas_call | solution.py:441
  24.7 3.3 %copy.37 = bf16[8,256,448]{1,2,0:T(8,128)(2,1)S(1)} copy(bf16[8,256,448]{2,1,0:T(8,128)(2,1)} %get-tuple-element.25) | data formatting | bytes 3670016 | tf_op jit(solution)/shard_map/core_split/pallas_call | solution.py:441
  28.5 5.2 %collective-permute-done.1 = bf16[8,256,448]{1,2,0:T(8,128)(2,1)} collective-permute-done((bf16[8,256,448]{1,2,0:T(8,128)(2,1)S(1)}, bf16[8,256,448]{1,2,0:T(8,128)(2,1)}, u32[]{:S(2)}, u32[]{:S(2)}) %collective-permute-start.1) | collective-permute-done | bytes 1835040 | tf_op jit(solution)/shard_map/ppermute | solution.py:19
  33.7 3.8 %copy.38.refs_2_ = bf16[8,256,448]{2,1,0:T(8,128)(2,1)} copy(bf16[8,256,448]{1,2,0:T(8,128)(2,1)} %collective-permute-done.1) | data formatting | bytes 3670016 | tf_op jit(solution)/shard_map/ppermute | solution.py:19
  37.6 44.5 %collective-permute-done.refs_0_ = bf16[896,2048]{1,0:T(8,128)(2,1)} collective-permute-done((bf16[896,2048]{1,0:T(8,128)(2,1)}, bf16[896,2048]{1,0:T(8,128)(2,1)}, u32[]{:S(2)}, u32[]{:S(2)}) %collective-permute-start) | collective-permute-done | bytes 3670048 | tf_op jit(solution)/shard_map/ppermute | solution.py:19
  82.6 8.4 %collective-permute-done.7.refs_0_ = bf16[1024,896]{1,0:T(8,128)(2,1)S(1)} collective-permute-done((bf16[1024,896]{1,0:T(8,128)(2,1)}, bf16[1024,896]{1,0:T(8,128)(2,1)S(1)}, u32[]{:S(2)}, u32[]{:S(2)}) %collective-permute-start.7) | collective-permute-done | bytes 1835040 | tf_op jit(solution)/shard_map/ppermute | solution.py:19
  95.7 4.6 %all-to-all-done.refs_0_ = bf16[4,136,3584]{2,1,0:T(8,128)(2,1)} async-done(((bf16[4,136,3584]{2,1,0:T(8,128)(2,1)}), bf16[4,136,3584]{2,1,0:T(8,128)(2,1)}, u32[]{:S(2)}, u32[]{:S(2)}) %all-to-all-start) | async-done | bytes 3899424 | tf_op jit(solution)/shard_map/all_to_all | solution.py:493
  100.3 3.4 %collective-permute-start.5 = (bf16[2,224,576]{2,1,0:T(8,128)(2,1)}, bf16[2,224,576]{2,1,0:T(8,128)(2,1)}, u32[]{:S(2)}, u32[]{:S(2)}) collective-permute-start(bf16[2,224,576]{2,1,0:T(8,128)(2,1)} %after.10), channel_id=1, source_target_pairs={{0,8},{1,9},{2,10},{3,11},{4,12},{5,13},{6,14},{7,15},{8,0},{9,1},... | collective-permute-start | bytes 1548296 | tf_op jit(solution)/shard_map/ppermute | solution.py:19
  105.8 6.8 %gate_up_product.3 = bf16[136,2048]{1,0:T(8,128)(2,1)S(1)} custom-call(s32[1]{0:T(128)} %bitcast.1.meta_ref.rank_ref, bf16[4,136,3584]{2,1,0:T(8,128)(2,1)} %get-tuple-element.29.refs_0_.refs_1_.refs_2_, bf16[896,2048]{1,0:T(8,128)(2,1)S(1)} %copy-done.1, bf16[896,2048]{1,0:T(8,128)(2,1)} %get-tuple-element.30.refs_4_.refs_2_, ...), custom_call_target="tpu_custom_call" | custom-call | flops 1996488704 | bytes 15654912 | tf_op jit(solution)/shard_map/gate_up_product/pallas_call | solution.py:237
  112.6 11.2 %gate_up_product.2 = (f32[136,2048]{1,0:T(8,128)S(1)}, bf16[136,2048]{1,0:T(8,128)(2,1)S(1)}, f32[136,2048]{1,0:T(8,128)S(1)}) custom-call(s32[1]{0:T(128)} %bitcast.1.meta_ref.rank_ref, bf16[4,136,3584]{2,1,0:T(8,128)(2,1)} %get-tuple-element.29.refs_0_.refs_1_.refs_2_, bf16[4,136,3584]{2,1,0:T(8,128)(2,1)} %get-tuple-element.29.refs_0_.refs_1_.refs_2_, ...), custom_call_target="tpu_custom_call" | custom-call | flops 5989466112 | bytes 17604608 | tf_op jit(solution)/shard_map/gate_up_product/pallas_call | solution.py:237
  126.6 8.2 %collective-permute-done.8.refs_0_ = bf16[1024,896]{1,0:T(8,128)(2,1)S(1)} collective-permute-done((bf16[1024,896]{1,0:T(8,128)(2,1)}, bf16[1024,896]{1,0:T(8,128)(2,1)S(1)}, u32[]{:S(2)}, u32[]{:S(2)}) %collective-permute-start.8) | collective-permute-done | bytes 1835040 | tf_op jit(solution)/shard_map/ppermute | solution.py:19
  149.3 5.7 %down_product.3.refs_1_ = bf16[2,136,3584]{2,1,0:T(8,128)(2,1)} custom-call(s32[1]{0:T(128)} %bitcast.1.meta_ref.rank_ref, bf16[136,1024]{1,0:T(8,128)(2,1)} %fusion.2.refs_1_.hidden_ref, bf16[1024,896]{1,0:T(8,128)(2,1)} %refs_0_.5, bf16[1024,896]{1,0:T(8,128)(2,1)} %after.11.refs_1_, bf16[256,896]{1,0:T(8,128)(2,1)} %get-tuple-element.40.refs_2_, ...), custom_call_target="tpu_custom_call" | custom-call | flops 998244352 | bytes 8593408 | tf_op jit(solution)/shard_map/down_product/pallas_call | solution.py:310
  155.0 5.0 %all-to-all-start.1 = ((bf16[2,136,3584]{2,1,0:T(8,128)(2,1)}), bf16[2,136,3584]{2,1,0:T(8,128)(2,1)}, u32[]{:S(2)}, u32[]{:S(2)}) async-start(bf16[2,136,3584]{2,1,0:T(8,128)(2,1)} %down_product.3.refs_1_), calls=%async_computation.1 | async-start | bytes 3899392 | tf_op jit(solution)/shard_map/all_to_all | solution.py:533
  160.0 6.2 %collective-permute-done.17.refs_0_ = bf16[136,1024]{1,0:T(8,128)(2,1)S(1)} collective-permute-done((bf16[136,1024]{1,0:T(8,128)(2,1)}, bf16[136,1024]{1,0:T(8,128)(2,1)S(1)}, u32[]{:S(2)}, u32[]{:S(2)}) %collective-permute-start.17) | collective-permute-done | bytes 278560 | tf_op jit(solution)/shard_map/ppermute | solution.py:19
  166.9 5.5 %down_product.4.refs_1_ = bf16[136,3584]{1,0:T(8,128)(2,1)} custom-call(s32[1]{0:T(128)} %bitcast.1.meta_ref.rank_ref, bf16[136,1024]{1,0:T(8,128)(2,1)} %after.15.hidden_ref, bf16[1024,896]{1,0:T(8,128)(2,1)} %refs_0_.5, bf16[1024,896]{1,0:T(8,128)(2,1)} %after.11.refs_1_, bf16[256,896]{1,0:T(8,128)(2,1)} %get-tuple-element.40.refs_2_, ...), custom_call_target="tpu_custom_call" | custom-call | flops 998244352 | bytes 8593408 | tf_op jit(solution)/shard_map/down_product/pallas_call | solution.py:310
  184.0 8.3 %collective-permute-done.18 = bf16[136,1024]{1,0:T(8,128)(2,1)S(1)} collective-permute-done((bf16[136,1024]{1,0:T(8,128)(2,1)S(1)}, bf16[136,1024]{1,0:T(8,128)(2,1)S(1)}, u32[]{:S(2)}, u32[]{:S(2)}) %collective-permute-start.18) | collective-permute-done | bytes 278560 | tf_op jit(solution)/shard_map/ppermute | solution.py:19
  193.1 6.6 %down_product.5 = (bf16[136,3584]{1,0:T(8,128)(2,1)}, bf16[136,3584]{1,0:T(8,128)(2,1)}) custom-call(s32[1]{0:T(128)} %bitcast.1.meta_ref.rank_ref, bf16[272,1024]{1,0:T(8,128)(2,1)} %pad_maximum_fusion.3.hidden_ref, bf16[1024,896]{1,0:T(8,128)(2,1)} %refs_0_.5, bf16[1024,896]{1,0:T(8,128)(2,1)} %after.11.refs_1_, ...), custom_call_target="tpu_custom_call" | custom-call | flops 1996488704 | bytes 9846784 | tf_op jit(solution)/shard_map/down_product/pallas_call | solution.py:310
  200.4 7.0 %collective-permute-done.14.refs_2_ = bf16[2,448,576]{2,1,0:T(8,128)(2,1)} collective-permute-done((bf16[2,448,576]{2,1,0:T(8,128)(2,1)S(1)}, bf16[2,448,576]{2,1,0:T(8,128)(2,1)}, u32[]{:S(2)}, u32[]{:S(2)}) %collective-permute-start.14) | collective-permute-done | bytes 1032224 | tf_op jit(solution)/shard_map/ppermute | solution.py:19
  207.4 22.5 %collective-permute-done.15.refs_3_ = bf16[2,448,576]{2,1,0:T(8,128)(2,1)} collective-permute-done((bf16[2,448,576]{2,1,0:T(8,128)(2,1)}, bf16[2,448,576]{2,1,0:T(8,128)(2,1)}, u32[]{:S(2)}, u32[]{:S(2)}) %collective-permute-start.15) | collective-permute-done | bytes 1032224 | tf_op jit(solution)/shard_map/ppermute | solution.py:19
  231.5 5.6 %latent_product.1 = (bf16[256,576]{1,0:T(8,128)(2,1)S(1)}, f32[256,576]{1,0:T(8,128)S(1)}) custom-call(s32[1]{0:T(128)} %bitcast.1.meta_ref.rank_ref, bf16[8,256,448]{2,1,0:T(8,128)(2,1)S(1)} %copy-done.4, bf16[8,256,448]{2,1,0:T(8,128)(2,1)S(1)} %copy-done, bf16[2,448,576]{2,1,0:T(8,128)(2,1)S(1)} %pad_maximum_fusion.refs_0_, ...), custom_call_target="tpu_custom_call" | custom-call | flops 2113929216 | bytes 7798784 | tf_op jit(solution)/shard_map/latent_product/pallas_call | solution.py:387
  238.7 5.6 %unpack_rows.2.refs_1_.refs_2_ = bf16[256,7168]{1,0:T(8,128)(2,1)} custom-call(s32[1]{0:T(128)} %bitcast.1.meta_ref.rank_ref, s32[16]{0:T(128)} %lengths_ref.5, s32[1,256]{1,0:T(1,128)} %bitcast.9, f32[1,256]{1,0:T(1,128)} %bitcast.11, bf16[136,3584]{1,0:T(8,128)(2,1)} %get-tuple-element.44.refs_0_, bf16[2,136,3584]{2,1,0:T(8,128)(2,1)} %all-to-all-done.1.refs_1_), custom_call_target="tpu_custom_call" | custom-call | flops 939524096 | bytes 3670016 | tf_op jit(solution)/shard_map/unpack_rows/pallas_call | solution.py:143
  245.7 5.5 %unpack_rows.3 = bf16[256,7168]{1,0:T(8,128)(2,1)} custom-call(s32[1]{0:T(128)} %bitcast.1.meta_ref.rank_ref, s32[16]{0:T(128)} %lengths_ref.5, s32[1,256]{1,0:T(1,128)} %bitcast.10, f32[1,256]{1,0:T(1,128)} %bitcast.12, bf16[136,3584]{1,0:T(8,128)(2,1)} %collective-permute-done.20.refs_0_, ...), custom_call_target="tpu_custom_call", output_to_operand_aliasing={{}: (6, {})} | custom-call | flops 939524096 | bytes 3670016 | tf_op jit(solution)/shard_map/unpack_rows/pallas_call | solution.py:143
  (115 shorter events, 50.7 us)
Async XLA Ops:
  0.6 81.5 %collective-permute-start = (bf16[896,2048]{1,0:T(8,128)(2,1)}, bf16[896,2048]{1,0:T(8,128)(2,1)}, u32[]{:S(2)}, u32[]{:S(2)}) collective-permute-start(bf16[896,2048]{1,0:T(8,128)(2,1)} %refs_1_.1), channel_id=1, source_target_pairs={{0,2},{1,3},{2,0},{3,1},{4,6},{5,7},{6,4},{7,5},{8,10},{9,11},{10,... | collective-permute-start | bytes 11010056 | tf_op jit(solution)/shard_map/ppermute | solution.py:19
  3.2 8.4 %collective-permute-start.2 = (bf16[1,224,576]{2,1,0:T(8,128)(2,1)S(1)}, bf16[1,224,576]{2,1,0:T(8,128)(2,1)S(1)}, u32[]{:S(2)}, u32[]{:S(2)}) collective-permute-start(bf16[1,224,576]{2,1,0:T(8,128)(2,1)S(1)} %dynamic-slice_bitcast_fusion), channel_id=1, source_target_pairs={{0,4},{1,5},{2,6},{3,7},{4,0},{5,1},{6,2},{7,3},{8,12},{9,13},{10,... | collective-permute-start | bytes 774152 | tf_op jit(solution)/shard_map/ppermute | solution.py:19
  12.3 88.1 %all-to-all-start = ((bf16[4,136,3584]{2,1,0:T(8,128)(2,1)}), bf16[4,136,3584]{2,1,0:T(8,128)(2,1)}, u32[]{:S(2)}, u32[]{:S(2)}) async-start(bf16[4,136,3584]{2,1,0:T(8,128)(2,1)} %after.9), calls=%async_computation | async-start | bytes 7798784 | tf_op jit(solution)/shard_map/all_to_all | solution.py:493
  27.9 5.8 %collective-permute-start.1 = (bf16[8,256,448]{1,2,0:T(8,128)(2,1)S(1)}, bf16[8,256,448]{1,2,0:T(8,128)(2,1)}, u32[]{:S(2)}, u32[]{:S(2)}) collective-permute-start(bf16[8,256,448]{1,2,0:T(8,128)(2,1)S(1)} %copy.37), channel_id=1, source_target_pairs={{0,1},{1,0},{2,3},{3,2},{4,5},{5,4},{6,7},{7,6},{8,9},{9,8},{10,11... | collective-permute-start | bytes 5505032 | tf_op jit(solution)/shard_map/ppermute | solution.py:19
  28.0 67.7 %collective-permute-start.3 = (bf16[896,2048]{1,0:T(8,128)(2,1)}, bf16[896,2048]{1,0:T(8,128)(2,1)}, u32[]{:S(2)}, u32[]{:S(2)}) collective-permute-start(bf16[896,2048]{1,0:T(8,128)(2,1)} %refs_1_.1), channel_id=1, source_target_pairs={{0,1},{1,0},{2,3},{3,2},{4,5},{5,4},{6,7},{7,6},{8,9},{9,8},{10,11... | collective-permute-start | bytes 11010056 | tf_op jit(solution)/shard_map/ppermute | solution.py:19
  82.1 18.3 %collective-permute-start.4 = (bf16[896,2048]{1,0:T(8,128)(2,1)}, bf16[896,2048]{1,0:T(8,128)(2,1)}, u32[]{:S(2)}, u32[]{:S(2)}) collective-permute-start(bf16[896,2048]{1,0:T(8,128)(2,1)} %get-tuple-element.28.refs_5_.refs_3_.refs_1_), channel_id=1, source_target_pairs={{0,1},{1,0},{2,3},{3,2},{4,5},{5,4},{6,7},{7,6},{8,9},{9,8},{10,11... | collective-permute-start | bytes 11010056 | tf_op jit(solution)/shard_map/ppermute | solution.py:19
  82.1 8.9 %collective-permute-start.7 = (bf16[1024,896]{1,0:T(8,128)(2,1)}, bf16[1024,896]{1,0:T(8,128)(2,1)S(1)}, u32[]{:S(2)}, u32[]{:S(2)}) collective-permute-start(bf16[1024,896]{1,0:T(8,128)(2,1)} %refs_0_.5), channel_id=1, source_target_pairs={{0,1},{1,0},{2,3},{3,2},{4,5},{5,4},{6,7},{7,6},{8,9},{9,8},{10,11... | collective-permute-start | bytes 5505032 | tf_op jit(solution)/shard_map/ppermute | solution.py:19
  92.3 42.5 %collective-permute-start.8 = (bf16[1024,896]{1,0:T(8,128)(2,1)}, bf16[1024,896]{1,0:T(8,128)(2,1)S(1)}, u32[]{:S(2)}, u32[]{:S(2)}) collective-permute-start(bf16[1024,896]{1,0:T(8,128)(2,1)} %after.11.refs_1_), channel_id=1, source_target_pairs={{0,2},{1,3},{2,0},{3,1},{4,6},{5,7},{6,4},{7,5},{8,10},{9,11},{10,... | collective-permute-start | bytes 5505032 | tf_op jit(solution)/shard_map/ppermute | solution.py:19
  100.3 26.3 %collective-permute-start.5 = (bf16[2,224,576]{2,1,0:T(8,128)(2,1)}, bf16[2,224,576]{2,1,0:T(8,128)(2,1)}, u32[]{:S(2)}, u32[]{:S(2)}) collective-permute-start(bf16[2,224,576]{2,1,0:T(8,128)(2,1)} %after.10), channel_id=1, source_target_pairs={{0,8},{1,9},{2,10},{3,11},{4,12},{5,13},{6,14},{7,15},{8,0},{9,1},... | collective-permute-start | bytes 1548296 | tf_op jit(solution)/shard_map/ppermute | solution.py:19
  112.5 26.2 %collective-permute-start.6 = (bf16[136,2048]{1,0:T(8,128)(2,1)S(1)}, bf16[136,2048]{1,0:T(8,128)(2,1)}, u32[]{:S(2)}, u32[]{:S(2)}) collective-permute-start(bf16[136,2048]{1,0:T(8,128)(2,1)S(1)} %gate_up_product.3), channel_id=1, source_target_pairs={{0,4},{1,5},{2,6},{3,7},{4,0},{5,1},{6,2},{7,3},{8,12},{9,13},{10,... | collective-permute-start | bytes 1671176 | tf_op jit(solution)/shard_map/ppermute | solution.py:19
  137.6 1.9 collective-permute-start.9
  137.7 2.6 %collective-permute-start.10 = (bf16[256,896]{1,0:T(8,128)(2,1)S(1)}, bf16[256,896]{1,0:T(8,128)(2,1)}, u32[]{:S(2)}, u32[]{:S(2)}) collective-permute-start(bf16[256,896]{1,0:T(8,128)(2,1)S(1)} %get-tuple-element.54), channel_id=1, source_target_pairs={{0,1},{1,0},{2,3},{3,2},{4,5},{5,4},{6,7},{7,6},{8,9},{9,8},{10,11... | collective-permute-start | bytes 1376264 | tf_op jit(solution)/shard_map/ppermute | solution.py:19
  138.2 2.7 %collective-permute-start.11 = (bf16[256,896]{1,0:T(8,128)(2,1)S(1)}, bf16[256,896]{1,0:T(8,128)(2,1)}, u32[]{:S(2)}, u32[]{:S(2)}) collective-permute-start(bf16[256,896]{1,0:T(8,128)(2,1)S(1)} %get-tuple-element.53), channel_id=1, source_target_pairs={{0,1},{1,0},{2,3},{3,2},{4,5},{5,4},{6,7},{7,6},{8,9},{9,8},{10,11... | collective-permute-start | bytes 1376264 | tf_op jit(solution)/shard_map/ppermute | solution.py:19
  138.3 3.3 %collective-permute-start.12 = (bf16[256,896]{1,0:T(8,128)(2,1)S(1)}, bf16[256,896]{1,0:T(8,128)(2,1)}, u32[]{:S(2)}, u32[]{:S(2)}) collective-permute-start(bf16[256,896]{1,0:T(8,128)(2,1)S(1)} %get-tuple-element.52), channel_id=1, source_target_pairs={{0,1},{1,0},{2,3},{3,2},{4,5},{5,4},{6,7},{7,6},{8,9},{9,8},{10,11... | collective-permute-start | bytes 1376264 | tf_op jit(solution)/shard_map/ppermute | solution.py:19
  143.7 28.7 %collective-permute-start.16 = (bf16[136,2048]{1,0:T(8,128)(2,1)}, bf16[136,2048]{1,0:T(8,128)(2,1)S(1)}, u32[]{:S(2)}, u32[]{:S(2)}) collective-permute-start(bf16[136,2048]{1,0:T(8,128)(2,1)} %after.14), channel_id=1, source_target_pairs={{0,4},{1,5},{2,6},{3,7},{4,0},{5,1},{6,2},{7,3},{8,12},{9,13},{10,... | collective-permute-start | bytes 1671176 | tf_op jit(solution)/shard_map/ppermute | solution.py:19
  143.9 22.3 %collective-permute-start.17 = (bf16[136,1024]{1,0:T(8,128)(2,1)}, bf16[136,1024]{1,0:T(8,128)(2,1)S(1)}, u32[]{:S(2)}, u32[]{:S(2)}) collective-permute-start(bf16[136,1024]{1,0:T(8,128)(2,1)} %fusion.2.refs_1_.hidden_ref), channel_id=1, source_target_pairs={{0,4},{1,5},{2,6},{3,7},{4,0},{5,1},{6,2},{7,3},{8,12},{9,13},{10,... | collective-permute-start | bytes 835592 | tf_op jit(solution)/shard_map/ppermute | solution.py:19
  147.8 29.2 %collective-permute-start.13 = (bf16[3,224,576]{2,1,0:T(8,128)(2,1)}, bf16[3,224,576]{2,1,0:T(8,128)(2,1)S(1)}, u32[]{:S(2)}, u32[]{:S(2)}) collective-permute-start(bf16[3,224,576]{2,1,0:T(8,128)(2,1)} %after.13), channel_id=1, source_target_pairs={{0,16},{16,0},{1,17},{17,1},{2,18},{18,2},{3,19},{19,3},{4,20},{20... | collective-permute-start | bytes 2322440 | tf_op jit(solution)/shard_map/ppermute | solution.py:547
  155.0 83.7 %all-to-all-start.1 = ((bf16[2,136,3584]{2,1,0:T(8,128)(2,1)}), bf16[2,136,3584]{2,1,0:T(8,128)(2,1)}, u32[]{:S(2)}, u32[]{:S(2)}) async-start(bf16[2,136,3584]{2,1,0:T(8,128)(2,1)} %down_product.3.refs_1_), calls=%async_computation.1 | async-start | bytes 3899392 | tf_op jit(solution)/shard_map/all_to_all | solution.py:533
  174.6 17.6 %collective-permute-start.18 = (bf16[136,1024]{1,0:T(8,128)(2,1)S(1)}, bf16[136,1024]{1,0:T(8,128)(2,1)S(1)}, u32[]{:S(2)}, u32[]{:S(2)}) collective-permute-start(bf16[136,1024]{1,0:T(8,128)(2,1)S(1)} %fusion.1), channel_id=1, source_target_pairs={{0,4},{1,5},{2,6},{3,7},{4,0},{5,1},{6,2},{7,3},{8,12},{9,13},{10,... | collective-permute-start | bytes 835592 | tf_op jit(solution)/shard_map/ppermute | solution.py:19
  179.1 28.3 %collective-permute-start.14 = (bf16[2,448,576]{2,1,0:T(8,128)(2,1)S(1)}, bf16[2,448,576]{2,1,0:T(8,128)(2,1)}, u32[]{:S(2)}, u32[]{:S(2)}) collective-permute-start(bf16[2,448,576]{2,1,0:T(8,128)(2,1)S(1)} %pad_maximum_fusion.refs_0_), channel_id=1, source_target_pairs={{0,2},{1,3},{2,0},{3,1},{4,6},{5,7},{6,4},{7,5},{8,10},{9,11},{10,... | collective-permute-start | bytes 3096584 | tf_op jit(solution)/shard_map/ppermute | solution.py:19
  180.8 49.1 %collective-permute-start.15 = (bf16[2,448,576]{2,1,0:T(8,128)(2,1)}, bf16[2,448,576]{2,1,0:T(8,128)(2,1)}, u32[]{:S(2)}, u32[]{:S(2)}) collective-permute-start(bf16[2,448,576]{2,1,0:T(8,128)(2,1)} %slice.62.refs_1_), channel_id=1, source_target_pairs={{0,2},{1,3},{2,0},{3,1},{4,6},{5,7},{6,4},{7,5},{8,10},{9,11},{10,... | collective-permute-start | bytes 3096584 | tf_op jit(solution)/shard_map/ppermute | solution.py:19
  181.1 64.6 %collective-permute-start.21 = (bf16[136,3584]{1,0:T(8,128)(2,1)}, bf16[136,3584]{1,0:T(8,128)(2,1)}, u32[]{:S(2)}, u32[]{:S(2)}) collective-permute-start(bf16[136,3584]{1,0:T(8,128)(2,1)} %down_product.4.refs_1_), channel_id=1, source_target_pairs={{0,12},{1,13},{2,14},{3,15},{4,8},{5,9},{6,10},{7,11},{8,4},{9,5},... | collective-permute-start | bytes 2924552 | tf_op jit(solution)/shard_map/ppermute | solution.py:19
  199.7 46.0 %collective-permute-start.20 = (bf16[136,3584]{1,0:T(8,128)(2,1)}, bf16[136,3584]{1,0:T(8,128)(2,1)}, u32[]{:S(2)}, u32[]{:S(2)}) collective-permute-start(bf16[136,3584]{1,0:T(8,128)(2,1)} %get-tuple-element.45), channel_id=1, source_target_pairs={{0,4},{1,5},{2,6},{3,7},{4,0},{5,1},{6,2},{7,3},{8,12},{9,13},{10,... | collective-permute-start | bytes 2924552 | tf_op jit(solution)/shard_map/ppermute | solution.py:19
  244.3 6.8 %collective-permute-start.19 = (bf16[256,576]{1,0:T(8,128)(2,1)}, bf16[256,576]{1,0:T(8,128)(2,1)S(1)}, u32[]{:S(2)}, u32[]{:S(2)}) collective-permute-start(bf16[256,576]{1,0:T(8,128)(2,1)} %after.17), channel_id=1, source_target_pairs={{0,1},{1,0},{2,3},{3,2},{4,5},{5,4},{6,7},{7,6},{8,9},{9,8},{10,11... | collective-permute-start | bytes 884744 | tf_op jit(solution)/shard_map/ppermute | solution.py:19
  (21 other events, 85.2 us)

commit v6 on v5

--- a/solution.py
+++ b/solution.py
@@ -40,7 +40,7 @@
     slot = lax.broadcasted_iota(jnp.int32, (size, rows), 0)
     for expert in range(experts):
         hit = (place == slot) & (chosen == expert)
-        picks_ref[expert] = hit.astype(jnp.float32).astype(jnp.bfloat16)
+        picks_ref[pl.ds(expert * size, size), :] = hit.astype(jnp.float32).astype(jnp.bfloat16)
 
 
 def picks_by_row(rank_ref, lengths_ref, ids_row, experts, size, picks_ref):
@@ -56,42 +56,60 @@
         picks_ref[expert] = hit.astype(jnp.float32).astype(jnp.bfloat16)
 
 
-def pack_body(rank_ref, lengths_ref, ids_ref, low_ref, high_ref, out_ref, picks_ref):
-    experts, size, _ = picks_ref.shape
-
-    @pl.when(pl.program_id(0) == 0)
-    def _():
-        picks_by_slot(rank_ref, lengths_ref, ids_ref[...], experts, size, picks_ref)
-
-    for side, source_ref in enumerate((low_ref, high_ref)):
+def pack_body(rank_ref, lengths_ref, ids_ref, tokens_ref, out_ref, rows_in, rows_out, picks_ref, came, went):
+    _, experts, size, part = rows_out.shape
+    quarter = rank_ref[0] % QUAD
+
+    def fetch(turn):
+        block = turn % 2 * QUAD + (quarter ^ (turn // 2))
+        column = pl.multiple_of(block * part, 128)
+        return pltpu.make_async_copy(
+            tokens_ref.at[:, pl.ds(column, part)], rows_in.at[turn], came.at[turn]
+        )
+
+    def send(turn, expert):
+        to = 2 * expert + turn % 2
+        return pltpu.make_async_copy(
+            rows_out.at[turn, expert],
+            out_ref.at[to, :, pl.ds(turn // 2 * part, part)],
+            went.at[turn, expert],
+        )
+
+    for turn in range(GROUP):
+        fetch(turn).start()
+    picks_by_slot(rank_ref, lengths_ref, ids_ref[...], experts, size, picks_ref)
+    for turn in range(GROUP):
+        fetch(turn).wait()
+        made = jnp.dot(picks_ref[...], rows_in[turn], preferred_element_type=jnp.float32)
         for expert in range(experts):
-            out_ref[2 * expert + side] = jnp.dot(
-                picks_ref[expert], source_ref[...], preferred_element_type=jnp.float32
-            ).astype(jnp.bfloat16)
+            rows = made[expert * size : (expert + 1) * size]
+            rows_out[turn, expert] = rows.astype(jnp.bfloat16)
+            send(turn, expert).start()
+    for turn in range(GROUP):
+        for expert in range(experts):
+            send(turn, expert).wait()
 
 
 def pack(rank_array, lengths, ids, tokens, experts, size):
     rows, width = tokens.shape
     part = width // GROUP
-
-    def column_of(side):
-        return lambda k, rank_ref, lengths_ref: (0, side * QUAD + ((rank_ref[0] % QUAD) ^ k))
-
-    whole = lambda k, rank_ref, lengths_ref: (0, 0)
     return pl.pallas_call(
         pack_body,
         grid_spec=pltpu.PrefetchScalarGridSpec(
             num_scalar_prefetch=2,
-            grid=(QUAD,),
+            grid=(),
             in_specs=[
-                pl.BlockSpec((1, rows), whole),
-                pl.BlockSpec((rows, part), column_of(0)),
-                pl.BlockSpec((rows, part), column_of(1)),
+                pl.BlockSpec(memory_space=pltpu.VMEM),
+                pl.BlockSpec(memory_space=pl.ANY),
             ],
-            out_specs=pl.BlockSpec(
-                (2 * experts, size, part), lambda k, rank_ref, lengths_ref: (0, 0, k)
-            ),
-            scratch_shapes=[pltpu.VMEM((experts, size, rows), jnp.bfloat16)],
+            out_specs=pl.BlockSpec(memory_space=pl.ANY),
+            scratch_shapes=[
+                pltpu.VMEM((GROUP, rows, part), jnp.bfloat16),
+                pltpu.VMEM((GROUP, experts, size, part), jnp.bfloat16),
+                pltpu.VMEM((experts * size, rows), jnp.bfloat16),
+                pltpu.SemaphoreType.DMA((GROUP,)),
+                pltpu.SemaphoreType.DMA((GROUP, experts)),
+            ],
         ),
         out_shape=jax.ShapeDtypeStruct((2 * experts, size, QUAD * part), jnp.bfloat16),
         compiler_params=pltpu.CompilerParams(vmem_limit_bytes=58 << 20),
@@ -99,29 +117,52 @@
             flops=4 * rows * rows * width, bytes_accessed=4 * rows * width, transcendentals=0
         ),
         name="pack_rows",
-    )(rank_array, lengths, ids.reshape(1, rows), tokens, tokens)
+    )(rank_array, lengths, ids.reshape(1, rows), tokens)
 
 
 def unpack_body(near, rank_ref, lengths_ref, ids_ref, gate_ref, *refs):
-    out_ref, picks_ref, gate_column_ref = refs[-3:]
+    out_ref, parts_in, rows_out, picks_ref, came, went = refs[-6:]
     experts, rows, size = picks_ref.shape
+    part = rows_out.shape[2]
     my_expert = rank_ref[0] // GROUP
-
-    @pl.when(pl.program_id(0) == 0)
-    def _():
-        picks_by_row(rank_ref, lengths_ref, ids_ref[...], experts, size, picks_ref)
-        down = lax.broadcasted_iota(jnp.int32, (rows, rows), 0)
-        along = lax.broadcasted_iota(jnp.int32, (rows, rows), 1)
-        gate_column_ref[...] = jnp.sum(
-            jnp.where(down == along, gate_ref[...], 0.0), axis=1, keepdims=True
+    quarter = rank_ref[0] % QUAD
+    high = (rank_ref[0] // QUAD) % 2
+    side = high if near else 1 - high
+
+    def fetch(k, number):
+        columns = pl.ds(k * part, part)
+        if near and number:
+            source = refs[1].at[my_expert ^ number, :, columns]
+        else:
+            source = refs[number].at[:, columns]
+        return pltpu.make_async_copy(source, parts_in.at[k, number], came.at[k, number])
+
+    def send(k):
+        column = pl.multiple_of((side * QUAD + (quarter ^ k)) * part, 128)
+        return pltpu.make_async_copy(
+            rows_out.at[k], out_ref.at[:, pl.ds(column, part)], went.at[k]
         )
 
-    total = jnp.zeros(out_ref.shape, jnp.float32)
-    for number in range(experts):
-        expert = my_expert ^ number
-        part = refs[1][expert] if near and number else refs[number][...]
-        total += jnp.dot(picks_ref[expert], part, preferred_element_type=jnp.float32)
-    out_ref[...] = (total * gate_column_ref[...]).astype(jnp.bfloat16)
+    for k in range(QUAD):
+        for number in range(experts):
+            fetch(k, number).start()
+    picks_by_row(rank_ref, lengths_ref, ids_ref[...], experts, size, picks_ref)
+    down = lax.broadcasted_iota(jnp.int32, (rows, rows), 0)
+    along = lax.broadcasted_iota(jnp.int32, (rows, rows), 1)
+    gate = jnp.sum(jnp.where(down == along, gate_ref[...], 0.0), axis=1, keepdims=True)
+    for k in range(QUAD):
+        total = jnp.zeros((rows, part), jnp.float32)
+        for number in range(experts):
+            fetch(k, number).wait()
+            total += jnp.dot(
+                picks_ref[my_expert ^ number],
+                parts_in[k, number],
+                preferred_element_type=jnp.float32,
+            )
+        rows_out[k] = (total * gate).astype(jnp.bfloat16)
+        send(k).start()
+    for k in range(QUAD):
+        send(k).wait()
 
 
 def unpack(rank_array, lengths, ids, gates, parts, width, near, base=()):
@@ -129,33 +170,25 @@
     part = width // GROUP
     size = parts[0].shape[-2]
     experts = parts[1].shape[0] if near else len(parts)
-
-    def out_index(k, rank_ref, lengths_ref):
-        quarter = rank_ref[0] % QUAD
-        high = (rank_ref[0] // QUAD) % 2
-        return (0, (high if near else 1 - high) * QUAD + (quarter ^ k))
-
-    whole = lambda k, rank_ref, lengths_ref: (0, 0)
-    specs = [pl.BlockSpec((size, part), lambda k, rank_ref, lengths_ref: (0, k))] * experts
-    if near:
-        both = pl.BlockSpec((experts, size, part), lambda k, rank_ref, lengths_ref: (0, 0, k))
-        specs = [specs[0], both]
+    inside = pl.BlockSpec(memory_space=pltpu.VMEM)
+    anywhere = pl.BlockSpec(memory_space=pl.ANY)
     return pl.pallas_call(
         functools.partial(unpack_body, near),
         grid_spec=pltpu.PrefetchScalarGridSpec(
             num_scalar_prefetch=2,
-            grid=(QUAD,),
-            in_specs=[pl.BlockSpec((1, rows), whole), pl.BlockSpec((1, rows), whole)]
-            + specs
-            + [pl.BlockSpec(memory_space=pl.ANY)] * len(base),
-            out_specs=pl.BlockSpec((rows, part), out_index),
+            grid=(),
+            in_specs=[inside, inside] + [anywhere] * (len(parts) + len(base)),
+            out_specs=anywhere,
             scratch_shapes=[
+                pltpu.VMEM((QUAD, experts, size, part), jnp.bfloat16),
+                pltpu.VMEM((QUAD, rows, part), jnp.bfloat16),
                 pltpu.VMEM((experts, rows, size), jnp.bfloat16),
-                pltpu.VMEM((rows, 1), jnp.float32),
+                pltpu.SemaphoreType.DMA((QUAD, experts)),
+                pltpu.SemaphoreType.DMA((QUAD,)),
             ],
         ),
         out_shape=jax.ShapeDtypeStruct((rows, width), jnp.bfloat16),
-        input_output_aliases={4 + len(specs): 0} if base else {},
+        input_output_aliases={4 + len(parts): 0} if base else {},
         compiler_params=pltpu.CompilerParams(vmem_limit_bytes=58 << 20),
         cost_estimate=pl.CostEstimate(
             flops=2 * rows * rows * width, bytes_accessed=2 * rows * width, transcendentals=0
@@ -488,14 +521,15 @@
     latent_1 = swapped(sent, QUAD)
     packed = after(packed, latent_1)
     gate_2, mine, other = together(swapped(gate_up, 2), mine, swapped(other, 1))
-    down_1 = swapped(down_weight, 1)
+    mid = down_weight.shape[0] // 2
+    down_1 = [swapped(half_rows, 1) for half_rows in (down_weight[:mid], down_weight[mid:])]
     arrived, gate_1, gate_3 = together(
         lax.all_to_all(packed, "dp", 0, 0, axis_index_groups=columns, tiled=True),
         swapped(gate_up, 1),
         swapped(gate_2, 1),
     )
-    down_1 = after(down_1, gate_2)
-    down_3 = swapped(down_1, 2)
+    down_1 = [after(piece, gate_2) for piece in down_1]
+    down_3 = [swapped(piece, 2) for piece in down_1]
     if middle:
         cut = swapped(after(jnp.concatenate([sent, latent_1], axis=0), arrived), 2 * QUAD)
     else:
@@ -515,11 +549,15 @@
     )
     if middle:
         ours, cut = together(ours, cut)
-    down_3 = after(down_3, ours)
-    split = down_3.shape[0] // 4
-    down_2 = [swapped(down_3[n * split : (n + 1) * split], 1) for n in range(4)]
+    down_3 = [after(piece, ours) for piece in down_3]
+    quarter = mid // 2
+    down_2 = [
+        swapped(part, 1)
+        for piece in down_3
+        for part in (piece[:quarter], piece[quarter:])
+    ]
     came, *down_2 = together(swapped(theirs, QUAD), *down_2)
-    weight_out = [down_weight, down_1, *down_2, down_3]
+    weight_out = [down_weight, *down_1, *down_2, *down_3]
 
     def activated(own, other):
         summed = own + other.astype(jnp.float32)
@@ -531,11 +569,11 @@
     (made_own,) = down_product(meta, hidden, weight_out, experts - 1, True)
     halves = [[GROUP * e + low for e in range(experts)] for low in range(GROUP)]
     near = lax.all_to_all(made_own, "dp", 0, 0, axis_index_groups=halves, tiled=True)
-    partner = after(partner, made_own)
+    partner, theirs_near = together(after(partner, made_own), theirs_near)
     made = down_product(meta, partner, weight_out, experts - 1, False)
     far = [swapped(made[n - 1], QUAD * (2 * n + 1)) for n in away]
 
-    came_near = after(swapped(after(theirs_near, hidden), QUAD), made[0])
+    came_near = after(swapped(theirs_near, QUAD), made[0])
     hidden_near = activated(ours_near, came_near)
     both = jnp.concatenate([hidden_near, swapped(hidden_near, QUAD)], axis=0)
     here, there = down_product(meta, both, weight_out, 2, False)

time: 257 us -> 254 us (0.988)
  waiting for transfers between devices: 121 us -> 112 us
  local copies, waits for them, and re-layouts: 24.2 us -> 30.9 us
    ppermute x21 -> x23, waiting for transfers between devices: 116 us -> 108 us  [swapped(): lax.ppermute(block, 'dp', [(low, low ^ bits) for low in range(count)])]
    unnamed x43 -> x51, local copies, waits for them, and re-layouts: 12.8 us -> 16.5 us
    slice x1 -> x3, local copies, waits for them, and re-layouts: 1.58 us -> 4.52 us  [the longest x2 3.41 us: shards(): piece[quarter:]]
    ppermute x21 -> x23, starting transfers between devices: 18.6 us -> 19.1 us  [swapped(): lax.ppermute(block, 'dp', [(low, low ^ bits) for low in range(count)])]
  transfers between devices with their start and end apart: 24 -> 26, of which waited for: 16 -> 13; matrix products, arithmetic and copies ran while one was open for 8% -> 9% of each run, Pallas kernels for 26% -> 26%
where the time goes in v6:
time: 254 us; the launch traced here: 251 us
  waiting for transfers between devices  112 us (44%)
  Pallas kernels  64.6 us (25%)
  local copies, waits for them, and re-layouts  30.9 us (12%)
  starting transfers between devices  30.8 us (12%)
  other arithmetic  11.3 us (4%)
    ppermute x23, waiting for transfers between devices, swapped(): lax.ppermute(block, 'dp', [(low, low ^ bits) for low in range(count)])  108 us
    ppermute x23, starting transfers between devices, swapped(): lax.ppermute(block, 'dp', [(low, low ^ bits) for low in range(count)])  19.1 us
    pallas_call x2, Pallas kernels, gate_up_product(): pl.pallas_call(functools.partial(gate_up_body, [len(numbers) for numbers,...  18 us
    pallas_call x3, Pallas kernels, down_product(): pl.pallas_call(functools.partial(down_body, places, joined), grid_spec=pl...  17.9 us
    unnamed x51, local copies, waits for them, and re-layouts  16.5 us
    pallas_call x2, Pallas kernels, unpack(): pl.pallas_call(functools.partial(unpack_body, near), grid_spec=pltpu.Pref...  10.1 us
    pallas_call x1, Pallas kernels, core_split(): pl.pallas_call(core_split_body, grid_spec=pltpu.PrefetchScalarGridSpec(nu...  7.04 us
    pallas_call x1, Pallas kernels, pack(): pl.pallas_call(pack_body, grid_spec=pltpu.PrefetchScalarGridSpec(num_scal...  5.88 us
  transfers between devices with their start and end apart: 26, of which 13 were waited for; matrix products, arithmetic and copies ran while one was open for 9% of the time, Pallas kernels for 26%

profile of v6, /device:TPU:8, one launch (start us, length us, event | category | flops | bytes accessed | tf_op | source)
XLA Modules:
  0.0 250.5 jit_solution(11887977286872121891)
XLA Ops:
  3.7 5.9 %pack_rows.1.refs_0_ = bf16[4,136,3584]{2,1,0:T(8,128)(2,1)} custom-call(s32[1]{0:T(128)} %bitcast.1.meta_ref.rank_ref, s32[16]{0:T(128)} %lengths_ref.5, s32[1,256]{1,0:T(1,128)} %bitcast.8, bf16[256,7168]{1,0:T(8,128)(2,1)} %tokens_ref.3), custom_call_target="tpu_custom_call" | custom-call | flops 1879048192 | bytes 7340032 | tf_op jit(solution)/shard_map/pack_rows/pallas_call | solution.py:96
  12.3 5.3 %all-to-all-start = ((bf16[4,136,3584]{2,1,0:T(8,128)(2,1)}), bf16[4,136,3584]{2,1,0:T(8,128)(2,1)}, u32[]{:S(2)}, u32[]{:S(2)}) async-start(bf16[4,136,3584]{2,1,0:T(8,128)(2,1)} %after.10), calls=%async_computation | async-start | bytes 7798784 | tf_op jit(solution)/shard_map/all_to_all | solution.py:527
  17.6 7.0 %core_split.1 = (bf16[8,256,448]{2,1,0:T(8,128)(2,1)}, bf16[8,256,448]{2,1,0:T(8,128)(2,1)}) custom-call(s32[1]{0:T(128)} %bitcast.1.meta_ref.rank_ref, bf16[256,7168]{1,0:T(8,128)(2,1)} %tokens_ref.3), custom_call_target="tpu_custom_call" | custom-call | tf_op jit(solution)/shard_map/core_split/pallas_call | solution.py:474
  24.6 3.3 %copy.40 = bf16[8,256,448]{1,2,0:T(8,128)(2,1)S(1)} copy(bf16[8,256,448]{2,1,0:T(8,128)(2,1)} %get-tuple-element.27) | data formatting | bytes 3670016 | tf_op jit(solution)/shard_map/core_split/pallas_call | solution.py:474
  28.5 5.2 %collective-permute-done.1 = bf16[8,256,448]{1,2,0:T(8,128)(2,1)} collective-permute-done((bf16[8,256,448]{1,2,0:T(8,128)(2,1)S(1)}, bf16[8,256,448]{1,2,0:T(8,128)(2,1)}, u32[]{:S(2)}, u32[]{:S(2)}) %collective-permute-start.1) | collective-permute-done | bytes 1835040 | tf_op jit(solution)/shard_map/ppermute | solution.py:19
  33.7 3.8 %copy.41.refs_2_ = bf16[8,256,448]{2,1,0:T(8,128)(2,1)} copy(bf16[8,256,448]{1,2,0:T(8,128)(2,1)} %collective-permute-done.1) | data formatting | bytes 3670016 | tf_op jit(solution)/shard_map/ppermute | solution.py:19
  37.5 44.6 %collective-permute-done.refs_0_ = bf16[896,2048]{1,0:T(8,128)(2,1)} collective-permute-done((bf16[896,2048]{1,0:T(8,128)(2,1)}, bf16[896,2048]{1,0:T(8,128)(2,1)}, u32[]{:S(2)}, u32[]{:S(2)}) %collective-permute-start) | collective-permute-done | bytes 3670048 | tf_op jit(solution)/shard_map/ppermute | solution.py:19
  85.2 5.9 %collective-permute-done.7.refs_0_ = bf16[512,896]{1,0:T(8,128)(2,1)S(1)} collective-permute-done((bf16[512,896]{1,0:T(8,128)(2,1)S(1)}, bf16[512,896]{1,0:T(8,128)(2,1)S(1)}, u32[]{:S(2)}, u32[]{:S(2)}) %collective-permute-start.7) | collective-permute-done | bytes 917536 | tf_op jit(solution)/shard_map/ppermute | solution.py:19
  96.0 4.3 %all-to-all-done.refs_0_ = bf16[4,136,3584]{2,1,0:T(8,128)(2,1)} async-done(((bf16[4,136,3584]{2,1,0:T(8,128)(2,1)}), bf16[4,136,3584]{2,1,0:T(8,128)(2,1)}, u32[]{:S(2)}, u32[]{:S(2)}) %all-to-all-start) | async-done | bytes 3899424 | tf_op jit(solution)/shard_map/all_to_all | solution.py:527
  100.3 3.4 %collective-permute-start.5 = (bf16[2,224,576]{2,1,0:T(8,128)(2,1)}, bf16[2,224,576]{2,1,0:T(8,128)(2,1)}, u32[]{:S(2)}, u32[]{:S(2)}) collective-permute-start(bf16[2,224,576]{2,1,0:T(8,128)(2,1)} %after.11), channel_id=1, source_target_pairs={{0,8},{1,9},{2,10},{3,11},{4,12},{5,13},{6,14},{7,15},{8,0},{9,1},... | collective-permute-start | bytes 1548296 | tf_op jit(solution)/shard_map/ppermute | solution.py:19
  105.7 6.8 %gate_up_product.3 = bf16[136,2048]{1,0:T(8,128)(2,1)S(1)} custom-call(s32[1]{0:T(128)} %bitcast.1.meta_ref.rank_ref, bf16[4,136,3584]{2,1,0:T(8,128)(2,1)} %get-tuple-element.31.refs_0_.refs_1_.refs_2_, bf16[896,2048]{1,0:T(8,128)(2,1)S(1)} %copy-done.3, bf16[896,2048]{1,0:T(8,128)(2,1)} %get-tuple-element.32.refs_4_.refs_2_, ...), custom_call_target="tpu_custom_call" | custom-call | flops 1996488704 | bytes 15654912 | tf_op jit(solution)/shard_map/gate_up_product/pallas_call | solution.py:270
  112.5 11.2 %gate_up_product.2 = (f32[136,2048]{1,0:T(8,128)S(1)}, bf16[136,2048]{1,0:T(8,128)(2,1)S(1)}, f32[136,2048]{1,0:T(8,128)S(1)}) custom-call(s32[1]{0:T(128)} %bitcast.1.meta_ref.rank_ref, bf16[4,136,3584]{2,1,0:T(8,128)(2,1)} %get-tuple-element.31.refs_0_.refs_1_.refs_2_, bf16[4,136,3584]{2,1,0:T(8,128)(2,1)} %get-tuple-element.31.refs_0_.refs_1_.refs_2_, ...), custom_call_target="tpu_custom_call" | custom-call | flops 5989466112 | bytes 17604608 | tf_op jit(solution)/shard_map/gate_up_product/pallas_call | solution.py:270
  130.1 4.3 %collective-permute-done.12.refs_0_ = bf16[512,896]{1,0:T(8,128)(2,1)} collective-permute-done((bf16[512,896]{1,0:T(8,128)(2,1)}, bf16[512,896]{1,0:T(8,128)(2,1)}, u32[]{:S(2)}, u32[]{:S(2)}) %collective-permute-start.12) | collective-permute-done | bytes 917536 | tf_op jit(solution)/shard_map/ppermute | solution.py:19
  143.2 5.6 %down_product.3.refs_1_ = bf16[2,136,3584]{2,1,0:T(8,128)(2,1)} custom-call(s32[1]{0:T(128)} %bitcast.1.meta_ref.rank_ref, bf16[136,1024]{1,0:T(8,128)(2,1)} %fusion.2.refs_1_.hidden_ref, bf16[1024,896]{1,0:T(8,128)(2,1)} %refs_0_.5, bf16[512,896]{1,0:T(8,128)(2,1)} %after.12.refs_1_, bf16[512,896]{1,0:T(8,128)(2,1)} %after.14.refs_2_, ...), custom_call_target="tpu_custom_call" | custom-call | flops 998244352 | bytes 8593408 | tf_op jit(solution)/shard_map/down_product/pallas_call | solution.py:343
  152.3 4.9 %all-to-all-start.1 = ((bf16[2,136,3584]{2,1,0:T(8,128)(2,1)}), bf16[2,136,3584]{2,1,0:T(8,128)(2,1)}, u32[]{:S(2)}, u32[]{:S(2)}) async-start(bf16[2,136,3584]{2,1,0:T(8,128)(2,1)} %down_product.3.refs_1_), calls=%async_computation.1 | async-start | bytes 3899392 | tf_op jit(solution)/shard_map/all_to_all | solution.py:571
  157.3 5.6 %down_product.4.refs_1_ = bf16[136,3584]{1,0:T(8,128)(2,1)} custom-call(s32[1]{0:T(128)} %bitcast.1.meta_ref.rank_ref, bf16[136,1024]{1,0:T(8,128)(2,1)} %get-tuple-element.47.hidden_ref, bf16[1024,896]{1,0:T(8,128)(2,1)} %refs_0_.5, bf16[512,896]{1,0:T(8,128)(2,1)} %after.12.refs_1_, bf16[512,896]{1,0:T(8,128)(2,1)} %after.14.refs_2_, ...), custom_call_target="tpu_custom_call" | custom-call | flops 998244352 | bytes 8593408 | tf_op jit(solution)/shard_map/down_product/pallas_call | solution.py:343
  166.1 4.5 %collective-permute-done.19.refs_0_ = bf16[136,2048]{1,0:T(8,128)(2,1)S(1)} collective-permute-done((bf16[136,2048]{1,0:T(8,128)(2,1)}, bf16[136,2048]{1,0:T(8,128)(2,1)S(1)}, u32[]{:S(2)}, u32[]{:S(2)}) %collective-permute-start.19) | collective-permute-done | bytes 557088 | tf_op jit(solution)/shard_map/ppermute | solution.py:19
  178.7 3.8 %collective-permute-start.23 = (bf16[136,3584]{1,0:T(8,128)(2,1)}, bf16[136,3584]{1,0:T(8,128)(2,1)}, u32[]{:S(2)}, u32[]{:S(2)}) collective-permute-start(bf16[136,3584]{1,0:T(8,128)(2,1)} %down_product.4.refs_1_), channel_id=1, source_target_pairs={{0,12},{1,13},{2,14},{3,15},{4,8},{5,9},{6,10},{7,11},{8,4},{9,5},... | collective-permute-start | bytes 2924552 | tf_op jit(solution)/shard_map/ppermute | solution.py:19
  182.5 12.0 %collective-permute-done.20 = bf16[136,1024]{1,0:T(8,128)(2,1)S(1)} collective-permute-done((bf16[136,1024]{1,0:T(8,128)(2,1)S(1)}, bf16[136,1024]{1,0:T(8,128)(2,1)S(1)}, u32[]{:S(2)}, u32[]{:S(2)}) %collective-permute-start.20) | collective-permute-done | bytes 278560 | tf_op jit(solution)/shard_map/ppermute | solution.py:19
  195.4 6.7 %down_product.5 = (bf16[136,3584]{1,0:T(8,128)(2,1)}, bf16[136,3584]{1,0:T(8,128)(2,1)}) custom-call(s32[1]{0:T(128)} %bitcast.1.meta_ref.rank_ref, bf16[272,1024]{1,0:T(8,128)(2,1)} %pad_maximum_fusion.3.hidden_ref, bf16[1024,896]{1,0:T(8,128)(2,1)} %refs_0_.5, bf16[512,896]{1,0:T(8,128)(2,1)} %after.12.refs_1_, bf16[512,896]{1,0:T(8,128)(2,1)} %after.14.refs_2_, ...), custom_call_target="tpu_custom_call" | custom-call | flops 1996488704 | bytes 9846784 | tf_op jit(solution)/shard_map/down_product/pallas_call | solution.py:343
  205.0 21.5 %collective-permute-done.17.refs_3_ = bf16[2,448,576]{2,1,0:T(8,128)(2,1)} collective-permute-done((bf16[2,448,576]{2,1,0:T(8,128)(2,1)}, bf16[2,448,576]{2,1,0:T(8,128)(2,1)}, u32[]{:S(2)}, u32[]{:S(2)}) %collective-permute-start.17) | collective-permute-done | bytes 1032224 | tf_op jit(solution)/shard_map/ppermute | solution.py:19
  228.1 5.6 %latent_product.1 = (bf16[256,576]{1,0:T(8,128)(2,1)S(1)}, f32[256,576]{1,0:T(8,128)S(1)}) custom-call(s32[1]{0:T(128)} %bitcast.1.meta_ref.rank_ref, bf16[8,256,448]{2,1,0:T(8,128)(2,1)S(1)} %copy-done.4, bf16[8,256,448]{2,1,0:T(8,128)(2,1)S(1)} %copy-done, bf16[2,448,576]{2,1,0:T(8,128)(2,1)S(1)} %pad_maximum_fusion.refs_0_, ...), custom_call_target="tpu_custom_call" | custom-call | flops 2113929216 | bytes 7798784 | tf_op jit(solution)/shard_map/latent_product/pallas_call | solution.py:420
  235.3 5.1 %unpack_rows.2.refs_1_.refs_2_ = bf16[256,7168]{1,0:T(8,128)(2,1)} custom-call(s32[1]{0:T(128)} %bitcast.1.meta_ref.rank_ref, s32[16]{0:T(128)} %lengths_ref.5, s32[1,256]{1,0:T(1,128)} %bitcast.9, f32[1,256]{1,0:T(1,128)} %bitcast.11, bf16[136,3584]{1,0:T(8,128)(2,1)} %get-tuple-element.48.refs_0_, bf16[2,136,3584]{2,1,0:T(8,128)(2,1)} %all-to-all-done.1.refs_1_), custom_call_target="tpu_custom_call" | custom-call | flops 939524096 | bytes 3670016 | tf_op jit(solution)/shard_map/unpack_rows/pallas_call | solution.py:175
  243.5 5.1 %unpack_rows.3 = bf16[256,7168]{1,0:T(8,128)(2,1)} custom-call(s32[1]{0:T(128)} %bitcast.1.meta_ref.rank_ref, s32[16]{0:T(128)} %lengths_ref.5, s32[1,256]{1,0:T(1,128)} %bitcast.10, f32[1,256]{1,0:T(1,128)} %bitcast.12, bf16[136,3584]{1,0:T(8,128)(2,1)} %collective-permute-done.22.refs_0_, ...), custom_call_target="tpu_custom_call", output_to_operand_aliasing={{}: (6, {})} | custom-call | flops 939524096 | bytes 3670016 | tf_op jit(solution)/shard_map/unpack_rows/pallas_call | solution.py:175
  (131 shorter events, 58.1 us)
Async XLA Ops:
  0.6 81.5 %collective-permute-start = (bf16[896,2048]{1,0:T(8,128)(2,1)}, bf16[896,2048]{1,0:T(8,128)(2,1)}, u32[]{:S(2)}, u32[]{:S(2)}) collective-permute-start(bf16[896,2048]{1,0:T(8,128)(2,1)} %refs_1_.1), channel_id=1, source_target_pairs={{0,2},{1,3},{2,0},{3,1},{4,6},{5,7},{6,4},{7,5},{8,10},{9,11},{10,... | collective-permute-start | bytes 11010056 | tf_op jit(solution)/shard_map/ppermute | solution.py:19
  3.2 8.4 %collective-permute-start.2 = (bf16[1,224,576]{2,1,0:T(8,128)(2,1)S(1)}, bf16[1,224,576]{2,1,0:T(8,128)(2,1)S(1)}, u32[]{:S(2)}, u32[]{:S(2)}) collective-permute-start(bf16[1,224,576]{2,1,0:T(8,128)(2,1)S(1)} %dynamic-slice_bitcast_fusion), channel_id=1, source_target_pairs={{0,4},{1,5},{2,6},{3,7},{4,0},{5,1},{6,2},{7,3},{8,12},{9,13},{10,... | collective-permute-start | bytes 774152 | tf_op jit(solution)/shard_map/ppermute | solution.py:19
  12.3 88.0 %all-to-all-start = ((bf16[4,136,3584]{2,1,0:T(8,128)(2,1)}), bf16[4,136,3584]{2,1,0:T(8,128)(2,1)}, u32[]{:S(2)}, u32[]{:S(2)}) async-start(bf16[4,136,3584]{2,1,0:T(8,128)(2,1)} %after.10), calls=%async_computation | async-start | bytes 7798784 | tf_op jit(solution)/shard_map/all_to_all | solution.py:527
  27.9 5.8 %collective-permute-start.1 = (bf16[8,256,448]{1,2,0:T(8,128)(2,1)S(1)}, bf16[8,256,448]{1,2,0:T(8,128)(2,1)}, u32[]{:S(2)}, u32[]{:S(2)}) collective-permute-start(bf16[8,256,448]{1,2,0:T(8,128)(2,1)S(1)} %copy.40), channel_id=1, source_target_pairs={{0,1},{1,0},{2,3},{3,2},{4,5},{5,4},{6,7},{7,6},{8,9},{9,8},{10,11... | collective-permute-start | bytes 5505032 | tf_op jit(solution)/shard_map/ppermute | solution.py:19
  28.0 68.0 %collective-permute-start.3 = (bf16[896,2048]{1,0:T(8,128)(2,1)}, bf16[896,2048]{1,0:T(8,128)(2,1)}, u32[]{:S(2)}, u32[]{:S(2)}) collective-permute-start(bf16[896,2048]{1,0:T(8,128)(2,1)} %refs_1_.1), channel_id=1, source_target_pairs={{0,1},{1,0},{2,3},{3,2},{4,5},{5,4},{6,7},{7,6},{8,9},{9,8},{10,11... | collective-permute-start | bytes 11010056 | tf_op jit(solution)/shard_map/ppermute | solution.py:19
  82.1 18.2 %collective-permute-start.4 = (bf16[896,2048]{1,0:T(8,128)(2,1)}, bf16[896,2048]{1,0:T(8,128)(2,1)}, u32[]{:S(2)}, u32[]{:S(2)}) collective-permute-start(bf16[896,2048]{1,0:T(8,128)(2,1)} %get-tuple-element.30.refs_5_.refs_3_.refs_1_), channel_id=1, source_target_pairs={{0,1},{1,0},{2,3},{3,2},{4,5},{5,4},{6,7},{7,6},{8,9},{9,8},{10,11... | collective-permute-start | bytes 11010056 | tf_op jit(solution)/shard_map/ppermute | solution.py:19
  84.7 6.4 %collective-permute-start.7 = (bf16[512,896]{1,0:T(8,128)(2,1)S(1)}, bf16[512,896]{1,0:T(8,128)(2,1)S(1)}, u32[]{:S(2)}, u32[]{:S(2)}) collective-permute-start(bf16[512,896]{1,0:T(8,128)(2,1)S(1)} %get-tuple-element.57), channel_id=1, source_target_pairs={{0,1},{1,0},{2,3},{3,2},{4,5},{5,4},{6,7},{7,6},{8,9},{9,8},{10,11... | collective-permute-start | bytes 2752520 | tf_op jit(solution)/shard_map/ppermute | solution.py:19
  84.7 9.8 %collective-permute-start.11 = (bf16[512,896]{1,0:T(8,128)(2,1)}, bf16[512,896]{1,0:T(8,128)(2,1)S(1)}, u32[]{:S(2)}, u32[]{:S(2)}) collective-permute-start(bf16[512,896]{1,0:T(8,128)(2,1)} %get-tuple-element.56), channel_id=1, source_target_pairs={{0,1},{1,0},{2,3},{3,2},{4,5},{5,4},{6,7},{7,6},{8,9},{9,8},{10,11... | collective-permute-start | bytes 2752520 | tf_op jit(solution)/shard_map/ppermute | solution.py:19
  92.1 34.4 %collective-permute-start.8 = (bf16[512,896]{1,0:T(8,128)(2,1)}, bf16[512,896]{1,0:T(8,128)(2,1)S(1)}, u32[]{:S(2)}, u32[]{:S(2)}) collective-permute-start(bf16[512,896]{1,0:T(8,128)(2,1)} %after.12.refs_1_), channel_id=1, source_target_pairs={{0,2},{1,3},{2,0},{3,1},{4,6},{5,7},{6,4},{7,5},{8,10},{9,11},{10,... | collective-permute-start | bytes 2752520 | tf_op jit(solution)/shard_map/ppermute | solution.py:19
  95.5 39.0 %collective-permute-start.12 = (bf16[512,896]{1,0:T(8,128)(2,1)}, bf16[512,896]{1,0:T(8,128)(2,1)}, u32[]{:S(2)}, u32[]{:S(2)}) collective-permute-start(bf16[512,896]{1,0:T(8,128)(2,1)} %after.14.refs_2_), channel_id=1, source_target_pairs={{0,2},{1,3},{2,0},{3,1},{4,6},{5,7},{6,4},{7,5},{8,10},{9,11},{10,... | collective-permute-start | bytes 2752520 | tf_op jit(solution)/shard_map/ppermute | solution.py:19
  100.3 26.2 %collective-permute-start.5 = (bf16[2,224,576]{2,1,0:T(8,128)(2,1)}, bf16[2,224,576]{2,1,0:T(8,128)(2,1)}, u32[]{:S(2)}, u32[]{:S(2)}) collective-permute-start(bf16[2,224,576]{2,1,0:T(8,128)(2,1)} %after.11), channel_id=1, source_target_pairs={{0,8},{1,9},{2,10},{3,11},{4,12},{5,13},{6,14},{7,15},{8,0},{9,1},... | collective-permute-start | bytes 1548296 | tf_op jit(solution)/shard_map/ppermute | solution.py:19
  112.4 26.0 %collective-permute-start.6 = (bf16[136,2048]{1,0:T(8,128)(2,1)S(1)}, bf16[136,2048]{1,0:T(8,128)(2,1)}, u32[]{:S(2)}, u32[]{:S(2)}) collective-permute-start(bf16[136,2048]{1,0:T(8,128)(2,1)S(1)} %gate_up_product.3), channel_id=1, source_target_pairs={{0,4},{1,5},{2,6},{3,7},{4,0},{5,1},{6,2},{7,3},{8,12},{9,13},{10,... | collective-permute-start | bytes 1671176 | tf_op jit(solution)/shard_map/ppermute | solution.py:19
  129.6 8.9 %collective-permute-start.9 = (bf16[256,896]{1,0:T(8,128)(2,1)}, bf16[256,896]{1,0:T(8,128)(2,1)S(1)}, u32[]{:S(2)}, u32[]{:S(2)}) collective-permute-start(bf16[256,896]{1,0:T(8,128)(2,1)} %get-tuple-element.61), channel_id=1, source_target_pairs={{0,1},{1,0},{2,3},{3,2},{4,5},{5,4},{6,7},{7,6},{8,9},{9,8},{10,11... | collective-permute-start | bytes 1376264 | tf_op jit(solution)/shard_map/ppermute | solution.py:19
  129.6 8.9 %collective-permute-start.10 = (bf16[256,896]{1,0:T(8,128)(2,1)}, bf16[256,896]{1,0:T(8,128)(2,1)}, u32[]{:S(2)}, u32[]{:S(2)}) collective-permute-start(bf16[256,896]{1,0:T(8,128)(2,1)} %get-tuple-element.60), channel_id=1, source_target_pairs={{0,1},{1,0},{2,3},{3,2},{4,5},{5,4},{6,7},{7,6},{8,9},{9,8},{10,11... | collective-permute-start | bytes 1376264 | tf_op jit(solution)/shard_map/ppermute | solution.py:19
  141.3 21.5 %collective-permute-start.15 = (bf16[3,224,576]{2,1,0:T(8,128)(2,1)}, bf16[3,224,576]{2,1,0:T(8,128)(2,1)}, u32[]{:S(2)}, u32[]{:S(2)}) collective-permute-start(bf16[3,224,576]{2,1,0:T(8,128)(2,1)} %after.16), channel_id=1, source_target_pairs={{0,16},{16,0},{1,17},{17,1},{2,18},{18,2},{3,19},{19,3},{4,20},{20... | collective-permute-start | bytes 2322440 | tf_op jit(solution)/shard_map/ppermute | solution.py:585
  142.8 8.4 %collective-permute-start.18 = (bf16[136,1024]{1,0:T(8,128)(2,1)S(1)}, bf16[136,1024]{1,0:T(8,128)(2,1)S(1)}, u32[]{:S(2)}, u32[]{:S(2)}) collective-permute-start(bf16[136,1024]{1,0:T(8,128)(2,1)S(1)} %copy-done.20), channel_id=1, source_target_pairs={{0,4},{1,5},{2,6},{3,7},{4,0},{5,1},{6,2},{7,3},{8,12},{9,13},{10,... | collective-permute-start | bytes 835592 | tf_op jit(solution)/shard_map/ppermute | solution.py:19
  151.9 18.8 %collective-permute-start.19 = (bf16[136,2048]{1,0:T(8,128)(2,1)}, bf16[136,2048]{1,0:T(8,128)(2,1)S(1)}, u32[]{:S(2)}, u32[]{:S(2)}) collective-permute-start(bf16[136,2048]{1,0:T(8,128)(2,1)} %get-tuple-element.46), channel_id=1, source_target_pairs={{0,4},{1,5},{2,6},{3,7},{4,0},{5,1},{6,2},{7,3},{8,12},{9,13},{10,... | collective-permute-start | bytes 1671176 | tf_op jit(solution)/shard_map/ppermute | solution.py:19
  152.3 83.0 %all-to-all-start.1 = ((bf16[2,136,3584]{2,1,0:T(8,128)(2,1)}), bf16[2,136,3584]{2,1,0:T(8,128)(2,1)}, u32[]{:S(2)}, u32[]{:S(2)}) async-start(bf16[2,136,3584]{2,1,0:T(8,128)(2,1)} %down_product.3.refs_1_), calls=%async_computation.1 | async-start | bytes 3899392 | tf_op jit(solution)/shard_map/all_to_all | solution.py:571
  172.9 21.6 %collective-permute-start.20 = (bf16[136,1024]{1,0:T(8,128)(2,1)S(1)}, bf16[136,1024]{1,0:T(8,128)(2,1)S(1)}, u32[]{:S(2)}, u32[]{:S(2)}) collective-permute-start(bf16[136,1024]{1,0:T(8,128)(2,1)S(1)} %fusion.1), channel_id=1, source_target_pairs={{0,4},{1,5},{2,6},{3,7},{4,0},{5,1},{6,2},{7,3},{8,12},{9,13},{10,... | collective-permute-start | bytes 835592 | tf_op jit(solution)/shard_map/ppermute | solution.py:19
  176.7 28.3 %collective-permute-start.16 = (bf16[2,448,576]{2,1,0:T(8,128)(2,1)S(1)}, bf16[2,448,576]{2,1,0:T(8,128)(2,1)}, u32[]{:S(2)}, u32[]{:S(2)}) collective-permute-start(bf16[2,448,576]{2,1,0:T(8,128)(2,1)S(1)} %pad_maximum_fusion.refs_0_), channel_id=1, source_target_pairs={{0,2},{1,3},{2,0},{3,1},{4,6},{5,7},{6,4},{7,5},{8,10},{9,11},{10,... | collective-permute-start | bytes 3096584 | tf_op jit(solution)/shard_map/ppermute | solution.py:19
  178.2 48.3 %collective-permute-start.17 = (bf16[2,448,576]{2,1,0:T(8,128)(2,1)}, bf16[2,448,576]{2,1,0:T(8,128)(2,1)}, u32[]{:S(2)}, u32[]{:S(2)}) collective-permute-start(bf16[2,448,576]{2,1,0:T(8,128)(2,1)} %slice.70.refs_1_), channel_id=1, source_target_pairs={{0,2},{1,3},{2,0},{3,1},{4,6},{5,7},{6,4},{7,5},{8,10},{9,11},{10,... | collective-permute-start | bytes 3096584 | tf_op jit(solution)/shard_map/ppermute | solution.py:19
  178.7 64.8 %collective-permute-start.23 = (bf16[136,3584]{1,0:T(8,128)(2,1)}, bf16[136,3584]{1,0:T(8,128)(2,1)}, u32[]{:S(2)}, u32[]{:S(2)}) collective-permute-start(bf16[136,3584]{1,0:T(8,128)(2,1)} %down_product.4.refs_1_), channel_id=1, source_target_pairs={{0,12},{1,13},{2,14},{3,15},{4,8},{5,9},{6,10},{7,11},{8,4},{9,5},... | collective-permute-start | bytes 2924552 | tf_op jit(solution)/shard_map/ppermute | solution.py:19
  202.1 41.4 %collective-permute-start.22 = (bf16[136,3584]{1,0:T(8,128)(2,1)}, bf16[136,3584]{1,0:T(8,128)(2,1)}, u32[]{:S(2)}, u32[]{:S(2)}) collective-permute-start(bf16[136,3584]{1,0:T(8,128)(2,1)} %get-tuple-element.49), channel_id=1, source_target_pairs={{0,4},{1,5},{2,6},{3,7},{4,0},{5,1},{6,2},{7,3},{8,12},{9,13},{10,... | collective-permute-start | bytes 2924552 | tf_op jit(solution)/shard_map/ppermute | solution.py:19
  240.4 8.2 %collective-permute-start.21 = (bf16[256,576]{1,0:T(8,128)(2,1)}, bf16[256,576]{1,0:T(8,128)(2,1)S(1)}, u32[]{:S(2)}, u32[]{:S(2)}) collective-permute-start(bf16[256,576]{1,0:T(8,128)(2,1)} %after.19), channel_id=1, source_target_pairs={{0,1},{1,0},{2,3},{3,2},{4,5},{5,4},{6,7},{7,6},{8,9},{9,8},{10,11... | collective-permute-start | bytes 884744 | tf_op jit(solution)/shard_map/ppermute | solution.py:19
  (27 other events, 93.0 us)

commit v7 on v5

--- a/solution.py
+++ b/solution.py
@@ -488,14 +488,15 @@
     latent_1 = swapped(sent, QUAD)
     packed = after(packed, latent_1)
     gate_2, mine, other = together(swapped(gate_up, 2), mine, swapped(other, 1))
-    down_1 = swapped(down_weight, 1)
+    mid = down_weight.shape[0] // 2
+    down_1 = [swapped(half_rows, 1) for half_rows in (down_weight[:mid], down_weight[mid:])]
     arrived, gate_1, gate_3 = together(
         lax.all_to_all(packed, "dp", 0, 0, axis_index_groups=columns, tiled=True),
         swapped(gate_up, 1),
         swapped(gate_2, 1),
     )
-    down_1 = after(down_1, gate_2)
-    down_3 = swapped(down_1, 2)
+    down_1 = [after(piece, gate_2) for piece in down_1]
+    down_3 = [swapped(piece, 2) for piece in down_1]
     if middle:
         cut = swapped(after(jnp.concatenate([sent, latent_1], axis=0), arrived), 2 * QUAD)
     else:
@@ -515,11 +516,15 @@
     )
     if middle:
         ours, cut = together(ours, cut)
-    down_3 = after(down_3, ours)
-    split = down_3.shape[0] // 4
-    down_2 = [swapped(down_3[n * split : (n + 1) * split], 1) for n in range(4)]
+    down_3 = [after(piece, ours) for piece in down_3]
+    quarter = mid // 2
+    down_2 = [
+        swapped(part, 1)
+        for piece in down_3
+        for part in (piece[:quarter], piece[quarter:])
+    ]
     came, *down_2 = together(swapped(theirs, QUAD), *down_2)
-    weight_out = [down_weight, down_1, *down_2, down_3]
+    weight_out = [down_weight, *down_1, *down_2, *down_3]
 
     def activated(own, other):
         summed = own + other.astype(jnp.float32)
@@ -531,11 +536,11 @@
     (made_own,) = down_product(meta, hidden, weight_out, experts - 1, True)
     halves = [[GROUP * e + low for e in range(experts)] for low in range(GROUP)]
     near = lax.all_to_all(made_own, "dp", 0, 0, axis_index_groups=halves, tiled=True)
-    partner = after(partner, made_own)
+    partner, theirs_near = together(after(partner, made_own), theirs_near)
     made = down_product(meta, partner, weight_out, experts - 1, False)
     far = [swapped(made[n - 1], QUAD * (2 * n + 1)) for n in away]
 
-    came_near = after(swapped(after(theirs_near, hidden), QUAD), made[0])
+    came_near = after(swapped(theirs_near, QUAD), made[0])
     hidden_near = activated(ours_near, came_near)
     both = jnp.concatenate([hidden_near, swapped(hidden_near, QUAD)], axis=0)
     here, there = down_product(meta, both, weight_out, 2, False)

time: 257 us -> 255 us (level)
  waiting for transfers between devices: 121 us -> 111 us
  local copies, waits for them, and re-layouts: 24.2 us -> 30.9 us
    ppermute x21 -> x23, waiting for transfers between devices: 116 us -> 107 us  [swapped(): lax.ppermute(block, 'dp', [(low, low ^ bits) for low in range(count)])]
    unnamed x43 -> x51, local copies, waits for them, and re-layouts: 12.8 us -> 16.5 us
    slice x1 -> x3, local copies, waits for them, and re-layouts: 1.58 us -> 4.52 us  [the longest x2 3.41 us: shards(): piece[quarter:]]
    ppermute x21 -> x23, starting transfers between devices: 18.6 us -> 19 us  [swapped(): lax.ppermute(block, 'dp', [(low, low ^ bits) for low in range(count)])]
  transfers between devices with their start and end apart: 24 -> 26, of which waited for: 16 -> 13; matrix products, arithmetic and copies ran while one was open for 8% -> 9% of each run, Pallas kernels for 26% -> 26%
where the time goes in v7:
time: 255 us; the launch traced here: 251 us
  waiting for transfers between devices  111 us (44%)
  Pallas kernels  66 us (26%)
  local copies, waits for them, and re-layouts  30.9 us (12%)
  starting transfers between devices  30.7 us (12%)
  other arithmetic  11.3 us (4%)
    ppermute x23, waiting for transfers between devices, swapped(): lax.ppermute(block, 'dp', [(low, low ^ bits) for low in range(count)])  107 us
    ppermute x23, starting transfers between devices, swapped(): lax.ppermute(block, 'dp', [(low, low ^ bits) for low in range(count)])  19 us
    pallas_call x2, Pallas kernels, gate_up_product(): pl.pallas_call(functools.partial(gate_up_body, [len(numbers) for numbers,...  18 us
    pallas_call x3, Pallas kernels, down_product(): pl.pallas_call(functools.partial(down_body, places, joined), grid_spec=pl...  17.9 us
    unnamed x51, local copies, waits for them, and re-layouts  16.5 us
    pallas_call x2, Pallas kernels, unpack(): pl.pallas_call(functools.partial(unpack_body, near), grid_spec=pltpu.Pref...  11.1 us
    pallas_call x1, Pallas kernels, core_split(): pl.pallas_call(core_split_body, grid_spec=pltpu.PrefetchScalarGridSpec(nu...  7.04 us
    pallas_call x1, Pallas kernels, pack(): pl.pallas_call(pack_body, grid_spec=pltpu.PrefetchScalarGridSpec(num_scal...  6.36 us
  transfers between devices with their start and end apart: 26, of which 13 were waited for; matrix products, arithmetic and copies ran while one was open for 9% of the time, Pallas kernels for 26%

profile of v7, /device:TPU:8, one launch (start us, length us, event | category | flops | bytes accessed | tf_op | source)
XLA Modules:
  0.0 250.9 jit_solution(16319645661929791148)
XLA Ops:
  3.7 6.4 %pack_rows.1.refs_0_ = bf16[4,136,3584]{2,1,0:T(8,128)(2,1)} custom-call(s32[1]{0:T(128)} %bitcast.1.meta_ref.rank_ref, s32[16]{0:T(128)} %lengths_ref.5, s32[1,256]{1,0:T(1,128)} %bitcast.8, bf16[256,7168]{1,0:T(8,128)(2,1)} %high_ref.1, bf16[256,7168]{1,0:T(8,128)(2,1)} %high_ref.1), custom_call_target="tpu_custom_call" | custom-call | flops 1879048192 | bytes 7340032 | tf_op jit(solution)/shard_map/pack_rows/pallas_call | solution.py:81
  12.3 5.3 %all-to-all-start = ((bf16[4,136,3584]{2,1,0:T(8,128)(2,1)}), bf16[4,136,3584]{2,1,0:T(8,128)(2,1)}, u32[]{:S(2)}, u32[]{:S(2)}) async-start(bf16[4,136,3584]{2,1,0:T(8,128)(2,1)} %after.10), calls=%async_computation | async-start | bytes 7798784 | tf_op jit(solution)/shard_map/all_to_all | solution.py:494
  17.6 7.0 %core_split.1 = (bf16[8,256,448]{2,1,0:T(8,128)(2,1)}, bf16[8,256,448]{2,1,0:T(8,128)(2,1)}) custom-call(s32[1]{0:T(128)} %bitcast.1.meta_ref.rank_ref, bf16[256,7168]{1,0:T(8,128)(2,1)} %high_ref.1), custom_call_target="tpu_custom_call" | custom-call | tf_op jit(solution)/shard_map/core_split/pallas_call | solution.py:441
  24.6 3.3 %copy.40 = bf16[8,256,448]{1,2,0:T(8,128)(2,1)S(1)} copy(bf16[8,256,448]{2,1,0:T(8,128)(2,1)} %get-tuple-element.27) | data formatting | bytes 3670016 | tf_op jit(solution)/shard_map/core_split/pallas_call | solution.py:441
  28.5 5.2 %collective-permute-done.1 = bf16[8,256,448]{1,2,0:T(8,128)(2,1)} collective-permute-done((bf16[8,256,448]{1,2,0:T(8,128)(2,1)S(1)}, bf16[8,256,448]{1,2,0:T(8,128)(2,1)}, u32[]{:S(2)}, u32[]{:S(2)}) %collective-permute-start.1) | collective-permute-done | bytes 1835040 | tf_op jit(solution)/shard_map/ppermute | solution.py:19
  33.7 3.8 %copy.41.refs_2_ = bf16[8,256,448]{2,1,0:T(8,128)(2,1)} copy(bf16[8,256,448]{1,2,0:T(8,128)(2,1)} %collective-permute-done.1) | data formatting | bytes 3670016 | tf_op jit(solution)/shard_map/ppermute | solution.py:19
  37.5 44.6 %collective-permute-done.refs_0_ = bf16[896,2048]{1,0:T(8,128)(2,1)} collective-permute-done((bf16[896,2048]{1,0:T(8,128)(2,1)}, bf16[896,2048]{1,0:T(8,128)(2,1)}, u32[]{:S(2)}, u32[]{:S(2)}) %collective-permute-start) | collective-permute-done | bytes 3670048 | tf_op jit(solution)/shard_map/ppermute | solution.py:19
  85.2 5.9 %collective-permute-done.7.refs_0_ = bf16[512,896]{1,0:T(8,128)(2,1)S(1)} collective-permute-done((bf16[512,896]{1,0:T(8,128)(2,1)S(1)}, bf16[512,896]{1,0:T(8,128)(2,1)S(1)}, u32[]{:S(2)}, u32[]{:S(2)}) %collective-permute-start.7) | collective-permute-done | bytes 917536 | tf_op jit(solution)/shard_map/ppermute | solution.py:19
  96.0 4.4 %all-to-all-done.refs_0_ = bf16[4,136,3584]{2,1,0:T(8,128)(2,1)} async-done(((bf16[4,136,3584]{2,1,0:T(8,128)(2,1)}), bf16[4,136,3584]{2,1,0:T(8,128)(2,1)}, u32[]{:S(2)}, u32[]{:S(2)}) %all-to-all-start) | async-done | bytes 3899424 | tf_op jit(solution)/shard_map/all_to_all | solution.py:494
  100.4 3.4 %collective-permute-start.5 = (bf16[2,224,576]{2,1,0:T(8,128)(2,1)}, bf16[2,224,576]{2,1,0:T(8,128)(2,1)}, u32[]{:S(2)}, u32[]{:S(2)}) collective-permute-start(bf16[2,224,576]{2,1,0:T(8,128)(2,1)} %after.11), channel_id=1, source_target_pairs={{0,8},{1,9},{2,10},{3,11},{4,12},{5,13},{6,14},{7,15},{8,0},{9,1},... | collective-permute-start | bytes 1548296 | tf_op jit(solution)/shard_map/ppermute | solution.py:19
  105.8 6.8 %gate_up_product.3 = bf16[136,2048]{1,0:T(8,128)(2,1)S(1)} custom-call(s32[1]{0:T(128)} %bitcast.1.meta_ref.rank_ref, bf16[4,136,3584]{2,1,0:T(8,128)(2,1)} %get-tuple-element.31.refs_0_.refs_1_.refs_2_, bf16[896,2048]{1,0:T(8,128)(2,1)S(1)} %copy-done.3, bf16[896,2048]{1,0:T(8,128)(2,1)} %get-tuple-element.32.refs_4_.refs_2_, ...), custom_call_target="tpu_custom_call" | custom-call | flops 1996488704 | bytes 15654912 | tf_op jit(solution)/shard_map/gate_up_product/pallas_call | solution.py:237
  112.7 11.2 %gate_up_product.2 = (f32[136,2048]{1,0:T(8,128)S(1)}, bf16[136,2048]{1,0:T(8,128)(2,1)S(1)}, f32[136,2048]{1,0:T(8,128)S(1)}) custom-call(s32[1]{0:T(128)} %bitcast.1.meta_ref.rank_ref, bf16[4,136,3584]{2,1,0:T(8,128)(2,1)} %get-tuple-element.31.refs_0_.refs_1_.refs_2_, bf16[4,136,3584]{2,1,0:T(8,128)(2,1)} %get-tuple-element.31.refs_0_.refs_1_.refs_2_, ...), custom_call_target="tpu_custom_call" | custom-call | flops 5989466112 | bytes 17604608 | tf_op jit(solution)/shard_map/gate_up_product/pallas_call | solution.py:237
  130.4 4.0 %collective-permute-done.12.refs_0_ = bf16[512,896]{1,0:T(8,128)(2,1)} collective-permute-done((bf16[512,896]{1,0:T(8,128)(2,1)}, bf16[512,896]{1,0:T(8,128)(2,1)}, u32[]{:S(2)}, u32[]{:S(2)}) %collective-permute-start.12) | collective-permute-done | bytes 917536 | tf_op jit(solution)/shard_map/ppermute | solution.py:19
  143.2 5.6 %down_product.3.refs_1_ = bf16[2,136,3584]{2,1,0:T(8,128)(2,1)} custom-call(s32[1]{0:T(128)} %bitcast.1.meta_ref.rank_ref, bf16[136,1024]{1,0:T(8,128)(2,1)} %fusion.2.refs_1_.hidden_ref, bf16[1024,896]{1,0:T(8,128)(2,1)} %refs_0_.5, bf16[512,896]{1,0:T(8,128)(2,1)} %after.12.refs_1_, bf16[512,896]{1,0:T(8,128)(2,1)} %after.14.refs_2_, ...), custom_call_target="tpu_custom_call" | custom-call | flops 998244352 | bytes 8593408 | tf_op jit(solution)/shard_map/down_product/pallas_call | solution.py:310
  152.3 4.9 %all-to-all-start.1 = ((bf16[2,136,3584]{2,1,0:T(8,128)(2,1)}), bf16[2,136,3584]{2,1,0:T(8,128)(2,1)}, u32[]{:S(2)}, u32[]{:S(2)}) async-start(bf16[2,136,3584]{2,1,0:T(8,128)(2,1)} %down_product.3.refs_1_), calls=%async_computation.1 | async-start | bytes 3899392 | tf_op jit(solution)/shard_map/all_to_all | solution.py:538
  157.3 5.6 %down_product.4.refs_1_ = bf16[136,3584]{1,0:T(8,128)(2,1)} custom-call(s32[1]{0:T(128)} %bitcast.1.meta_ref.rank_ref, bf16[136,1024]{1,0:T(8,128)(2,1)} %get-tuple-element.47.hidden_ref, bf16[1024,896]{1,0:T(8,128)(2,1)} %refs_0_.5, bf16[512,896]{1,0:T(8,128)(2,1)} %after.12.refs_1_, bf16[512,896]{1,0:T(8,128)(2,1)} %after.14.refs_2_, ...), custom_call_target="tpu_custom_call" | custom-call | flops 998244352 | bytes 8593408 | tf_op jit(solution)/shard_map/down_product/pallas_call | solution.py:310
  166.1 4.5 %collective-permute-done.19.refs_0_ = bf16[136,2048]{1,0:T(8,128)(2,1)S(1)} collective-permute-done((bf16[136,2048]{1,0:T(8,128)(2,1)}, bf16[136,2048]{1,0:T(8,128)(2,1)S(1)}, u32[]{:S(2)}, u32[]{:S(2)}) %collective-permute-start.19) | collective-permute-done | bytes 557088 | tf_op jit(solution)/shard_map/ppermute | solution.py:19
  178.7 3.8 %collective-permute-start.23 = (bf16[136,3584]{1,0:T(8,128)(2,1)}, bf16[136,3584]{1,0:T(8,128)(2,1)}, u32[]{:S(2)}, u32[]{:S(2)}) collective-permute-start(bf16[136,3584]{1,0:T(8,128)(2,1)} %down_product.4.refs_1_), channel_id=1, source_target_pairs={{0,12},{1,13},{2,14},{3,15},{4,8},{5,9},{6,10},{7,11},{8,4},{9,5},... | collective-permute-start | bytes 2924552 | tf_op jit(solution)/shard_map/ppermute | solution.py:19
  182.5 12.0 %collective-permute-done.20 = bf16[136,1024]{1,0:T(8,128)(2,1)S(1)} collective-permute-done((bf16[136,1024]{1,0:T(8,128)(2,1)S(1)}, bf16[136,1024]{1,0:T(8,128)(2,1)S(1)}, u32[]{:S(2)}, u32[]{:S(2)}) %collective-permute-start.20) | collective-permute-done | bytes 278560 | tf_op jit(solution)/shard_map/ppermute | solution.py:19
  195.4 6.7 %down_product.5 = (bf16[136,3584]{1,0:T(8,128)(2,1)}, bf16[136,3584]{1,0:T(8,128)(2,1)}) custom-call(s32[1]{0:T(128)} %bitcast.1.meta_ref.rank_ref, bf16[272,1024]{1,0:T(8,128)(2,1)} %pad_maximum_fusion.3.hidden_ref, bf16[1024,896]{1,0:T(8,128)(2,1)} %refs_0_.5, bf16[512,896]{1,0:T(8,128)(2,1)} %after.12.refs_1_, bf16[512,896]{1,0:T(8,128)(2,1)} %after.14.refs_2_, ...), custom_call_target="tpu_custom_call" | custom-call | flops 1996488704 | bytes 9846784 | tf_op jit(solution)/shard_map/down_product/pallas_call | solution.py:310
  205.0 21.5 %collective-permute-done.17.refs_3_ = bf16[2,448,576]{2,1,0:T(8,128)(2,1)} collective-permute-done((bf16[2,448,576]{2,1,0:T(8,128)(2,1)}, bf16[2,448,576]{2,1,0:T(8,128)(2,1)}, u32[]{:S(2)}, u32[]{:S(2)}) %collective-permute-start.17) | collective-permute-done | bytes 1032224 | tf_op jit(solution)/shard_map/ppermute | solution.py:19
  228.1 5.6 %latent_product.1 = (bf16[256,576]{1,0:T(8,128)(2,1)S(1)}, f32[256,576]{1,0:T(8,128)S(1)}) custom-call(s32[1]{0:T(128)} %bitcast.1.meta_ref.rank_ref, bf16[8,256,448]{2,1,0:T(8,128)(2,1)S(1)} %copy-done.4, bf16[8,256,448]{2,1,0:T(8,128)(2,1)S(1)} %copy-done, bf16[2,448,576]{2,1,0:T(8,128)(2,1)S(1)} %pad_maximum_fusion.refs_0_, ...), custom_call_target="tpu_custom_call" | custom-call | flops 2113929216 | bytes 7798784 | tf_op jit(solution)/shard_map/latent_product/pallas_call | solution.py:387
  235.3 5.6 %unpack_rows.2.refs_1_.refs_2_ = bf16[256,7168]{1,0:T(8,128)(2,1)} custom-call(s32[1]{0:T(128)} %bitcast.1.meta_ref.rank_ref, s32[16]{0:T(128)} %lengths_ref.5, s32[1,256]{1,0:T(1,128)} %bitcast.9, f32[1,256]{1,0:T(1,128)} %bitcast.11, bf16[136,3584]{1,0:T(8,128)(2,1)} %get-tuple-element.48.refs_0_, bf16[2,136,3584]{2,1,0:T(8,128)(2,1)} %all-to-all-done.1.refs_1_), custom_call_target="tpu_custom_call" | custom-call | flops 939524096 | bytes 3670016 | tf_op jit(solution)/shard_map/unpack_rows/pallas_call | solution.py:143
  243.5 5.5 %unpack_rows.3 = bf16[256,7168]{1,0:T(8,128)(2,1)} custom-call(s32[1]{0:T(128)} %bitcast.1.meta_ref.rank_ref, s32[16]{0:T(128)} %lengths_ref.5, s32[1,256]{1,0:T(1,128)} %bitcast.10, f32[1,256]{1,0:T(1,128)} %bitcast.12, bf16[136,3584]{1,0:T(8,128)(2,1)} %collective-permute-done.22.refs_0_, ...), custom_call_target="tpu_custom_call", output_to_operand_aliasing={{}: (6, {})} | custom-call | flops 939524096 | bytes 3670016 | tf_op jit(solution)/shard_map/unpack_rows/pallas_call | solution.py:143
  (131 shorter events, 57.2 us)
Async XLA Ops:
  0.6 81.5 %collective-permute-start = (bf16[896,2048]{1,0:T(8,128)(2,1)}, bf16[896,2048]{1,0:T(8,128)(2,1)}, u32[]{:S(2)}, u32[]{:S(2)}) collective-permute-start(bf16[896,2048]{1,0:T(8,128)(2,1)} %refs_1_.1), channel_id=1, source_target_pairs={{0,2},{1,3},{2,0},{3,1},{4,6},{5,7},{6,4},{7,5},{8,10},{9,11},{10,... | collective-permute-start | bytes 11010056 | tf_op jit(solution)/shard_map/ppermute | solution.py:19
  3.2 8.4 %collective-permute-start.2 = (bf16[1,224,576]{2,1,0:T(8,128)(2,1)S(1)}, bf16[1,224,576]{2,1,0:T(8,128)(2,1)S(1)}, u32[]{:S(2)}, u32[]{:S(2)}) collective-permute-start(bf16[1,224,576]{2,1,0:T(8,128)(2,1)S(1)} %dynamic-slice_bitcast_fusion), channel_id=1, source_target_pairs={{0,4},{1,5},{2,6},{3,7},{4,0},{5,1},{6,2},{7,3},{8,12},{9,13},{10,... | collective-permute-start | bytes 774152 | tf_op jit(solution)/shard_map/ppermute | solution.py:19
  12.3 88.1 %all-to-all-start = ((bf16[4,136,3584]{2,1,0:T(8,128)(2,1)}), bf16[4,136,3584]{2,1,0:T(8,128)(2,1)}, u32[]{:S(2)}, u32[]{:S(2)}) async-start(bf16[4,136,3584]{2,1,0:T(8,128)(2,1)} %after.10), calls=%async_computation | async-start | bytes 7798784 | tf_op jit(solution)/shard_map/all_to_all | solution.py:494
  27.9 5.8 %collective-permute-start.1 = (bf16[8,256,448]{1,2,0:T(8,128)(2,1)S(1)}, bf16[8,256,448]{1,2,0:T(8,128)(2,1)}, u32[]{:S(2)}, u32[]{:S(2)}) collective-permute-start(bf16[8,256,448]{1,2,0:T(8,128)(2,1)S(1)} %copy.40), channel_id=1, source_target_pairs={{0,1},{1,0},{2,3},{3,2},{4,5},{5,4},{6,7},{7,6},{8,9},{9,8},{10,11... | collective-permute-start | bytes 5505032 | tf_op jit(solution)/shard_map/ppermute | solution.py:19
  28.0 68.0 %collective-permute-start.3 = (bf16[896,2048]{1,0:T(8,128)(2,1)}, bf16[896,2048]{1,0:T(8,128)(2,1)}, u32[]{:S(2)}, u32[]{:S(2)}) collective-permute-start(bf16[896,2048]{1,0:T(8,128)(2,1)} %refs_1_.1), channel_id=1, source_target_pairs={{0,1},{1,0},{2,3},{3,2},{4,5},{5,4},{6,7},{7,6},{8,9},{9,8},{10,11... | collective-permute-start | bytes 11010056 | tf_op jit(solution)/shard_map/ppermute | solution.py:19
  82.1 18.3 %collective-permute-start.4 = (bf16[896,2048]{1,0:T(8,128)(2,1)}, bf16[896,2048]{1,0:T(8,128)(2,1)}, u32[]{:S(2)}, u32[]{:S(2)}) collective-permute-start(bf16[896,2048]{1,0:T(8,128)(2,1)} %get-tuple-element.30.refs_5_.refs_3_.refs_1_), channel_id=1, source_target_pairs={{0,1},{1,0},{2,3},{3,2},{4,5},{5,4},{6,7},{7,6},{8,9},{9,8},{10,11... | collective-permute-start | bytes 11010056 | tf_op jit(solution)/shard_map/ppermute | solution.py:19
  84.7 6.4 %collective-permute-start.7 = (bf16[512,896]{1,0:T(8,128)(2,1)S(1)}, bf16[512,896]{1,0:T(8,128)(2,1)S(1)}, u32[]{:S(2)}, u32[]{:S(2)}) collective-permute-start(bf16[512,896]{1,0:T(8,128)(2,1)S(1)} %get-tuple-element.57), channel_id=1, source_target_pairs={{0,1},{1,0},{2,3},{3,2},{4,5},{5,4},{6,7},{7,6},{8,9},{9,8},{10,11... | collective-permute-start | bytes 2752520 | tf_op jit(solution)/shard_map/ppermute | solution.py:19
  84.7 9.8 %collective-permute-start.11 = (bf16[512,896]{1,0:T(8,128)(2,1)}, bf16[512,896]{1,0:T(8,128)(2,1)S(1)}, u32[]{:S(2)}, u32[]{:S(2)}) collective-permute-start(bf16[512,896]{1,0:T(8,128)(2,1)} %get-tuple-element.56), channel_id=1, source_target_pairs={{0,1},{1,0},{2,3},{3,2},{4,5},{5,4},{6,7},{7,6},{8,9},{9,8},{10,11... | collective-permute-start | bytes 2752520 | tf_op jit(solution)/shard_map/ppermute | solution.py:19
  92.1 34.7 %collective-permute-start.8 = (bf16[512,896]{1,0:T(8,128)(2,1)}, bf16[512,896]{1,0:T(8,128)(2,1)S(1)}, u32[]{:S(2)}, u32[]{:S(2)}) collective-permute-start(bf16[512,896]{1,0:T(8,128)(2,1)} %after.12.refs_1_), channel_id=1, source_target_pairs={{0,2},{1,3},{2,0},{3,1},{4,6},{5,7},{6,4},{7,5},{8,10},{9,11},{10,... | collective-permute-start | bytes 2752520 | tf_op jit(solution)/shard_map/ppermute | solution.py:19
  95.5 39.0 %collective-permute-start.12 = (bf16[512,896]{1,0:T(8,128)(2,1)}, bf16[512,896]{1,0:T(8,128)(2,1)}, u32[]{:S(2)}, u32[]{:S(2)}) collective-permute-start(bf16[512,896]{1,0:T(8,128)(2,1)} %after.14.refs_2_), channel_id=1, source_target_pairs={{0,2},{1,3},{2,0},{3,1},{4,6},{5,7},{6,4},{7,5},{8,10},{9,11},{10,... | collective-permute-start | bytes 2752520 | tf_op jit(solution)/shard_map/ppermute | solution.py:19
  100.4 26.3 %collective-permute-start.5 = (bf16[2,224,576]{2,1,0:T(8,128)(2,1)}, bf16[2,224,576]{2,1,0:T(8,128)(2,1)}, u32[]{:S(2)}, u32[]{:S(2)}) collective-permute-start(bf16[2,224,576]{2,1,0:T(8,128)(2,1)} %after.11), channel_id=1, source_target_pairs={{0,8},{1,9},{2,10},{3,11},{4,12},{5,13},{6,14},{7,15},{8,0},{9,1},... | collective-permute-start | bytes 1548296 | tf_op jit(solution)/shard_map/ppermute | solution.py:19
  112.6 25.9 %collective-permute-start.6 = (bf16[136,2048]{1,0:T(8,128)(2,1)S(1)}, bf16[136,2048]{1,0:T(8,128)(2,1)}, u32[]{:S(2)}, u32[]{:S(2)}) collective-permute-start(bf16[136,2048]{1,0:T(8,128)(2,1)S(1)} %gate_up_product.3), channel_id=1, source_target_pairs={{0,4},{1,5},{2,6},{3,7},{4,0},{5,1},{6,2},{7,3},{8,12},{9,13},{10,... | collective-permute-start | bytes 1671176 | tf_op jit(solution)/shard_map/ppermute | solution.py:19
  129.9 8.6 %collective-permute-start.9 = (bf16[256,896]{1,0:T(8,128)(2,1)}, bf16[256,896]{1,0:T(8,128)(2,1)S(1)}, u32[]{:S(2)}, u32[]{:S(2)}) collective-permute-start(bf16[256,896]{1,0:T(8,128)(2,1)} %get-tuple-element.61), channel_id=1, source_target_pairs={{0,1},{1,0},{2,3},{3,2},{4,5},{5,4},{6,7},{7,6},{8,9},{9,8},{10,11... | collective-permute-start | bytes 1376264 | tf_op jit(solution)/shard_map/ppermute | solution.py:19
  129.9 8.6 %collective-permute-start.10 = (bf16[256,896]{1,0:T(8,128)(2,1)}, bf16[256,896]{1,0:T(8,128)(2,1)}, u32[]{:S(2)}, u32[]{:S(2)}) collective-permute-start(bf16[256,896]{1,0:T(8,128)(2,1)} %get-tuple-element.60), channel_id=1, source_target_pairs={{0,1},{1,0},{2,3},{3,2},{4,5},{5,4},{6,7},{7,6},{8,9},{9,8},{10,11... | collective-permute-start | bytes 1376264 | tf_op jit(solution)/shard_map/ppermute | solution.py:19
  141.3 21.5 %collective-permute-start.15 = (bf16[3,224,576]{2,1,0:T(8,128)(2,1)}, bf16[3,224,576]{2,1,0:T(8,128)(2,1)}, u32[]{:S(2)}, u32[]{:S(2)}) collective-permute-start(bf16[3,224,576]{2,1,0:T(8,128)(2,1)} %after.16), channel_id=1, source_target_pairs={{0,16},{16,0},{1,17},{17,1},{2,18},{18,2},{3,19},{19,3},{4,20},{20... | collective-permute-start | bytes 2322440 | tf_op jit(solution)/shard_map/ppermute | solution.py:552
  142.8 8.4 %collective-permute-start.18 = (bf16[136,1024]{1,0:T(8,128)(2,1)S(1)}, bf16[136,1024]{1,0:T(8,128)(2,1)S(1)}, u32[]{:S(2)}, u32[]{:S(2)}) collective-permute-start(bf16[136,1024]{1,0:T(8,128)(2,1)S(1)} %copy-done.20), channel_id=1, source_target_pairs={{0,4},{1,5},{2,6},{3,7},{4,0},{5,1},{6,2},{7,3},{8,12},{9,13},{10,... | collective-permute-start | bytes 835592 | tf_op jit(solution)/shard_map/ppermute | solution.py:19
  151.9 18.8 %collective-permute-start.19 = (bf16[136,2048]{1,0:T(8,128)(2,1)}, bf16[136,2048]{1,0:T(8,128)(2,1)S(1)}, u32[]{:S(2)}, u32[]{:S(2)}) collective-permute-start(bf16[136,2048]{1,0:T(8,128)(2,1)} %get-tuple-element.46), channel_id=1, source_target_pairs={{0,4},{1,5},{2,6},{3,7},{4,0},{5,1},{6,2},{7,3},{8,12},{9,13},{10,... | collective-permute-start | bytes 1671176 | tf_op jit(solution)/shard_map/ppermute | solution.py:19
  152.3 83.0 %all-to-all-start.1 = ((bf16[2,136,3584]{2,1,0:T(8,128)(2,1)}), bf16[2,136,3584]{2,1,0:T(8,128)(2,1)}, u32[]{:S(2)}, u32[]{:S(2)}) async-start(bf16[2,136,3584]{2,1,0:T(8,128)(2,1)} %down_product.3.refs_1_), calls=%async_computation.1 | async-start | bytes 3899392 | tf_op jit(solution)/shard_map/all_to_all | solution.py:538
  172.9 21.6 %collective-permute-start.20 = (bf16[136,1024]{1,0:T(8,128)(2,1)S(1)}, bf16[136,1024]{1,0:T(8,128)(2,1)S(1)}, u32[]{:S(2)}, u32[]{:S(2)}) collective-permute-start(bf16[136,1024]{1,0:T(8,128)(2,1)S(1)} %fusion.1), channel_id=1, source_target_pairs={{0,4},{1,5},{2,6},{3,7},{4,0},{5,1},{6,2},{7,3},{8,12},{9,13},{10,... | collective-permute-start | bytes 835592 | tf_op jit(solution)/shard_map/ppermute | solution.py:19
  176.7 28.3 %collective-permute-start.16 = (bf16[2,448,576]{2,1,0:T(8,128)(2,1)S(1)}, bf16[2,448,576]{2,1,0:T(8,128)(2,1)}, u32[]{:S(2)}, u32[]{:S(2)}) collective-permute-start(bf16[2,448,576]{2,1,0:T(8,128)(2,1)S(1)} %pad_maximum_fusion.refs_0_), channel_id=1, source_target_pairs={{0,2},{1,3},{2,0},{3,1},{4,6},{5,7},{6,4},{7,5},{8,10},{9,11},{10,... | collective-permute-start | bytes 3096584 | tf_op jit(solution)/shard_map/ppermute | solution.py:19
  178.2 48.3 %collective-permute-start.17 = (bf16[2,448,576]{2,1,0:T(8,128)(2,1)}, bf16[2,448,576]{2,1,0:T(8,128)(2,1)}, u32[]{:S(2)}, u32[]{:S(2)}) collective-permute-start(bf16[2,448,576]{2,1,0:T(8,128)(2,1)} %slice.70.refs_1_), channel_id=1, source_target_pairs={{0,2},{1,3},{2,0},{3,1},{4,6},{5,7},{6,4},{7,5},{8,10},{9,11},{10,... | collective-permute-start | bytes 3096584 | tf_op jit(solution)/shard_map/ppermute | solution.py:19
  178.7 64.8 %collective-permute-start.23 = (bf16[136,3584]{1,0:T(8,128)(2,1)}, bf16[136,3584]{1,0:T(8,128)(2,1)}, u32[]{:S(2)}, u32[]{:S(2)}) collective-permute-start(bf16[136,3584]{1,0:T(8,128)(2,1)} %down_product.4.refs_1_), channel_id=1, source_target_pairs={{0,12},{1,13},{2,14},{3,15},{4,8},{5,9},{6,10},{7,11},{8,4},{9,5},... | collective-permute-start | bytes 2924552 | tf_op jit(solution)/shard_map/ppermute | solution.py:19
  202.1 41.4 %collective-permute-start.22 = (bf16[136,3584]{1,0:T(8,128)(2,1)}, bf16[136,3584]{1,0:T(8,128)(2,1)}, u32[]{:S(2)}, u32[]{:S(2)}) collective-permute-start(bf16[136,3584]{1,0:T(8,128)(2,1)} %get-tuple-element.49), channel_id=1, source_target_pairs={{0,4},{1,5},{2,6},{3,7},{4,0},{5,1},{6,2},{7,3},{8,12},{9,13},{10,... | collective-permute-start | bytes 2924552 | tf_op jit(solution)/shard_map/ppermute | solution.py:19
  240.9 8.1 %collective-permute-start.21 = (bf16[256,576]{1,0:T(8,128)(2,1)}, bf16[256,576]{1,0:T(8,128)(2,1)S(1)}, u32[]{:S(2)}, u32[]{:S(2)}) collective-permute-start(bf16[256,576]{1,0:T(8,128)(2,1)} %after.19), channel_id=1, source_target_pairs={{0,1},{1,0},{2,3},{3,2},{4,5},{5,4},{6,7},{7,6},{8,9},{9,8},{10,11... | collective-permute-start | bytes 884744 | tf_op jit(solution)/shard_map/ppermute | solution.py:19
  (27 other events, 92.9 us)

commit v8 on v7

--- a/solution.py
+++ b/solution.py
@@ -536,11 +536,11 @@
     (made_own,) = down_product(meta, hidden, weight_out, experts - 1, True)
     halves = [[GROUP * e + low for e in range(experts)] for low in range(GROUP)]
     near = lax.all_to_all(made_own, "dp", 0, 0, axis_index_groups=halves, tiled=True)
-    partner, theirs_near = together(after(partner, made_own), theirs_near)
+    partner = after(partner, made_own)
     made = down_product(meta, partner, weight_out, experts - 1, False)
     far = [swapped(made[n - 1], QUAD * (2 * n + 1)) for n in away]
 
-    came_near = after(swapped(theirs_near, QUAD), made[0])
+    came_near = after(swapped(after(theirs_near, hidden), QUAD), made[0])
     hidden_near = activated(ours_near, came_near)
     both = jnp.concatenate([hidden_near, swapped(hidden_near, QUAD)], axis=0)
     here, there = down_product(meta, both, weight_out, 2, False)

time: 255 us -> 255 us (level)
    unnamed x51 -> x49, local copies, waits for them, and re-layouts: 16.5 us -> 15.5 us
  transfers between devices with their start and end apart: 26 -> 26, of which waited for: 13 -> 14; matrix products, arithmetic and copies ran while one was open for 9% -> 8% of each run, Pallas kernels for 26% -> 26%
where the time goes in v8:
time: 255 us; the launch traced here: 251 us
  waiting for transfers between devices  113 us (44%)
  Pallas kernels  65.8 us (26%)
  starting transfers between devices  30.9 us (12%)
  local copies, waits for them, and re-layouts  30 us (12%)
  other arithmetic  9.91 us (4%)
    ppermute x23, waiting for transfers between devices, swapped(): lax.ppermute(block, 'dp', [(low, low ^ bits) for low in range(count)])  109 us
    ppermute x23, starting transfers between devices, swapped(): lax.ppermute(block, 'dp', [(low, low ^ bits) for low in range(count)])  19.1 us
    pallas_call x2, Pallas kernels, gate_up_product(): pl.pallas_call(functools.partial(gate_up_body, [len(numbers) for numbers,...  18 us
    pallas_call x3, Pallas kernels, down_product(): pl.pallas_call(functools.partial(down_body, places, joined), grid_spec=pl...  17.8 us
    unnamed x49, local copies, waits for them, and re-layouts  15.5 us
    pallas_call x2, Pallas kernels, unpack(): pl.pallas_call(functools.partial(unpack_body, near), grid_spec=pltpu.Pref...  11.1 us
    pallas_call x1, Pallas kernels, core_split(): pl.pallas_call(core_split_body, grid_spec=pltpu.PrefetchScalarGridSpec(nu...  7.03 us
    pallas_call x1, Pallas kernels, pack(): pl.pallas_call(pack_body, grid_spec=pltpu.PrefetchScalarGridSpec(num_scal...  6.3 us
  transfers between devices with their start and end apart: 26, of which 14 were waited for; matrix products, arithmetic and copies ran while one was open for 8% of the time, Pallas kernels for 26%

profile of v8, /device:TPU:8, one launch (start us, length us, event | category | flops | bytes accessed | tf_op | source)
XLA Modules:
  0.0 250.8 jit_solution(16032136908472313241)
XLA Ops:
  3.7 6.3 %pack_rows.1.refs_0_ = bf16[4,136,3584]{2,1,0:T(8,128)(2,1)} custom-call(s32[1]{0:T(128)} %bitcast.1.meta_ref.rank_ref, s32[16]{0:T(128)} %lengths_ref.5, s32[1,256]{1,0:T(1,128)} %bitcast.8, bf16[256,7168]{1,0:T(8,128)(2,1)} %high_ref.1, bf16[256,7168]{1,0:T(8,128)(2,1)} %high_ref.1), custom_call_target="tpu_custom_call" | custom-call | flops 1879048192 | bytes 7340032 | tf_op jit(solution)/shard_map/pack_rows/pallas_call | solution.py:81
  12.3 5.3 %all-to-all-start = ((bf16[4,136,3584]{2,1,0:T(8,128)(2,1)}), bf16[4,136,3584]{2,1,0:T(8,128)(2,1)}, u32[]{:S(2)}, u32[]{:S(2)}) async-start(bf16[4,136,3584]{2,1,0:T(8,128)(2,1)} %after.11), calls=%async_computation | async-start | bytes 7798784 | tf_op jit(solution)/shard_map/all_to_all | solution.py:494
  17.6 7.0 %core_split.1 = (bf16[8,256,448]{2,1,0:T(8,128)(2,1)}, bf16[8,256,448]{2,1,0:T(8,128)(2,1)}) custom-call(s32[1]{0:T(128)} %bitcast.1.meta_ref.rank_ref, bf16[256,7168]{1,0:T(8,128)(2,1)} %high_ref.1), custom_call_target="tpu_custom_call" | custom-call | tf_op jit(solution)/shard_map/core_split/pallas_call | solution.py:441
  24.6 3.3 %copy.39 = bf16[8,256,448]{1,2,0:T(8,128)(2,1)S(1)} copy(bf16[8,256,448]{2,1,0:T(8,128)(2,1)} %get-tuple-element.25) | data formatting | bytes 3670016 | tf_op jit(solution)/shard_map/core_split/pallas_call | solution.py:441
  28.5 5.2 %collective-permute-done.1 = bf16[8,256,448]{1,2,0:T(8,128)(2,1)} collective-permute-done((bf16[8,256,448]{1,2,0:T(8,128)(2,1)S(1)}, bf16[8,256,448]{1,2,0:T(8,128)(2,1)}, u32[]{:S(2)}, u32[]{:S(2)}) %collective-permute-start.1) | collective-permute-done | bytes 1835040 | tf_op jit(solution)/shard_map/ppermute | solution.py:19
  33.7 3.8 %copy.40.refs_2_ = bf16[8,256,448]{2,1,0:T(8,128)(2,1)} copy(bf16[8,256,448]{1,2,0:T(8,128)(2,1)} %collective-permute-done.1) | data formatting | bytes 3670016 | tf_op jit(solution)/shard_map/ppermute | solution.py:19
  37.5 44.6 %collective-permute-done.refs_0_ = bf16[896,2048]{1,0:T(8,128)(2,1)} collective-permute-done((bf16[896,2048]{1,0:T(8,128)(2,1)}, bf16[896,2048]{1,0:T(8,128)(2,1)}, u32[]{:S(2)}, u32[]{:S(2)}) %collective-permute-start) | collective-permute-done | bytes 3670048 | tf_op jit(solution)/shard_map/ppermute | solution.py:19
  85.2 5.9 %collective-permute-done.7.refs_0_ = bf16[512,896]{1,0:T(8,128)(2,1)S(1)} collective-permute-done((bf16[512,896]{1,0:T(8,128)(2,1)S(1)}, bf16[512,896]{1,0:T(8,128)(2,1)S(1)}, u32[]{:S(2)}, u32[]{:S(2)}) %collective-permute-start.7) | collective-permute-done | bytes 917536 | tf_op jit(solution)/shard_map/ppermute | solution.py:19
  96.0 4.3 %all-to-all-done.refs_0_ = bf16[4,136,3584]{2,1,0:T(8,128)(2,1)} async-done(((bf16[4,136,3584]{2,1,0:T(8,128)(2,1)}), bf16[4,136,3584]{2,1,0:T(8,128)(2,1)}, u32[]{:S(2)}, u32[]{:S(2)}) %all-to-all-start) | async-done | bytes 3899424 | tf_op jit(solution)/shard_map/all_to_all | solution.py:494
  100.3 3.4 %collective-permute-start.5 = (bf16[2,224,576]{2,1,0:T(8,128)(2,1)}, bf16[2,224,576]{2,1,0:T(8,128)(2,1)}, u32[]{:S(2)}, u32[]{:S(2)}) collective-permute-start(bf16[2,224,576]{2,1,0:T(8,128)(2,1)} %after.12), channel_id=1, source_target_pairs={{0,8},{1,9},{2,10},{3,11},{4,12},{5,13},{6,14},{7,15},{8,0},{9,1},... | collective-permute-start | bytes 1548296 | tf_op jit(solution)/shard_map/ppermute | solution.py:19
  105.7 6.8 %gate_up_product.3 = bf16[136,2048]{1,0:T(8,128)(2,1)S(1)} custom-call(s32[1]{0:T(128)} %bitcast.1.meta_ref.rank_ref, bf16[4,136,3584]{2,1,0:T(8,128)(2,1)} %get-tuple-element.29.refs_0_.refs_1_.refs_2_, bf16[896,2048]{1,0:T(8,128)(2,1)S(1)} %copy-done.3, bf16[896,2048]{1,0:T(8,128)(2,1)} %get-tuple-element.30.refs_4_.refs_2_, ...), custom_call_target="tpu_custom_call" | custom-call | flops 1996488704 | bytes 15654912 | tf_op jit(solution)/shard_map/gate_up_product/pallas_call | solution.py:237
  112.6 11.2 %gate_up_product.2 = (f32[136,2048]{1,0:T(8,128)S(1)}, bf16[136,2048]{1,0:T(8,128)(2,1)S(1)}, f32[136,2048]{1,0:T(8,128)S(1)}) custom-call(s32[1]{0:T(128)} %bitcast.1.meta_ref.rank_ref, bf16[4,136,3584]{2,1,0:T(8,128)(2,1)} %get-tuple-element.29.refs_0_.refs_1_.refs_2_, bf16[4,136,3584]{2,1,0:T(8,128)(2,1)} %get-tuple-element.29.refs_0_.refs_1_.refs_2_, ...), custom_call_target="tpu_custom_call" | custom-call | flops 5989466112 | bytes 17604608 | tf_op jit(solution)/shard_map/gate_up_product/pallas_call | solution.py:237
  130.2 4.1 %collective-permute-done.12.refs_0_ = bf16[512,896]{1,0:T(8,128)(2,1)S(1)} collective-permute-done((bf16[512,896]{1,0:T(8,128)(2,1)}, bf16[512,896]{1,0:T(8,128)(2,1)S(1)}, u32[]{:S(2)}, u32[]{:S(2)}) %collective-permute-start.12) | collective-permute-done | bytes 917536 | tf_op jit(solution)/shard_map/ppermute | solution.py:19
  147.0 5.7 %down_product.3.refs_1_ = bf16[2,136,3584]{2,1,0:T(8,128)(2,1)} custom-call(s32[1]{0:T(128)} %bitcast.1.meta_ref.rank_ref, bf16[136,1024]{1,0:T(8,128)(2,1)} %fusion.2.refs_1_.hidden_ref, bf16[1024,896]{1,0:T(8,128)(2,1)} %refs_0_.5, bf16[512,896]{1,0:T(8,128)(2,1)} %after.13.refs_1_, bf16[512,896]{1,0:T(8,128)(2,1)} %after.15.refs_2_, ...), custom_call_target="tpu_custom_call" | custom-call | flops 998244352 | bytes 8593408 | tf_op jit(solution)/shard_map/down_product/pallas_call | solution.py:310
  152.7 5.0 %all-to-all-start.1 = ((bf16[2,136,3584]{2,1,0:T(8,128)(2,1)}), bf16[2,136,3584]{2,1,0:T(8,128)(2,1)}, u32[]{:S(2)}, u32[]{:S(2)}) async-start(bf16[2,136,3584]{2,1,0:T(8,128)(2,1)} %down_product.3.refs_1_), calls=%async_computation.1 | async-start | bytes 3899392 | tf_op jit(solution)/shard_map/all_to_all | solution.py:538
  157.7 6.2 %collective-permute-done.19.refs_0_ = bf16[136,1024]{1,0:T(8,128)(2,1)S(1)} collective-permute-done((bf16[136,1024]{1,0:T(8,128)(2,1)}, bf16[136,1024]{1,0:T(8,128)(2,1)S(1)}, u32[]{:S(2)}, u32[]{:S(2)}) %collective-permute-start.19) | collective-permute-done | bytes 278560 | tf_op jit(solution)/shard_map/ppermute | solution.py:19
  164.6 5.5 %down_product.4.refs_1_ = bf16[136,3584]{1,0:T(8,128)(2,1)} custom-call(s32[1]{0:T(128)} %bitcast.1.meta_ref.rank_ref, bf16[136,1024]{1,0:T(8,128)(2,1)} %after.19.hidden_ref, bf16[1024,896]{1,0:T(8,128)(2,1)} %refs_0_.5, bf16[512,896]{1,0:T(8,128)(2,1)} %after.13.refs_1_, bf16[512,896]{1,0:T(8,128)(2,1)} %after.15.refs_2_, ...), custom_call_target="tpu_custom_call" | custom-call | flops 998244352 | bytes 8593408 | tf_op jit(solution)/shard_map/down_product/pallas_call | solution.py:310
  181.8 8.2 %collective-permute-done.20 = bf16[136,1024]{1,0:T(8,128)(2,1)S(1)} collective-permute-done((bf16[136,1024]{1,0:T(8,128)(2,1)S(1)}, bf16[136,1024]{1,0:T(8,128)(2,1)S(1)}, u32[]{:S(2)}, u32[]{:S(2)}) %collective-permute-start.20) | collective-permute-done | bytes 278560 | tf_op jit(solution)/shard_map/ppermute | solution.py:19
  190.8 6.6 %down_product.5 = (bf16[136,3584]{1,0:T(8,128)(2,1)}, bf16[136,3584]{1,0:T(8,128)(2,1)}) custom-call(s32[1]{0:T(128)} %bitcast.1.meta_ref.rank_ref, bf16[272,1024]{1,0:T(8,128)(2,1)} %pad_maximum_fusion.3.hidden_ref, bf16[1024,896]{1,0:T(8,128)(2,1)} %refs_0_.5, bf16[512,896]{1,0:T(8,128)(2,1)} %after.13.refs_1_, bf16[512,896]{1,0:T(8,128)(2,1)} %after.15.refs_2_, ...), custom_call_target="tpu_custom_call" | custom-call | flops 1996488704 | bytes 9846784 | tf_op jit(solution)/shard_map/down_product/pallas_call | solution.py:310
  198.2 7.0 %collective-permute-done.16.refs_2_ = bf16[2,448,576]{2,1,0:T(8,128)(2,1)} collective-permute-done((bf16[2,448,576]{2,1,0:T(8,128)(2,1)S(1)}, bf16[2,448,576]{2,1,0:T(8,128)(2,1)}, u32[]{:S(2)}, u32[]{:S(2)}) %collective-permute-start.16) | collective-permute-done | bytes 1032224 | tf_op jit(solution)/shard_map/ppermute | solution.py:19
  205.2 22.5 %collective-permute-done.17.refs_3_ = bf16[2,448,576]{2,1,0:T(8,128)(2,1)} collective-permute-done((bf16[2,448,576]{2,1,0:T(8,128)(2,1)}, bf16[2,448,576]{2,1,0:T(8,128)(2,1)}, u32[]{:S(2)}, u32[]{:S(2)}) %collective-permute-start.17) | collective-permute-done | bytes 1032224 | tf_op jit(solution)/shard_map/ppermute | solution.py:19
  229.3 5.6 %latent_product.1 = (bf16[256,576]{1,0:T(8,128)(2,1)S(1)}, f32[256,576]{1,0:T(8,128)S(1)}) custom-call(s32[1]{0:T(128)} %bitcast.1.meta_ref.rank_ref, bf16[8,256,448]{2,1,0:T(8,128)(2,1)S(1)} %copy-done.4, bf16[8,256,448]{2,1,0:T(8,128)(2,1)S(1)} %copy-done, bf16[2,448,576]{2,1,0:T(8,128)(2,1)S(1)} %pad_maximum_fusion.refs_0_, ...), custom_call_target="tpu_custom_call" | custom-call | flops 2113929216 | bytes 7798784 | tf_op jit(solution)/shard_map/latent_product/pallas_call | solution.py:387
  236.5 5.6 %unpack_rows.2.refs_1_.refs_2_ = bf16[256,7168]{1,0:T(8,128)(2,1)} custom-call(s32[1]{0:T(128)} %bitcast.1.meta_ref.rank_ref, s32[16]{0:T(128)} %lengths_ref.5, s32[1,256]{1,0:T(1,128)} %bitcast.9, f32[1,256]{1,0:T(1,128)} %bitcast.11, bf16[136,3584]{1,0:T(8,128)(2,1)} %get-tuple-element.44.refs_0_, bf16[2,136,3584]{2,1,0:T(8,128)(2,1)} %all-to-all-done.1.refs_1_), custom_call_target="tpu_custom_call" | custom-call | flops 939524096 | bytes 3670016 | tf_op jit(solution)/shard_map/unpack_rows/pallas_call | solution.py:143
  243.4 5.5 %unpack_rows.3 = bf16[256,7168]{1,0:T(8,128)(2,1)} custom-call(s32[1]{0:T(128)} %bitcast.1.meta_ref.rank_ref, s32[16]{0:T(128)} %lengths_ref.5, s32[1,256]{1,0:T(1,128)} %bitcast.10, f32[1,256]{1,0:T(1,128)} %bitcast.12, bf16[136,3584]{1,0:T(8,128)(2,1)} %collective-permute-done.22.refs_0_, ...), custom_call_target="tpu_custom_call", output_to_operand_aliasing={{}: (6, {})} | custom-call | flops 939524096 | bytes 3670016 | tf_op jit(solution)/shard_map/unpack_rows/pallas_call | solution.py:143
  (129 shorter events, 55.2 us)
Async XLA Ops:
  0.6 81.5 %collective-permute-start = (bf16[896,2048]{1,0:T(8,128)(2,1)}, bf16[896,2048]{1,0:T(8,128)(2,1)}, u32[]{:S(2)}, u32[]{:S(2)}) collective-permute-start(bf16[896,2048]{1,0:T(8,128)(2,1)} %refs_1_.1), channel_id=1, source_target_pairs={{0,2},{1,3},{2,0},{3,1},{4,6},{5,7},{6,4},{7,5},{8,10},{9,11},{10,... | collective-permute-start | bytes 11010056 | tf_op jit(solution)/shard_map/ppermute | solution.py:19
  3.2 8.4 %collective-permute-start.2 = (bf16[1,224,576]{2,1,0:T(8,128)(2,1)S(1)}, bf16[1,224,576]{2,1,0:T(8,128)(2,1)S(1)}, u32[]{:S(2)}, u32[]{:S(2)}) collective-permute-start(bf16[1,224,576]{2,1,0:T(8,128)(2,1)S(1)} %dynamic-slice_bitcast_fusion), channel_id=1, source_target_pairs={{0,4},{1,5},{2,6},{3,7},{4,0},{5,1},{6,2},{7,3},{8,12},{9,13},{10,... | collective-permute-start | bytes 774152 | tf_op jit(solution)/shard_map/ppermute | solution.py:19
  12.3 88.0 %all-to-all-start = ((bf16[4,136,3584]{2,1,0:T(8,128)(2,1)}), bf16[4,136,3584]{2,1,0:T(8,128)(2,1)}, u32[]{:S(2)}, u32[]{:S(2)}) async-start(bf16[4,136,3584]{2,1,0:T(8,128)(2,1)} %after.11), calls=%async_computation | async-start | bytes 7798784 | tf_op jit(solution)/shard_map/all_to_all | solution.py:494
  27.9 5.8 %collective-permute-start.1 = (bf16[8,256,448]{1,2,0:T(8,128)(2,1)S(1)}, bf16[8,256,448]{1,2,0:T(8,128)(2,1)}, u32[]{:S(2)}, u32[]{:S(2)}) collective-permute-start(bf16[8,256,448]{1,2,0:T(8,128)(2,1)S(1)} %copy.39), channel_id=1, source_target_pairs={{0,1},{1,0},{2,3},{3,2},{4,5},{5,4},{6,7},{7,6},{8,9},{9,8},{10,11... | collective-permute-start | bytes 5505032 | tf_op jit(solution)/shard_map/ppermute | solution.py:19
  28.0 68.0 %collective-permute-start.3 = (bf16[896,2048]{1,0:T(8,128)(2,1)}, bf16[896,2048]{1,0:T(8,128)(2,1)}, u32[]{:S(2)}, u32[]{:S(2)}) collective-permute-start(bf16[896,2048]{1,0:T(8,128)(2,1)} %refs_1_.1), channel_id=1, source_target_pairs={{0,1},{1,0},{2,3},{3,2},{4,5},{5,4},{6,7},{7,6},{8,9},{9,8},{10,11... | collective-permute-start | bytes 11010056 | tf_op jit(solution)/shard_map/ppermute | solution.py:19
  82.1 18.2 %collective-permute-start.4 = (bf16[896,2048]{1,0:T(8,128)(2,1)}, bf16[896,2048]{1,0:T(8,128)(2,1)}, u32[]{:S(2)}, u32[]{:S(2)}) collective-permute-start(bf16[896,2048]{1,0:T(8,128)(2,1)} %get-tuple-element.28.refs_5_.refs_3_.refs_1_), channel_id=1, source_target_pairs={{0,1},{1,0},{2,3},{3,2},{4,5},{5,4},{6,7},{7,6},{8,9},{9,8},{10,11... | collective-permute-start | bytes 11010056 | tf_op jit(solution)/shard_map/ppermute | solution.py:19
  84.7 6.4 %collective-permute-start.7 = (bf16[512,896]{1,0:T(8,128)(2,1)S(1)}, bf16[512,896]{1,0:T(8,128)(2,1)S(1)}, u32[]{:S(2)}, u32[]{:S(2)}) collective-permute-start(bf16[512,896]{1,0:T(8,128)(2,1)S(1)} %get-tuple-element.53), channel_id=1, source_target_pairs={{0,1},{1,0},{2,3},{3,2},{4,5},{5,4},{6,7},{7,6},{8,9},{9,8},{10,11... | collective-permute-start | bytes 2752520 | tf_op jit(solution)/shard_map/ppermute | solution.py:19
  84.7 9.8 %collective-permute-start.11 = (bf16[512,896]{1,0:T(8,128)(2,1)}, bf16[512,896]{1,0:T(8,128)(2,1)S(1)}, u32[]{:S(2)}, u32[]{:S(2)}) collective-permute-start(bf16[512,896]{1,0:T(8,128)(2,1)} %get-tuple-element.52), channel_id=1, source_target_pairs={{0,1},{1,0},{2,3},{3,2},{4,5},{5,4},{6,7},{7,6},{8,9},{9,8},{10,11... | collective-permute-start | bytes 2752520 | tf_op jit(solution)/shard_map/ppermute | solution.py:19
  92.1 34.5 %collective-permute-start.8 = (bf16[512,896]{1,0:T(8,128)(2,1)}, bf16[512,896]{1,0:T(8,128)(2,1)S(1)}, u32[]{:S(2)}, u32[]{:S(2)}) collective-permute-start(bf16[512,896]{1,0:T(8,128)(2,1)} %after.13.refs_1_), channel_id=1, source_target_pairs={{0,2},{1,3},{2,0},{3,1},{4,6},{5,7},{6,4},{7,5},{8,10},{9,11},{10,... | collective-permute-start | bytes 2752520 | tf_op jit(solution)/shard_map/ppermute | solution.py:19
  95.5 38.9 %collective-permute-start.12 = (bf16[512,896]{1,0:T(8,128)(2,1)}, bf16[512,896]{1,0:T(8,128)(2,1)S(1)}, u32[]{:S(2)}, u32[]{:S(2)}) collective-permute-start(bf16[512,896]{1,0:T(8,128)(2,1)} %after.15.refs_2_), channel_id=1, source_target_pairs={{0,2},{1,3},{2,0},{3,1},{4,6},{5,7},{6,4},{7,5},{8,10},{9,11},{10,... | collective-permute-start | bytes 2752520 | tf_op jit(solution)/shard_map/ppermute | solution.py:19
  100.3 26.2 %collective-permute-start.5 = (bf16[2,224,576]{2,1,0:T(8,128)(2,1)}, bf16[2,224,576]{2,1,0:T(8,128)(2,1)}, u32[]{:S(2)}, u32[]{:S(2)}) collective-permute-start(bf16[2,224,576]{2,1,0:T(8,128)(2,1)} %after.12), channel_id=1, source_target_pairs={{0,8},{1,9},{2,10},{3,11},{4,12},{5,13},{6,14},{7,15},{8,0},{9,1},... | collective-permute-start | bytes 1548296 | tf_op jit(solution)/shard_map/ppermute | solution.py:19
  112.5 24.7 %collective-permute-start.6 = (bf16[136,2048]{1,0:T(8,128)(2,1)S(1)}, bf16[136,2048]{1,0:T(8,128)(2,1)}, u32[]{:S(2)}, u32[]{:S(2)}) collective-permute-start(bf16[136,2048]{1,0:T(8,128)(2,1)S(1)} %gate_up_product.3), channel_id=1, source_target_pairs={{0,4},{1,5},{2,6},{3,7},{4,0},{5,1},{6,2},{7,3},{8,12},{9,13},{10,... | collective-permute-start | bytes 1671176 | tf_op jit(solution)/shard_map/ppermute | solution.py:19
  129.7 7.5 %collective-permute-start.9 = (bf16[256,896]{1,0:T(8,128)(2,1)}, bf16[256,896]{1,0:T(8,128)(2,1)S(1)}, u32[]{:S(2)}, u32[]{:S(2)}) collective-permute-start(bf16[256,896]{1,0:T(8,128)(2,1)} %get-tuple-element.57), channel_id=1, source_target_pairs={{0,1},{1,0},{2,3},{3,2},{4,5},{5,4},{6,7},{7,6},{8,9},{9,8},{10,11... | collective-permute-start | bytes 1376264 | tf_op jit(solution)/shard_map/ppermute | solution.py:19
  129.7 7.5 %collective-permute-start.10 = (bf16[256,896]{1,0:T(8,128)(2,1)}, bf16[256,896]{1,0:T(8,128)(2,1)}, u32[]{:S(2)}, u32[]{:S(2)}) collective-permute-start(bf16[256,896]{1,0:T(8,128)(2,1)} %get-tuple-element.56), channel_id=1, source_target_pairs={{0,1},{1,0},{2,3},{3,2},{4,5},{5,4},{6,7},{7,6},{8,9},{9,8},{10,11... | collective-permute-start | bytes 1376264 | tf_op jit(solution)/shard_map/ppermute | solution.py:19
  141.4 28.7 %collective-permute-start.18 = (bf16[136,2048]{1,0:T(8,128)(2,1)}, bf16[136,2048]{1,0:T(8,128)(2,1)S(1)}, u32[]{:S(2)}, u32[]{:S(2)}) collective-permute-start(bf16[136,2048]{1,0:T(8,128)(2,1)} %after.18), channel_id=1, source_target_pairs={{0,4},{1,5},{2,6},{3,7},{4,0},{5,1},{6,2},{7,3},{8,12},{9,13},{10,... | collective-permute-start | bytes 1671176 | tf_op jit(solution)/shard_map/ppermute | solution.py:19
  141.7 22.3 %collective-permute-start.19 = (bf16[136,1024]{1,0:T(8,128)(2,1)}, bf16[136,1024]{1,0:T(8,128)(2,1)S(1)}, u32[]{:S(2)}, u32[]{:S(2)}) collective-permute-start(bf16[136,1024]{1,0:T(8,128)(2,1)} %fusion.2.refs_1_.hidden_ref), channel_id=1, source_target_pairs={{0,4},{1,5},{2,6},{3,7},{4,0},{5,1},{6,2},{7,3},{8,12},{9,13},{10,... | collective-permute-start | bytes 835592 | tf_op jit(solution)/shard_map/ppermute | solution.py:19
  145.5 29.3 %collective-permute-start.15 = (bf16[3,224,576]{2,1,0:T(8,128)(2,1)}, bf16[3,224,576]{2,1,0:T(8,128)(2,1)S(1)}, u32[]{:S(2)}, u32[]{:S(2)}) collective-permute-start(bf16[3,224,576]{2,1,0:T(8,128)(2,1)} %after.17), channel_id=1, source_target_pairs={{0,16},{16,0},{1,17},{17,1},{2,18},{18,2},{3,19},{19,3},{4,20},{20... | collective-permute-start | bytes 2322440 | tf_op jit(solution)/shard_map/ppermute | solution.py:552
  152.7 83.8 %all-to-all-start.1 = ((bf16[2,136,3584]{2,1,0:T(8,128)(2,1)}), bf16[2,136,3584]{2,1,0:T(8,128)(2,1)}, u32[]{:S(2)}, u32[]{:S(2)}) async-start(bf16[2,136,3584]{2,1,0:T(8,128)(2,1)} %down_product.3.refs_1_), calls=%async_computation.1 | async-start | bytes 3899392 | tf_op jit(solution)/shard_map/all_to_all | solution.py:538
  172.4 17.6 %collective-permute-start.20 = (bf16[136,1024]{1,0:T(8,128)(2,1)S(1)}, bf16[136,1024]{1,0:T(8,128)(2,1)S(1)}, u32[]{:S(2)}, u32[]{:S(2)}) collective-permute-start(bf16[136,1024]{1,0:T(8,128)(2,1)S(1)} %fusion.1), channel_id=1, source_target_pairs={{0,4},{1,5},{2,6},{3,7},{4,0},{5,1},{6,2},{7,3},{8,12},{9,13},{10,... | collective-permute-start | bytes 835592 | tf_op jit(solution)/shard_map/ppermute | solution.py:19
  176.9 28.3 %collective-permute-start.16 = (bf16[2,448,576]{2,1,0:T(8,128)(2,1)S(1)}, bf16[2,448,576]{2,1,0:T(8,128)(2,1)}, u32[]{:S(2)}, u32[]{:S(2)}) collective-permute-start(bf16[2,448,576]{2,1,0:T(8,128)(2,1)S(1)} %pad_maximum_fusion.refs_0_), channel_id=1, source_target_pairs={{0,2},{1,3},{2,0},{3,1},{4,6},{5,7},{6,4},{7,5},{8,10},{9,11},{10,... | collective-permute-start | bytes 3096584 | tf_op jit(solution)/shard_map/ppermute | solution.py:19
  178.6 49.1 %collective-permute-start.17 = (bf16[2,448,576]{2,1,0:T(8,128)(2,1)}, bf16[2,448,576]{2,1,0:T(8,128)(2,1)}, u32[]{:S(2)}, u32[]{:S(2)}) collective-permute-start(bf16[2,448,576]{2,1,0:T(8,128)(2,1)} %slice.70.refs_1_), channel_id=1, source_target_pairs={{0,2},{1,3},{2,0},{3,1},{4,6},{5,7},{6,4},{7,5},{8,10},{9,11},{10,... | collective-permute-start | bytes 3096584 | tf_op jit(solution)/shard_map/ppermute | solution.py:19
  178.9 64.5 %collective-permute-start.23 = (bf16[136,3584]{1,0:T(8,128)(2,1)}, bf16[136,3584]{1,0:T(8,128)(2,1)}, u32[]{:S(2)}, u32[]{:S(2)}) collective-permute-start(bf16[136,3584]{1,0:T(8,128)(2,1)} %down_product.4.refs_1_), channel_id=1, source_target_pairs={{0,12},{1,13},{2,14},{3,15},{4,8},{5,9},{6,10},{7,11},{8,4},{9,5},... | collective-permute-start | bytes 2924552 | tf_op jit(solution)/shard_map/ppermute | solution.py:19
  197.5 45.9 %collective-permute-start.22 = (bf16[136,3584]{1,0:T(8,128)(2,1)}, bf16[136,3584]{1,0:T(8,128)(2,1)}, u32[]{:S(2)}, u32[]{:S(2)}) collective-permute-start(bf16[136,3584]{1,0:T(8,128)(2,1)} %get-tuple-element.45), channel_id=1, source_target_pairs={{0,4},{1,5},{2,6},{3,7},{4,0},{5,1},{6,2},{7,3},{8,12},{9,13},{10,... | collective-permute-start | bytes 2924552 | tf_op jit(solution)/shard_map/ppermute | solution.py:19
  242.1 6.7 %collective-permute-start.21 = (bf16[256,576]{1,0:T(8,128)(2,1)}, bf16[256,576]{1,0:T(8,128)(2,1)S(1)}, u32[]{:S(2)}, u32[]{:S(2)}) collective-permute-start(bf16[256,576]{1,0:T(8,128)(2,1)} %after.21), channel_id=1, source_target_pairs={{0,1},{1,0},{2,3},{3,2},{4,5},{5,4},{6,7},{7,6},{8,9},{9,8},{10,11... | collective-permute-start | bytes 884744 | tf_op jit(solution)/shard_map/ppermute | solution.py:19
  (26 other events, 94.6 us)

commit v9 on v8

--- a/solution.py
+++ b/solution.py
@@ -248,7 +248,7 @@
             jax.ShapeDtypeStruct((height, columns), dtype)
             for height, (_, _, dtype) in zip(heights, groups)
         ],
-        compiler_params=pltpu.CompilerParams(vmem_limit_bytes=32 << 20),
+        compiler_params=pltpu.CompilerParams(vmem_limit_bytes=24 << 20),
         cost_estimate=pl.CostEstimate(
             flops=2 * rows * width * columns,
             bytes_accessed=2 * width * (rows + columns),

time: 255 us -> 255 us (level)
  no operation moved by 1% of the time
where the time goes in v9:
time: 255 us; the launch traced here: 251 us
  waiting for transfers between devices  113 us (44%)
  Pallas kernels  65.8 us (26%)
  starting transfers between devices  30.9 us (12%)
  local copies, waits for them, and re-layouts  30 us (12%)
  other arithmetic  9.91 us (4%)
    ppermute x23, waiting for transfers between devices, swapped(): lax.ppermute(block, 'dp', [(low, low ^ bits) for low in range(count)])  109 us
    ppermute x23, starting transfers between devices, swapped(): lax.ppermute(block, 'dp', [(low, low ^ bits) for low in range(count)])  19.1 us
    pallas_call x2, Pallas kernels, gate_up_product(): pl.pallas_call(functools.partial(gate_up_body, [len(numbers) for numbers,...  18 us
    pallas_call x3, Pallas kernels, down_product(): pl.pallas_call(functools.partial(down_body, places, joined), grid_spec=pl...  17.8 us
    unnamed x49, local copies, waits for them, and re-layouts  15.5 us
    pallas_call x2, Pallas kernels, unpack(): pl.pallas_call(functools.partial(unpack_body, near), grid_spec=pltpu.Pref...  11.1 us
    pallas_call x1, Pallas kernels, core_split(): pl.pallas_call(core_split_body, grid_spec=pltpu.PrefetchScalarGridSpec(nu...  7.03 us
    pallas_call x1, Pallas kernels, pack(): pl.pallas_call(pack_body, grid_spec=pltpu.PrefetchScalarGridSpec(num_scal...  6.3 us
  transfers between devices with their start and end apart: 26, of which 14 were waited for; matrix products, arithmetic and copies ran while one was open for 8% of the time, Pallas kernels for 26%

profile of v9, /device:TPU:8, one launch (start us, length us, event | category | flops | bytes accessed | tf_op | source)
XLA Modules:
  0.0 250.8 jit_solution(11285026993590824036)
XLA Ops:
  3.7 6.3 %pack_rows.1.refs_0_ = bf16[4,136,3584]{2,1,0:T(8,128)(2,1)} custom-call(s32[1]{0:T(128)} %bitcast.1.meta_ref.rank_ref, s32[16]{0:T(128)} %lengths_ref.5, s32[1,256]{1,0:T(1,128)} %bitcast.8, bf16[256,7168]{1,0:T(8,128)(2,1)} %high_ref.1, bf16[256,7168]{1,0:T(8,128)(2,1)} %high_ref.1), custom_call_target="tpu_custom_call" | custom-call | flops 1879048192 | bytes 7340032 | tf_op jit(solution)/shard_map/pack_rows/pallas_call | solution.py:81
  12.3 5.3 %all-to-all-start = ((bf16[4,136,3584]{2,1,0:T(8,128)(2,1)}), bf16[4,136,3584]{2,1,0:T(8,128)(2,1)}, u32[]{:S(2)}, u32[]{:S(2)}) async-start(bf16[4,136,3584]{2,1,0:T(8,128)(2,1)} %after.11), calls=%async_computation | async-start | bytes 7798784 | tf_op jit(solution)/shard_map/all_to_all | solution.py:494
  17.6 7.0 %core_split.1 = (bf16[8,256,448]{2,1,0:T(8,128)(2,1)}, bf16[8,256,448]{2,1,0:T(8,128)(2,1)}) custom-call(s32[1]{0:T(128)} %bitcast.1.meta_ref.rank_ref, bf16[256,7168]{1,0:T(8,128)(2,1)} %high_ref.1), custom_call_target="tpu_custom_call" | custom-call | tf_op jit(solution)/shard_map/core_split/pallas_call | solution.py:441
  24.6 3.3 %copy.39 = bf16[8,256,448]{1,2,0:T(8,128)(2,1)S(1)} copy(bf16[8,256,448]{2,1,0:T(8,128)(2,1)} %get-tuple-element.25) | data formatting | bytes 3670016 | tf_op jit(solution)/shard_map/core_split/pallas_call | solution.py:441
  28.5 5.2 %collective-permute-done.1 = bf16[8,256,448]{1,2,0:T(8,128)(2,1)} collective-permute-done((bf16[8,256,448]{1,2,0:T(8,128)(2,1)S(1)}, bf16[8,256,448]{1,2,0:T(8,128)(2,1)}, u32[]{:S(2)}, u32[]{:S(2)}) %collective-permute-start.1) | collective-permute-done | bytes 1835040 | tf_op jit(solution)/shard_map/ppermute | solution.py:19
  33.7 3.8 %copy.40.refs_2_ = bf16[8,256,448]{2,1,0:T(8,128)(2,1)} copy(bf16[8,256,448]{1,2,0:T(8,128)(2,1)} %collective-permute-done.1) | data formatting | bytes 3670016 | tf_op jit(solution)/shard_map/ppermute | solution.py:19
  37.5 44.6 %collective-permute-done.refs_0_ = bf16[896,2048]{1,0:T(8,128)(2,1)} collective-permute-done((bf16[896,2048]{1,0:T(8,128)(2,1)}, bf16[896,2048]{1,0:T(8,128)(2,1)}, u32[]{:S(2)}, u32[]{:S(2)}) %collective-permute-start) | collective-permute-done | bytes 3670048 | tf_op jit(solution)/shard_map/ppermute | solution.py:19
  85.2 5.9 %collective-permute-done.7.refs_0_ = bf16[512,896]{1,0:T(8,128)(2,1)S(1)} collective-permute-done((bf16[512,896]{1,0:T(8,128)(2,1)S(1)}, bf16[512,896]{1,0:T(8,128)(2,1)S(1)}, u32[]{:S(2)}, u32[]{:S(2)}) %collective-permute-start.7) | collective-permute-done | bytes 917536 | tf_op jit(solution)/shard_map/ppermute | solution.py:19
  96.0 4.3 %all-to-all-done.refs_0_ = bf16[4,136,3584]{2,1,0:T(8,128)(2,1)} async-done(((bf16[4,136,3584]{2,1,0:T(8,128)(2,1)}), bf16[4,136,3584]{2,1,0:T(8,128)(2,1)}, u32[]{:S(2)}, u32[]{:S(2)}) %all-to-all-start) | async-done | bytes 3899424 | tf_op jit(solution)/shard_map/all_to_all | solution.py:494
  100.3 3.4 %collective-permute-start.5 = (bf16[2,224,576]{2,1,0:T(8,128)(2,1)}, bf16[2,224,576]{2,1,0:T(8,128)(2,1)}, u32[]{:S(2)}, u32[]{:S(2)}) collective-permute-start(bf16[2,224,576]{2,1,0:T(8,128)(2,1)} %after.12), channel_id=1, source_target_pairs={{0,8},{1,9},{2,10},{3,11},{4,12},{5,13},{6,14},{7,15},{8,0},{9,1},... | collective-permute-start | bytes 1548296 | tf_op jit(solution)/shard_map/ppermute | solution.py:19
  105.7 6.8 %gate_up_product.3 = bf16[136,2048]{1,0:T(8,128)(2,1)S(1)} custom-call(s32[1]{0:T(128)} %bitcast.1.meta_ref.rank_ref, bf16[4,136,3584]{2,1,0:T(8,128)(2,1)} %get-tuple-element.29.refs_0_.refs_1_.refs_2_, bf16[896,2048]{1,0:T(8,128)(2,1)S(1)} %copy-done.3, bf16[896,2048]{1,0:T(8,128)(2,1)} %get-tuple-element.30.refs_4_.refs_2_, ...), custom_call_target="tpu_custom_call" | custom-call | flops 1996488704 | bytes 15654912 | tf_op jit(solution)/shard_map/gate_up_product/pallas_call | solution.py:237
  112.6 11.2 %gate_up_product.2 = (f32[136,2048]{1,0:T(8,128)S(1)}, bf16[136,2048]{1,0:T(8,128)(2,1)S(1)}, f32[136,2048]{1,0:T(8,128)S(1)}) custom-call(s32[1]{0:T(128)} %bitcast.1.meta_ref.rank_ref, bf16[4,136,3584]{2,1,0:T(8,128)(2,1)} %get-tuple-element.29.refs_0_.refs_1_.refs_2_, bf16[4,136,3584]{2,1,0:T(8,128)(2,1)} %get-tuple-element.29.refs_0_.refs_1_.refs_2_, ...), custom_call_target="tpu_custom_call" | custom-call | flops 5989466112 | bytes 17604608 | tf_op jit(solution)/shard_map/gate_up_product/pallas_call | solution.py:237
  130.2 4.1 %collective-permute-done.12.refs_0_ = bf16[512,896]{1,0:T(8,128)(2,1)S(1)} collective-permute-done((bf16[512,896]{1,0:T(8,128)(2,1)}, bf16[512,896]{1,0:T(8,128)(2,1)S(1)}, u32[]{:S(2)}, u32[]{:S(2)}) %collective-permute-start.12) | collective-permute-done | bytes 917536 | tf_op jit(solution)/shard_map/ppermute | solution.py:19
  147.0 5.7 %down_product.3.refs_1_ = bf16[2,136,3584]{2,1,0:T(8,128)(2,1)} custom-call(s32[1]{0:T(128)} %bitcast.1.meta_ref.rank_ref, bf16[136,1024]{1,0:T(8,128)(2,1)} %fusion.2.refs_1_.hidden_ref, bf16[1024,896]{1,0:T(8,128)(2,1)} %refs_0_.5, bf16[512,896]{1,0:T(8,128)(2,1)} %after.13.refs_1_, bf16[512,896]{1,0:T(8,128)(2,1)} %after.15.refs_2_, ...), custom_call_target="tpu_custom_call" | custom-call | flops 998244352 | bytes 8593408 | tf_op jit(solution)/shard_map/down_product/pallas_call | solution.py:310
  152.7 5.0 %all-to-all-start.1 = ((bf16[2,136,3584]{2,1,0:T(8,128)(2,1)}), bf16[2,136,3584]{2,1,0:T(8,128)(2,1)}, u32[]{:S(2)}, u32[]{:S(2)}) async-start(bf16[2,136,3584]{2,1,0:T(8,128)(2,1)} %down_product.3.refs_1_), calls=%async_computation.1 | async-start | bytes 3899392 | tf_op jit(solution)/shard_map/all_to_all | solution.py:538
  157.7 6.2 %collective-permute-done.19.refs_0_ = bf16[136,1024]{1,0:T(8,128)(2,1)S(1)} collective-permute-done((bf16[136,1024]{1,0:T(8,128)(2,1)}, bf16[136,1024]{1,0:T(8,128)(2,1)S(1)}, u32[]{:S(2)}, u32[]{:S(2)}) %collective-permute-start.19) | collective-permute-done | bytes 278560 | tf_op jit(solution)/shard_map/ppermute | solution.py:19
  164.6 5.5 %down_product.4.refs_1_ = bf16[136,3584]{1,0:T(8,128)(2,1)} custom-call(s32[1]{0:T(128)} %bitcast.1.meta_ref.rank_ref, bf16[136,1024]{1,0:T(8,128)(2,1)} %after.19.hidden_ref, bf16[1024,896]{1,0:T(8,128)(2,1)} %refs_0_.5, bf16[512,896]{1,0:T(8,128)(2,1)} %after.13.refs_1_, bf16[512,896]{1,0:T(8,128)(2,1)} %after.15.refs_2_, ...), custom_call_target="tpu_custom_call" | custom-call | flops 998244352 | bytes 8593408 | tf_op jit(solution)/shard_map/down_product/pallas_call | solution.py:310
  181.8 8.2 %collective-permute-done.20 = bf16[136,1024]{1,0:T(8,128)(2,1)S(1)} collective-permute-done((bf16[136,1024]{1,0:T(8,128)(2,1)S(1)}, bf16[136,1024]{1,0:T(8,128)(2,1)S(1)}, u32[]{:S(2)}, u32[]{:S(2)}) %collective-permute-start.20) | collective-permute-done | bytes 278560 | tf_op jit(solution)/shard_map/ppermute | solution.py:19
  190.8 6.6 %down_product.5 = (bf16[136,3584]{1,0:T(8,128)(2,1)}, bf16[136,3584]{1,0:T(8,128)(2,1)}) custom-call(s32[1]{0:T(128)} %bitcast.1.meta_ref.rank_ref, bf16[272,1024]{1,0:T(8,128)(2,1)} %pad_maximum_fusion.3.hidden_ref, bf16[1024,896]{1,0:T(8,128)(2,1)} %refs_0_.5, bf16[512,896]{1,0:T(8,128)(2,1)} %after.13.refs_1_, bf16[512,896]{1,0:T(8,128)(2,1)} %after.15.refs_2_, ...), custom_call_target="tpu_custom_call" | custom-call | flops 1996488704 | bytes 9846784 | tf_op jit(solution)/shard_map/down_product/pallas_call | solution.py:310
  198.2 7.0 %collective-permute-done.16.refs_2_ = bf16[2,448,576]{2,1,0:T(8,128)(2,1)} collective-permute-done((bf16[2,448,576]{2,1,0:T(8,128)(2,1)S(1)}, bf16[2,448,576]{2,1,0:T(8,128)(2,1)}, u32[]{:S(2)}, u32[]{:S(2)}) %collective-permute-start.16) | collective-permute-done | bytes 1032224 | tf_op jit(solution)/shard_map/ppermute | solution.py:19
  205.2 22.5 %collective-permute-done.17.refs_3_ = bf16[2,448,576]{2,1,0:T(8,128)(2,1)} collective-permute-done((bf16[2,448,576]{2,1,0:T(8,128)(2,1)}, bf16[2,448,576]{2,1,0:T(8,128)(2,1)}, u32[]{:S(2)}, u32[]{:S(2)}) %collective-permute-start.17) | collective-permute-done | bytes 1032224 | tf_op jit(solution)/shard_map/ppermute | solution.py:19
  229.3 5.6 %latent_product.1 = (bf16[256,576]{1,0:T(8,128)(2,1)S(1)}, f32[256,576]{1,0:T(8,128)S(1)}) custom-call(s32[1]{0:T(128)} %bitcast.1.meta_ref.rank_ref, bf16[8,256,448]{2,1,0:T(8,128)(2,1)S(1)} %copy-done.4, bf16[8,256,448]{2,1,0:T(8,128)(2,1)S(1)} %copy-done, bf16[2,448,576]{2,1,0:T(8,128)(2,1)S(1)} %pad_maximum_fusion.refs_0_, ...), custom_call_target="tpu_custom_call" | custom-call | flops 2113929216 | bytes 7798784 | tf_op jit(solution)/shard_map/latent_product/pallas_call | solution.py:387
  236.5 5.6 %unpack_rows.2.refs_1_.refs_2_ = bf16[256,7168]{1,0:T(8,128)(2,1)} custom-call(s32[1]{0:T(128)} %bitcast.1.meta_ref.rank_ref, s32[16]{0:T(128)} %lengths_ref.5, s32[1,256]{1,0:T(1,128)} %bitcast.9, f32[1,256]{1,0:T(1,128)} %bitcast.11, bf16[136,3584]{1,0:T(8,128)(2,1)} %get-tuple-element.44.refs_0_, bf16[2,136,3584]{2,1,0:T(8,128)(2,1)} %all-to-all-done.1.refs_1_), custom_call_target="tpu_custom_call" | custom-call | flops 939524096 | bytes 3670016 | tf_op jit(solution)/shard_map/unpack_rows/pallas_call | solution.py:143
  243.4 5.5 %unpack_rows.3 = bf16[256,7168]{1,0:T(8,128)(2,1)} custom-call(s32[1]{0:T(128)} %bitcast.1.meta_ref.rank_ref, s32[16]{0:T(128)} %lengths_ref.5, s32[1,256]{1,0:T(1,128)} %bitcast.10, f32[1,256]{1,0:T(1,128)} %bitcast.12, bf16[136,3584]{1,0:T(8,128)(2,1)} %collective-permute-done.22.refs_0_, ...), custom_call_target="tpu_custom_call", output_to_operand_aliasing={{}: (6, {})} | custom-call | flops 939524096 | bytes 3670016 | tf_op jit(solution)/shard_map/unpack_rows/pallas_call | solution.py:143
  (129 shorter events, 55.2 us)
Async XLA Ops:
  0.6 81.5 %collective-permute-start = (bf16[896,2048]{1,0:T(8,128)(2,1)}, bf16[896,2048]{1,0:T(8,128)(2,1)}, u32[]{:S(2)}, u32[]{:S(2)}) collective-permute-start(bf16[896,2048]{1,0:T(8,128)(2,1)} %refs_1_.1), channel_id=1, source_target_pairs={{0,2},{1,3},{2,0},{3,1},{4,6},{5,7},{6,4},{7,5},{8,10},{9,11},{10,... | collective-permute-start | bytes 11010056 | tf_op jit(solution)/shard_map/ppermute | solution.py:19
  3.2 8.4 %collective-permute-start.2 = (bf16[1,224,576]{2,1,0:T(8,128)(2,1)S(1)}, bf16[1,224,576]{2,1,0:T(8,128)(2,1)S(1)}, u32[]{:S(2)}, u32[]{:S(2)}) collective-permute-start(bf16[1,224,576]{2,1,0:T(8,128)(2,1)S(1)} %dynamic-slice_bitcast_fusion), channel_id=1, source_target_pairs={{0,4},{1,5},{2,6},{3,7},{4,0},{5,1},{6,2},{7,3},{8,12},{9,13},{10,... | collective-permute-start | bytes 774152 | tf_op jit(solution)/shard_map/ppermute | solution.py:19
  12.3 88.0 %all-to-all-start = ((bf16[4,136,3584]{2,1,0:T(8,128)(2,1)}), bf16[4,136,3584]{2,1,0:T(8,128)(2,1)}, u32[]{:S(2)}, u32[]{:S(2)}) async-start(bf16[4,136,3584]{2,1,0:T(8,128)(2,1)} %after.11), calls=%async_computation | async-start | bytes 7798784 | tf_op jit(solution)/shard_map/all_to_all | solution.py:494
  27.9 5.8 %collective-permute-start.1 = (bf16[8,256,448]{1,2,0:T(8,128)(2,1)S(1)}, bf16[8,256,448]{1,2,0:T(8,128)(2,1)}, u32[]{:S(2)}, u32[]{:S(2)}) collective-permute-start(bf16[8,256,448]{1,2,0:T(8,128)(2,1)S(1)} %copy.39), channel_id=1, source_target_pairs={{0,1},{1,0},{2,3},{3,2},{4,5},{5,4},{6,7},{7,6},{8,9},{9,8},{10,11... | collective-permute-start | bytes 5505032 | tf_op jit(solution)/shard_map/ppermute | solution.py:19
  28.0 68.0 %collective-permute-start.3 = (bf16[896,2048]{1,0:T(8,128)(2,1)}, bf16[896,2048]{1,0:T(8,128)(2,1)}, u32[]{:S(2)}, u32[]{:S(2)}) collective-permute-start(bf16[896,2048]{1,0:T(8,128)(2,1)} %refs_1_.1), channel_id=1, source_target_pairs={{0,1},{1,0},{2,3},{3,2},{4,5},{5,4},{6,7},{7,6},{8,9},{9,8},{10,11... | collective-permute-start | bytes 11010056 | tf_op jit(solution)/shard_map/ppermute | solution.py:19
  82.1 18.2 %collective-permute-start.4 = (bf16[896,2048]{1,0:T(8,128)(2,1)}, bf16[896,2048]{1,0:T(8,128)(2,1)}, u32[]{:S(2)}, u32[]{:S(2)}) collective-permute-start(bf16[896,2048]{1,0:T(8,128)(2,1)} %get-tuple-element.28.refs_5_.refs_3_.refs_1_), channel_id=1, source_target_pairs={{0,1},{1,0},{2,3},{3,2},{4,5},{5,4},{6,7},{7,6},{8,9},{9,8},{10,11... | collective-permute-start | bytes 11010056 | tf_op jit(solution)/shard_map/ppermute | solution.py:19
  84.7 6.4 %collective-permute-start.7 = (bf16[512,896]{1,0:T(8,128)(2,1)S(1)}, bf16[512,896]{1,0:T(8,128)(2,1)S(1)}, u32[]{:S(2)}, u32[]{:S(2)}) collective-permute-start(bf16[512,896]{1,0:T(8,128)(2,1)S(1)} %get-tuple-element.53), channel_id=1, source_target_pairs={{0,1},{1,0},{2,3},{3,2},{4,5},{5,4},{6,7},{7,6},{8,9},{9,8},{10,11... | collective-permute-start | bytes 2752520 | tf_op jit(solution)/shard_map/ppermute | solution.py:19
  84.7 9.8 %collective-permute-start.11 = (bf16[512,896]{1,0:T(8,128)(2,1)}, bf16[512,896]{1,0:T(8,128)(2,1)S(1)}, u32[]{:S(2)}, u32[]{:S(2)}) collective-permute-start(bf16[512,896]{1,0:T(8,128)(2,1)} %get-tuple-element.52), channel_id=1, source_target_pairs={{0,1},{1,0},{2,3},{3,2},{4,5},{5,4},{6,7},{7,6},{8,9},{9,8},{10,11... | collective-permute-start | bytes 2752520 | tf_op jit(solution)/shard_map/ppermute | solution.py:19
  92.1 34.5 %collective-permute-start.8 = (bf16[512,896]{1,0:T(8,128)(2,1)}, bf16[512,896]{1,0:T(8,128)(2,1)S(1)}, u32[]{:S(2)}, u32[]{:S(2)}) collective-permute-start(bf16[512,896]{1,0:T(8,128)(2,1)} %after.13.refs_1_), channel_id=1, source_target_pairs={{0,2},{1,3},{2,0},{3,1},{4,6},{5,7},{6,4},{7,5},{8,10},{9,11},{10,... | collective-permute-start | bytes 2752520 | tf_op jit(solution)/shard_map/ppermute | solution.py:19
  95.5 38.9 %collective-permute-start.12 = (bf16[512,896]{1,0:T(8,128)(2,1)}, bf16[512,896]{1,0:T(8,128)(2,1)S(1)}, u32[]{:S(2)}, u32[]{:S(2)}) collective-permute-start(bf16[512,896]{1,0:T(8,128)(2,1)} %after.15.refs_2_), channel_id=1, source_target_pairs={{0,2},{1,3},{2,0},{3,1},{4,6},{5,7},{6,4},{7,5},{8,10},{9,11},{10,... | collective-permute-start | bytes 2752520 | tf_op jit(solution)/shard_map/ppermute | solution.py:19
  100.3 26.2 %collective-permute-start.5 = (bf16[2,224,576]{2,1,0:T(8,128)(2,1)}, bf16[2,224,576]{2,1,0:T(8,128)(2,1)}, u32[]{:S(2)}, u32[]{:S(2)}) collective-permute-start(bf16[2,224,576]{2,1,0:T(8,128)(2,1)} %after.12), channel_id=1, source_target_pairs={{0,8},{1,9},{2,10},{3,11},{4,12},{5,13},{6,14},{7,15},{8,0},{9,1},... | collective-permute-start | bytes 1548296 | tf_op jit(solution)/shard_map/ppermute | solution.py:19
  112.5 24.7 %collective-permute-start.6 = (bf16[136,2048]{1,0:T(8,128)(2,1)S(1)}, bf16[136,2048]{1,0:T(8,128)(2,1)}, u32[]{:S(2)}, u32[]{:S(2)}) collective-permute-start(bf16[136,2048]{1,0:T(8,128)(2,1)S(1)} %gate_up_product.3), channel_id=1, source_target_pairs={{0,4},{1,5},{2,6},{3,7},{4,0},{5,1},{6,2},{7,3},{8,12},{9,13},{10,... | collective-permute-start | bytes 1671176 | tf_op jit(solution)/shard_map/ppermute | solution.py:19
  129.7 7.5 %collective-permute-start.9 = (bf16[256,896]{1,0:T(8,128)(2,1)}, bf16[256,896]{1,0:T(8,128)(2,1)S(1)}, u32[]{:S(2)}, u32[]{:S(2)}) collective-permute-start(bf16[256,896]{1,0:T(8,128)(2,1)} %get-tuple-element.57), channel_id=1, source_target_pairs={{0,1},{1,0},{2,3},{3,2},{4,5},{5,4},{6,7},{7,6},{8,9},{9,8},{10,11... | collective-permute-start | bytes 1376264 | tf_op jit(solution)/shard_map/ppermute | solution.py:19
  129.7 7.5 %collective-permute-start.10 = (bf16[256,896]{1,0:T(8,128)(2,1)}, bf16[256,896]{1,0:T(8,128)(2,1)}, u32[]{:S(2)}, u32[]{:S(2)}) collective-permute-start(bf16[256,896]{1,0:T(8,128)(2,1)} %get-tuple-element.56), channel_id=1, source_target_pairs={{0,1},{1,0},{2,3},{3,2},{4,5},{5,4},{6,7},{7,6},{8,9},{9,8},{10,11... | collective-permute-start | bytes 1376264 | tf_op jit(solution)/shard_map/ppermute | solution.py:19
  141.4 28.7 %collective-permute-start.18 = (bf16[136,2048]{1,0:T(8,128)(2,1)}, bf16[136,2048]{1,0:T(8,128)(2,1)S(1)}, u32[]{:S(2)}, u32[]{:S(2)}) collective-permute-start(bf16[136,2048]{1,0:T(8,128)(2,1)} %after.18), channel_id=1, source_target_pairs={{0,4},{1,5},{2,6},{3,7},{4,0},{5,1},{6,2},{7,3},{8,12},{9,13},{10,... | collective-permute-start | bytes 1671176 | tf_op jit(solution)/shard_map/ppermute | solution.py:19
  141.7 22.3 %collective-permute-start.19 = (bf16[136,1024]{1,0:T(8,128)(2,1)}, bf16[136,1024]{1,0:T(8,128)(2,1)S(1)}, u32[]{:S(2)}, u32[]{:S(2)}) collective-permute-start(bf16[136,1024]{1,0:T(8,128)(2,1)} %fusion.2.refs_1_.hidden_ref), channel_id=1, source_target_pairs={{0,4},{1,5},{2,6},{3,7},{4,0},{5,1},{6,2},{7,3},{8,12},{9,13},{10,... | collective-permute-start | bytes 835592 | tf_op jit(solution)/shard_map/ppermute | solution.py:19
  145.5 29.3 %collective-permute-start.15 = (bf16[3,224,576]{2,1,0:T(8,128)(2,1)}, bf16[3,224,576]{2,1,0:T(8,128)(2,1)S(1)}, u32[]{:S(2)}, u32[]{:S(2)}) collective-permute-start(bf16[3,224,576]{2,1,0:T(8,128)(2,1)} %after.17), channel_id=1, source_target_pairs={{0,16},{16,0},{1,17},{17,1},{2,18},{18,2},{3,19},{19,3},{4,20},{20... | collective-permute-start | bytes 2322440 | tf_op jit(solution)/shard_map/ppermute | solution.py:552
  152.7 83.8 %all-to-all-start.1 = ((bf16[2,136,3584]{2,1,0:T(8,128)(2,1)}), bf16[2,136,3584]{2,1,0:T(8,128)(2,1)}, u32[]{:S(2)}, u32[]{:S(2)}) async-start(bf16[2,136,3584]{2,1,0:T(8,128)(2,1)} %down_product.3.refs_1_), calls=%async_computation.1 | async-start | bytes 3899392 | tf_op jit(solution)/shard_map/all_to_all | solution.py:538
  172.4 17.6 %collective-permute-start.20 = (bf16[136,1024]{1,0:T(8,128)(2,1)S(1)}, bf16[136,1024]{1,0:T(8,128)(2,1)S(1)}, u32[]{:S(2)}, u32[]{:S(2)}) collective-permute-start(bf16[136,1024]{1,0:T(8,128)(2,1)S(1)} %fusion.1), channel_id=1, source_target_pairs={{0,4},{1,5},{2,6},{3,7},{4,0},{5,1},{6,2},{7,3},{8,12},{9,13},{10,... | collective-permute-start | bytes 835592 | tf_op jit(solution)/shard_map/ppermute | solution.py:19
  176.9 28.3 %collective-permute-start.16 = (bf16[2,448,576]{2,1,0:T(8,128)(2,1)S(1)}, bf16[2,448,576]{2,1,0:T(8,128)(2,1)}, u32[]{:S(2)}, u32[]{:S(2)}) collective-permute-start(bf16[2,448,576]{2,1,0:T(8,128)(2,1)S(1)} %pad_maximum_fusion.refs_0_), channel_id=1, source_target_pairs={{0,2},{1,3},{2,0},{3,1},{4,6},{5,7},{6,4},{7,5},{8,10},{9,11},{10,... | collective-permute-start | bytes 3096584 | tf_op jit(solution)/shard_map/ppermute | solution.py:19
  178.6 49.1 %collective-permute-start.17 = (bf16[2,448,576]{2,1,0:T(8,128)(2,1)}, bf16[2,448,576]{2,1,0:T(8,128)(2,1)}, u32[]{:S(2)}, u32[]{:S(2)}) collective-permute-start(bf16[2,448,576]{2,1,0:T(8,128)(2,1)} %slice.70.refs_1_), channel_id=1, source_target_pairs={{0,2},{1,3},{2,0},{3,1},{4,6},{5,7},{6,4},{7,5},{8,10},{9,11},{10,... | collective-permute-start | bytes 3096584 | tf_op jit(solution)/shard_map/ppermute | solution.py:19
  178.9 64.5 %collective-permute-start.23 = (bf16[136,3584]{1,0:T(8,128)(2,1)}, bf16[136,3584]{1,0:T(8,128)(2,1)}, u32[]{:S(2)}, u32[]{:S(2)}) collective-permute-start(bf16[136,3584]{1,0:T(8,128)(2,1)} %down_product.4.refs_1_), channel_id=1, source_target_pairs={{0,12},{1,13},{2,14},{3,15},{4,8},{5,9},{6,10},{7,11},{8,4},{9,5},... | collective-permute-start | bytes 2924552 | tf_op jit(solution)/shard_map/ppermute | solution.py:19
  197.5 45.9 %collective-permute-start.22 = (bf16[136,3584]{1,0:T(8,128)(2,1)}, bf16[136,3584]{1,0:T(8,128)(2,1)}, u32[]{:S(2)}, u32[]{:S(2)}) collective-permute-start(bf16[136,3584]{1,0:T(8,128)(2,1)} %get-tuple-element.45), channel_id=1, source_target_pairs={{0,4},{1,5},{2,6},{3,7},{4,0},{5,1},{6,2},{7,3},{8,12},{9,13},{10,... | collective-permute-start | bytes 2924552 | tf_op jit(solution)/shard_map/ppermute | solution.py:19
  242.1 6.7 %collective-permute-start.21 = (bf16[256,576]{1,0:T(8,128)(2,1)}, bf16[256,576]{1,0:T(8,128)(2,1)S(1)}, u32[]{:S(2)}, u32[]{:S(2)}) collective-permute-start(bf16[256,576]{1,0:T(8,128)(2,1)} %after.21), channel_id=1, source_target_pairs={{0,1},{1,0},{2,3},{3,2},{4,5},{5,4},{6,7},{7,6},{8,9},{9,8},{10,11... | collective-permute-start | bytes 884744 | tf_op jit(solution)/shard_map/ppermute | solution.py:19
  (26 other events, 94.6 us)
